TPU v7x, 32 devices: a whole 2x2x4 slice. The times are simulated.
32 devices in a mesh: group: 2 (over y), fsdp: 16 (over z, x, core).
Axes of the slice: x: 2, y: 2, z: 4, core: 2. Of those that a mesh axis runs over, the one named last changes fastest.
Arguments:
- hidden: bfloat16 [2, 32, 256, 5120], P('group', 'fsdp'), may hold values from -600 to 600
- norm_gain: float32 [5120], replicated, may hold values from 0.1 to 1.9
- queries: bfloat16 [2, 32, 256, 2560], P('group', 'fsdp'), may hold values from -800 to 800
- out_grad: bfloat16 [2, 32, 256, 2560], P('group', 'fsdp'), may hold values from -6 to 6
- kv_inner: bfloat16 [2, 5120, 1024], P('group', 'fsdp'), may hold values from -6 to 6
- kv_outer: float32 [5120, 1024], P('fsdp'), may hold values from -6 to 6
- momentum: float32 [5120, 1024], P('fsdp'), may hold values from -2 to 2
Outputs:
- blended: bfloat16 [2, 5120, 1024], P('group', 'fsdp')
- outer_new: float32 [5120, 1024], P('fsdp')
- momentum_new: float32 [5120, 1024], P('fsdp')
All inputs are finite; a program needn't handle non-finite values. Where the computation divides by a largest or mean magnitude, that divisor is 1e-20 or more.
Results may differ from a plain program's by a relative error of at most 0.025.
The roundings to bfloat16 on the way count: a program that leaves them out, or rounds other values in their place, can miss the bound.
Values may be sent and summed in bfloat16 or wider, within the bound.
No kernel may reach another device: no remote copies, remote signals or barrier semaphores. Data moves between devices by JAX's collectives and lax.ppermute only.
A program may use at most 128 MiB of HBM per device.

v0:
```python
import jax
import jax.numpy as jnp
from jax import lax
from jax.sharding import PartitionSpec as P

D = 5120
HD = 128
QBLOCK = 128


inner_rate = 0.25
outer_rate = 0.7
momentum_decay = 0.9
blend_share = 0.5
norm_eps = 1e-06
scale_eps = 1e-06


def normed_rows(hidden_rows, norm_gain):
    looked = hidden_rows.reshape(-1, hidden_rows.shape[-1]).astype(jnp.float32)
    mean_sq = jnp.mean(looked * looked, axis=-1, keepdims=True)
    return (looked * lax.rsqrt(mean_sq + norm_eps) * norm_gain).astype(jnp.bfloat16)


def attend(queries, kv_rows):
    seq_count, length, query_width = queries.shape
    kv_width = kv_rows.shape[-1] // 2
    kv_heads = kv_width // HD
    repeat = query_width // (kv_heads * HD)
    query_h = queries.reshape(seq_count, length, kv_heads, repeat, HD)
    key_h = kv_rows[..., :kv_width].reshape(seq_count, length, kv_heads, HD)
    value_h = kv_rows[..., kv_width:].reshape(seq_count, length, kv_heads, HD)
    scores = jnp.einsum(
        "slgrd,smgd->sgrlm", query_h, key_h, preferred_element_type=jnp.float32
    ) * HD ** (-0.5)
    places = jnp.arange(length)
    causal = places[None, :] <= places[:, None]
    scores = jnp.where(causal, scores, -1e30)
    highest = lax.stop_gradient(jnp.max(scores, axis=-1, keepdims=True))
    exp_scores = jnp.exp(scores - highest)
    prob_rows = (exp_scores / jnp.sum(exp_scores, axis=-1, keepdims=True)).astype(jnp.bfloat16)
    mixed_out = jnp.einsum(
        "sgrlm,smgd->slgrd", prob_rows, value_h, preferred_element_type=jnp.float32
    )
    return mixed_out.reshape(seq_count, length, query_width)


def kv_grads(queries, kv_rows, out_grad):

    def loss_part(kv_value):
        return attend(queries, kv_value)

    _, pullback = jax.vjp(loss_part, kv_rows)
    return pullback(out_grad.astype(jnp.float32))[0]


def quantize(delta):
    row_count = delta.shape[0]
    shaped = delta.reshape(row_count, -1, QBLOCK)
    scales = (jnp.max(jnp.abs(shaped), axis=-1) + scale_eps).astype(jnp.bfloat16)
    coded = (shaped / scales.astype(jnp.float32)[..., None]).astype(jnp.bfloat16)
    return (coded.reshape(row_count, -1), scales)


def dequantize(coded, scales):
    row_count = coded.shape[0]
    shaped = coded.reshape(row_count, scales.shape[1], -1).astype(jnp.float32)
    return (shaped * scales.astype(jnp.float32)[..., None]).reshape(row_count, -1)


def nesterov(outer_rows, moment_rows, average):
    moment_next = momentum_decay * moment_rows + average
    outer_next = outer_rows - outer_rate * (momentum_decay * moment_next + average)
    return (outer_next, moment_next)


def grad_term(rows_in, kv_part, inv_root):
    product = lax.dot_general(
        rows_in, kv_part, (((0,), (0,)), ((), ())), preferred_element_type=jnp.float32
    )
    return product * inv_root


def local(hidden, norm_gain, queries, out_grad, kv_inner, kv_outer, momentum):
    inv_root = D ** (-0.5)
    groups = lax.axis_size("group")
    rows_in = normed_rows(hidden[0], norm_gain)
    local_weights = kv_inner[0]
    kv_cols = local_weights.shape[1]
    projected = jnp.dot(
        rows_in,
        lax.all_gather(local_weights, "fsdp", axis=0, tiled=True),
        preferred_element_type=jnp.float32,
    )
    kv_rows = (projected * inv_root).astype(jnp.bfloat16)
    seq_local = queries.shape[1]
    kv_rows = kv_rows.reshape(seq_local, queries.shape[2], kv_cols)
    kv_grad = kv_grads(queries[0], kv_rows, out_grad[0]).reshape(-1, kv_cols)
    gradient = lax.psum_scatter(
        grad_term(rows_in, kv_grad, inv_root).astype(jnp.bfloat16),
        "fsdp",
        scatter_dimension=0,
        tiled=True,
    ).astype(jnp.float32)
    fresh = local_weights.astype(jnp.float32) - inner_rate * gradient
    coded, scales = quantize(kv_outer - fresh)
    all_coded, all_scales = (
        lax.all_gather(coded[None], "group", axis=0, tiled=True),
        lax.all_gather(scales[None], "group", axis=0, tiled=True),
    )
    totals = jnp.zeros(kv_outer.shape, jnp.float32)
    for member in range(groups):
        totals = totals + dequantize(all_coded[member], all_scales[member])
    average = totals / groups
    outer_new, momentum_new = nesterov(kv_outer, momentum, average)
    blended = (blend_share * fresh + (1.0 - blend_share) * outer_new).astype(jnp.bfloat16)
    return (blended[None], outer_new, momentum_new)


def solution(mesh):
    in_specs = (
        P("group", "fsdp", None, None),
        P(),
        P("group", "fsdp", None, None),
        P("group", "fsdp", None, None),
        P("group", "fsdp", None),
        P("fsdp", None),
        P("fsdp", None),
    )
    out_specs = (P("group", "fsdp", None), P("fsdp", None), P("fsdp", None))
    return jax.shard_map(local, mesh=mesh, in_specs=in_specs, out_specs=out_specs, check_vma=False)
```

profile of v0, /device:TPU:0, one launch (start us, length us, event | category | flops | bytes accessed | tf_op | source)
XLA Modules:
  0.0 313.0 jit_solution(17865042799683106233)
XLA Ops:
  8.0 3.6 %multiply_reduce_fusion = f32[2,256]{1,0:T(2,128)S(1)} fusion(bf16[1,2,256,5120]{3,2,1,0:T(8,128)(2,1)} %param.7), kind=kLoop, calls=%fused_computation.20 | loop fusion | flops 7863808 | bytes 5244928 | tf_op jit(solution)/shard_map/reduce_sum | solution.py:21
  11.6 2.6 copy.38
  14.2 4.5 %copy.41 = bf16[1,2,256,2560]{2,3,1,0:T(8,128)(2,1)} copy(bf16[1,2,256,2560]{3,2,1,0:T(8,128)(2,1)} %param.10) | data formatting | bytes 5242880 | tf_op args[3]
  18.8 7.3 %fusion.11 = bf16[512,5120]{1,0:T(8,128)(2,1)} fusion(f32[5120]{0:T(1024)S(1)} %copy-done.9, f32[512]{0:T(512)S(1)} %bitcast.175, bf16[1,2,256,5120]{3,2,1,0:T(8,128)(2,1)} %param.7), kind=kLoop, calls=%fused_computation.16 | loop fusion | flops 10485760 | bytes 10508288 | tf_op jit(solution)/shard_map/convert_element_type | solution.py:22
  26.0 4.3 %multiply_convert_fusion.1 = bf16[1,2,256,5120]{3,2,1,0:T(8,128)(2,1)} fusion(f32[5120]{0:T(1024)S(1)} %copy-done.9, f32[2,256]{1,0:T(2,128)S(1)} %get-tuple-element.13, bf16[1,2,256,5120]{3,2,1,0:T(8,128)(2,1)S(1)} %bitcast.155), kind=kLoop, calls=%fused_computation.19 | loop fusion | flops 10485760 | bytes 10508288 | tf_op jit(solution)/shard_map/convert_element_type | solution.py:22
  30.3 70.6 %all-gather.7.cloned.1.call-done = bf16[1,5120,1024]{2,1,0:T(8,128)(2,1)} async-done(((bf16[1,320,1024]{2,1,0:T(8,128)(2,1)}), bf16[1,5120,1024]{2,1,0:T(8,128)(2,1)}) %all-gather.7.cloned.1.call-update) | async-done | bytes 10485776 | tf_op jit(solution)/shard_map/all_gather | solution.py:92
  100.9 10.0 %multiply_convert_fusion.2 = bf16[512,1024]{1,0:T(8,128)(2,1)S(1)} fusion(bf16[512,5120]{1,0:T(8,128)(2,1)} %fusion.11, bf16[1,5120,1024]{2,1,0:T(8,128)(2,1)} %all-gather.7.cloned.1.call-done), kind=kOutput, calls=%fused_computation.34 | convolution fusion | flops 5369757696 | bytes 16777216 | tf_op jit(solution)/shard_map/dot_general | solution.py:90
  111.8 2.0 copy.60
  113.8 2.9 fusion.14
  116.7 2.6 fusion.16
  119.3 1.4 copy-done
  120.7 1.0 copy.61
  121.7 7.7 %fusion.37 = bf16[2,4,256,128]{2,3,1,0:T(8,128)(2,1)S(1)} fusion(bf16[2,4,128,5,256]{4,2,3,1,0:T(8,128)(2,1)} %bitcast.165, f32[2,4,256,256,5]{3,2,4,1,0:T(8,128)} %copy-done, f32[2,4,5,256]{3,2,1,0:T(8,128)S(1)} %fusion.16, f32[2,4,5,256]{3,2,1,0:T(8,128)S(1)} %get-tuple-element.14, pred[256,256]{0,1:T(8,128)(4,1)S(1)} %iota_compare_fusion.1), kind=kOutput, calls=%fused_computation.49 | convolution fusion | flops 684457984 | bytes 13778944 | tf_op jit(solution)/shard_map/transpose(jvp(sgrlm,smgd->slgrd))/dot_general | solution.py:42
  129.8 5.3 %fusion.7 = (f32[2,4,5,256]{3,2,1,0:T(8,128)S(1)}, bf16[2,4,256,5,256]{4,2,3,1,0:T(8,128)(2,1)}) fusion(f32[2,4,256,256,5]{3,2,4,1,0:T(8,128)S(1)} %bitcast.157, f32[2,4,5,256]{3,2,1,0:T(8,128)S(1)} %multiply_divide_fusion, f32[2,4,5,256]{3,2,1,0:T(8,128)S(1)} %get-tuple-element.14, pred[256,256]{0,1:T(8,128)(4,1)S(1)} %iota_compare_fusion.1, ...), kind=kOutput, calls=%fused_computation.10 | convolution fusion | flops 692049920 | bytes 19062784 | tf_op jit(solution)/shard_map/transpose(jvp(sgrlm,smgd->slgrd))/dot_general | solution.py:42
  135.1 6.5 %fusion.34 = bf16[2,4,256,128]{2,3,1,0:T(8,128)(2,1)S(1)} fusion(bf16[2,256,4,5,128]{1,4,3,2,0:T(8,128)(2,1)S(1)} %bitcast.159, bf16[2,4,256,5,256]{4,2,3,1,0:T(8,128)(2,1)} %get-tuple-element.17, f32[2,4,256,256,5]{3,2,4,1,0:T(8,128)S(1)} %bitcast.157, f32[2,4,256,5]{2,3,1,0:T(8,128)S(1)} %bitcast.173, f32[2,4,256,5]{2,3,1,0:T(8,128)S(1)} %negate_bitcast_fusion, ...), kind=kOutput, calls=%fused_computation.48 | convolution fusion | flops 694943744 | bytes 19062784 | tf_op jit(solution)/shard_map/transpose(jvp(slgrd,smgd->sgrlm))/dot_general | solution.py:33
  142.2 10.9 %multiply_convert_fusion = bf16[5120,1024]{1,0:T(8,128)(2,1)} fusion(bf16[512,5120]{1,0:T(8,128)(2,1)} %bitcast.161, bf16[512,1024]{1,0:T(8,128)(2,1)S(1)} %bitcast.169), kind=kOutput, calls=%fused_computation | convolution fusion | flops 5379194880 | bytes 16777216 | tf_op jit(solution)/shard_map/dot_general | solution.py:78
  153.2 117.4 %reduce-scatter.2.cloned.1.call-done = bf16[320,1024]{1,0:T(8,128)(2,1)} async-done(((bf16[5120,1024]{1,0:T(8,128)(2,1)}), bf16[320,1024]{1,0:T(8,128)(2,1)}) %reduce-scatter.2.cloned.1.call-update) | async-done | bytes 655376 | tf_op jit(solution)/shard_map/reduce_scatter | solution.py:99
  270.5 1.5 abs_bitcast_fusion
  272.0 1.3 copy.63
  273.3 1.7 reduce_max.19
  275.5 1.5 fusion.33
  277.0 4.4 %all-gather.3 = bf16[2,320,8]{1,2,0:T(8,128)(2,1)S(1)} all-gather(bf16[1,320,8]{1,2,0:T(8,128)(2,1)S(1)} %copy.47), channel_id=4, replica_groups=mesh['group'=2,'fsdp'=16] {'group'}, dimensions={0}, use_global_device_ids=true | all-gather | bytes 15360 | tf_op jit(solution)/shard_map/all_gather | solution.py:109
  281.7 19.4 %all-gather.9.cloned.1.call-done = bf16[640,1024]{1,0:T(8,128)(2,1)} async-done(((bf16[320,1024]{1,0:T(8,128)(2,1)}), bf16[640,1024]{1,0:T(8,128)(2,1)}) %all-gather.9.cloned.1.call-update) | async-done | bytes 1310736 | tf_op jit(solution)/shard_map/all_gather | solution.py:108
  301.9 4.5 %fusion.39 = (bf16[1,320,1024]{2,1,0:T(8,128)(2,1)}, f32[320,1024]{1,0:T(8,128)}, f32[320,1024]{1,0:T(8,128)}) fusion(bf16[320,1024]{1,0:T(8,128)(2,1)S(1)} %copy-done.5, bf16[1,320,1024]{2,1,0:T(8,128)(2,1)S(1)} %copy-done.4, f32[320,1024]{1,0:T(8,128)S(1)} %copy-done.1, f32[40,8,8,128]{3,2,1,0:T(8,128)S(1)} %bitcast.164, ...), kind=kLoop, calls=%fused_computation.52 | loop fusion | flops 6225920 | bytes 11141120 | tf_op jit(solution)/shard_map/broadcast_in_dim | solution.py:117
  (55 shorter events, 4.3 us)
Async XLA Ops:
  7.2 4.4 %copy-start.6 = (bf16[1,2,256,2560]{3,2,1,0:T(8,128)(2,1)S(1)}, bf16[1,2,256,2560]{3,2,1,0:T(8,128)(2,1)}, u32[]{:S(2)}) copy-start(bf16[1,2,256,2560]{3,2,1,0:T(8,128)(2,1)} %param.9) | copy-start | bytes 7864324
  7.2 93.7 %all-gather.7.cloned.1.call-start = ((), (), s32[]{:S(2)}) async-start(), calls=%async_computation.2 | async-start | bytes 11141120 | tf_op jit(solution)/shard_map/all_gather | solution.py:92
  7.9 262.6 %reduce-scatter.2.cloned.1.call-start = ((), (), s32[]{:S(2)}) async-start(), calls=%async_computation.1 | async-start | bytes 11141120 | tf_op jit(solution)/shard_map/reduce_scatter | solution.py:99
  11.6 7.2 %copy-start.9 = (f32[5120]{0:T(1024)S(1)}, f32[5120]{0:T(1024)}, u32[]{:S(2)}) copy-start(f32[5120]{0:T(1024)} %param.8) | copy-start | bytes 61444
  14.2 11.9 %slice-start = ((s8[5242880]{0:T(1024)(128)(4,1)}), s8[1048576]{0:T(1024)(128)(4,1)S(1)}, s32[]{:S(2)}) async-start(s8[5242880]{0:T(1024)(128)(4,1)} %bitcast.154), calls=%async_computation.4 | async-start | bytes 2097152
  18.7 7.3 %slice-start.1 = ((s8[5242880]{0:T(1024)(128)(4,1)}), s8[4194304]{0:T(1024)(128)(4,1)S(1)}, s32[]{:S(2)}) async-start(s8[5242880]{0:T(1024)(128)(4,1)} %bitcast.154), calls=%async_computation.5 | async-start | bytes 8388608
  30.3 83.5 %copy-start.2 = (bf16[1,2,256,2560]{2,3,1,0:T(8,128)(2,1)S(1)}, bf16[1,2,256,2560]{2,3,1,0:T(8,128)(2,1)}, u32[]{:S(2)}) copy-start(bf16[1,2,256,2560]{2,3,1,0:T(8,128)(2,1)} %copy.38) | copy-start | bytes 7864324
  116.7 4.0 %copy-start = (f32[2,4,256,256,5]{3,2,4,1,0:T(8,128)}, f32[2,4,256,256,5]{3,2,4,1,0:T(8,128)S(1)}, u32[]{:S(2)}) copy-start(f32[2,4,256,256,5]{3,2,4,1,0:T(8,128)S(1)} %get-tuple-element.15) | copy-start | bytes 31457284
  120.7 8.7 %slice-start.2 = ((s8[10485760]{0:T(1024)(128)(4,1)}), s8[2097152]{0:T(1024)(128)(4,1)S(1)}, s32[]{:S(2)}) async-start(s8[10485760]{0:T(1024)(128)(4,1)} %bitcast.156), calls=%async_computation.6 | async-start | bytes 4194304
  121.7 7.7 %slice-start.3 = ((s8[10485760]{0:T(1024)(128)(4,1)}), s8[4194304]{0:T(1024)(128)(4,1)S(1)}, s32[]{:S(2)}) async-start(s8[10485760]{0:T(1024)(128)(4,1)} %bitcast.156), calls=%async_computation.7 | async-start | bytes 8388608
  121.7 7.7 %slice-start.4 = ((s8[10485760]{0:T(1024)(128)(4,1)}), s8[4194304]{0:T(1024)(128)(4,1)S(1)}, s32[]{:S(2)}) async-start(s8[10485760]{0:T(1024)(128)(4,1)} %bitcast.156), calls=%async_computation.8 | async-start | bytes 8388608
  121.7 8.0 %copy-start.7 = (bf16[1,2,256,2560]{2,3,1,0:T(8,128)(2,1)S(1)}, bf16[1,2,256,2560]{2,3,1,0:T(8,128)(2,1)}, u32[]{:S(2)}) copy-start(bf16[1,2,256,2560]{2,3,1,0:T(8,128)(2,1)} %copy.41) | copy-start | bytes 7864324
  121.7 8.1 %copy-start.8 = (bf16[2,256,512]{1,2,0:T(8,128)(2,1)S(1)}, bf16[2,256,512]{1,2,0:T(8,128)(2,1)}, u32[]{:S(2)}) copy-start(bf16[2,256,512]{1,2,0:T(8,128)(2,1)} %copy.61) | copy-start | bytes 1572868
  129.8 5.3 %copy-start.3 = (bf16[1,2,256,2560]{2,3,1,0:T(8,128)(2,1)S(1)}, bf16[1,2,256,2560]{2,3,1,0:T(8,128)(2,1)}, u32[]{:S(2)}) copy-start(bf16[1,2,256,2560]{2,3,1,0:T(8,128)(2,1)} %copy.38) | copy-start | bytes 7864324
  153.1 117.4 %copy-start.1 = (f32[320,1024]{1,0:T(8,128)S(1)}, f32[320,1024]{1,0:T(8,128)}, u32[]{:S(2)}) copy-start(f32[320,1024]{1,0:T(8,128)} %param.12) | copy-start | bytes 3932164
  153.1 117.4 %copy-start.4 = (bf16[1,320,1024]{2,1,0:T(8,128)(2,1)S(1)}, bf16[1,320,1024]{2,1,0:T(8,128)(2,1)}, u32[]{:S(2)}) copy-start(bf16[1,320,1024]{2,1,0:T(8,128)(2,1)} %param.11) | copy-start | bytes 1966084
  153.1 148.0 %all-gather.9.cloned.1.call-start = ((), (), s32[]{:S(2)}) async-start(), calls=%async_computation.3 | async-start | bytes 1966080 | tf_op jit(solution)/shard_map/all_gather | solution.py:108
  270.5 5.0 %copy-start.5 = (bf16[320,1024]{1,0:T(8,128)(2,1)S(1)}, bf16[320,1024]{1,0:T(8,128)(2,1)}, u32[]{:S(2)}) copy-start(bf16[320,1024]{1,0:T(8,128)(2,1)} %reduce-scatter.2.cloned.1.call-done) | copy-start | bytes 1966084
Sparse Core Ops, SparseCore 0:
  10.3 90.5 all-gather.6
  153.2 117.2 reduce-scatter.1
  277.1 23.9 all-gather.8
where the time goes:
time: 313 us
  waiting for transfers between devices  208 us (66%)
  matrix products  43.3 us (14%)
  other arithmetic  27.1 us (9%)
  local copies, waits for them, and re-layouts  16.1 us (5%)
  between operations  14 us (4%)
  blocking collectives  4.36 us (1%)
    reduce_scatter x1, waiting for transfers between devices, local(): lax.psum_scatter(grad_term(rows_in, kv_grad, inv_root).astype(jnp.bfloat1...  117 us
    all_gather x1, waiting for transfers between devices, local(): lax.all_gather(local_weights, 'fsdp', axis=0, tiled=True)  70.6 us
    all_gather x1, waiting for transfers between devices, local(): lax.all_gather(coded[None], 'group', axis=0, tiled=True)  19.4 us
    unnamed x37, local copies, waits for them, and re-layouts  13.3 us
    dot_general x2, matrix products, attend(): jnp.einsum('sgrlm,smgd->slgrd', prob_rows, value_h, preferred_element_typ...  13 us
    convert_element_type x2, other arithmetic, normed_rows(): (looked * lax.rsqrt(mean_sq + norm_eps) * norm_gain).astype(jnp.bfloat16)  11.6 us
    dot_general x1, matrix products, grad_term(): lax.dot_general(rows_in, kv_part, (((0,), (0,)), ((), ())), preferred_ele...  10.9 us
    dot_general x1, matrix products, local(): jnp.dot(rows_in, lax.all_gather(local_weights, 'fsdp', axis=0, tiled=True...  10 us
  transfers between devices with their start and end apart: 3, of which 3 were waited for; matrix products, arithmetic and copies ran while one was open for 7% of the time, Pallas kernels for 0%

commit v1 on v0

v1 whole, which is shorter than its diff:
```python
import functools

import jax
import jax.numpy as jnp
import numpy as np
from jax import lax
from jax.experimental import pallas as pl
from jax.experimental.pallas import tpu as pltpu
from jax.sharding import PartitionSpec as P

HD = 128

inner_rate = 0.25
outer_rate = 0.7
momentum_decay = 0.9
blend_share = 0.5
norm_eps = 1e-06
scale_eps = 1e-06

F32 = jnp.float32
BF16 = jnp.bfloat16
VMEM_LIMIT = 56 * 1024 * 1024
SCALE_ROWS = 16


def ring_order(count):
    return list(range(0, count, 2)) + list(range(1, count, 2))[::-1]


def call(body, out_shape, in_specs, out_specs, grid=(1,), scratch=(), flops=0, moved=0, name=None):
    return pl.pallas_call(
        body,
        out_shape=out_shape,
        grid_spec=pltpu.PrefetchScalarGridSpec(
            num_scalar_prefetch=1,
            grid=grid,
            in_specs=in_specs,
            out_specs=out_specs,
            scratch_shapes=list(scratch),
        ),
        compiler_params=pltpu.CompilerParams(
            vmem_limit_bytes=VMEM_LIMIT, dimension_semantics=("arbitrary",) * len(grid)
        ),
        cost_estimate=pl.CostEstimate(flops=int(flops), bytes_accessed=int(moved), transcendentals=0),
        name=name,
    )


def whole(shape):
    zeros = (0,) * len(shape)
    return pl.BlockSpec(shape, lambda i, s: zeros)


def dot_nn(a, b):
    return lax.dot_general(a, b, (((1,), (0,)), ((), ())), preferred_element_type=F32)


def dot_nt(a, b):
    return lax.dot_general(a, b, (((1,), (1,)), ((), ())), preferred_element_type=F32)


def dot_tn(a, b):
    return lax.dot_general(a, b, (((0,), (0,)), ((), ())), preferred_element_type=F32)


def norm_rows(scalars, hidden_rows, norm_gain, chips):
    tokens, width = hidden_rows.shape
    part = width // chips
    tile = 128

    def body(s, x_ref, g_ref, o_ref):
        total = jnp.zeros((tile, 1), F32)
        for b in range(chips):
            x = x_ref[:, b * part : (b + 1) * part].astype(F32)
            total = total + jnp.sum(x * x, axis=-1, keepdims=True)
        factor = lax.rsqrt(total * (1.0 / width) + norm_eps)
        for b in range(chips):
            x = x_ref[:, b * part : (b + 1) * part].astype(F32)
            o_ref[b] = (x * factor * g_ref[:, b * part : (b + 1) * part]).astype(BF16)

    return call(
        body,
        jax.ShapeDtypeStruct((chips, tokens, part), BF16),
        [pl.BlockSpec((tile, width), lambda i, s: (i, 0)), whole((1, width))],
        pl.BlockSpec((chips, tile, part), lambda i, s: (0, i, 0)),
        grid=(tokens // tile,),
        flops=tokens * width * 6,
        moved=tokens * width * 4,
        name="norm",
    )(scalars, hidden_rows, norm_gain.reshape(1, width))


def columns_of(core, head, kv, heads, kv_width):
    return pl.multiple_of(kv * kv_width + (core * heads + head) * HD, HD)


def pick_columns(scalars, weight, heads, name):
    rows, cols = weight.shape

    def body(s, w_ref, o_ref):
        other = 1 - s[0]
        for h in range(heads):
            for kv in range(2):
                at = (h * 2 + kv) * HD
                o_ref[:, at : at + HD] = w_ref[:, pl.ds(columns_of(other, h, kv, heads, cols // 2), HD)]

    return call(
        body,
        jax.ShapeDtypeStruct((rows, cols // 2), weight.dtype),
        [whole((rows, cols))],
        whole((rows, cols // 2)),
        moved=rows * cols * 3,
        name=name,
    )(scalars, weight)


def own_blocks(scalars, weight, received, heads):
    rows, cols = weight.shape

    def body(s, w_ref, r_ref, *o_refs):
        core = s[0]
        mine = pl.multiple_of(core * rows, 16)
        theirs = pl.multiple_of((1 - core) * rows, 16)
        for h in range(heads):
            for kv in range(2):
                at = (h * 2 + kv) * HD
                o_refs[h][pl.ds(mine, rows), kv * HD : (kv + 1) * HD] = w_ref[
                    :, pl.ds(columns_of(core, h, kv, heads, cols // 2), HD)
                ]
                o_refs[h][pl.ds(theirs, rows), kv * HD : (kv + 1) * HD] = r_ref[:, at : at + HD]

    shape = (2 * rows, 2 * HD)
    return call(
        body,
        [jax.ShapeDtypeStruct(shape, weight.dtype)] * heads,
        [whole((rows, cols)), whole((rows, cols // 2))],
        [whole(shape)] * heads,
        moved=rows * cols * 5,
        name="own_blocks",
    )(scalars, weight, received)


def start_deltas(scalars, blocks, outer, received, heads):
    rows, cols = outer.shape

    def body(s, o_ref, r_ref, *refs):
        core = s[0]
        for h in range(heads):
            block_ref, out_ref = refs[h], refs[heads + h]
            for kv in range(2):
                at = (h * 2 + kv) * HD
                mine = o_ref[:, pl.ds(columns_of(core, h, kv, heads, cols // 2), HD)]
                theirs = r_ref[:, at : at + HD]
                first = jnp.where(core == 0, mine, theirs)
                second = jnp.where(core == 0, theirs, mine)
                both = jnp.concatenate([first, second], axis=0)
                both = both - block_ref[:, kv * HD : (kv + 1) * HD].astype(F32)
                out_ref[kv * HD : (kv + 1) * HD, :] = both.T

    return call(
        body,
        [jax.ShapeDtypeStruct((2 * HD, 2 * rows), F32)] * heads,
        [whole((rows, cols)), whole((rows, cols // 2))] + [whole((2 * rows, 2 * HD))] * heads,
        [whole((2 * HD, 2 * rows))] * heads,
        moved=rows * cols * 14,
        name="start_deltas",
    )(scalars, outer, received, *blocks)


def attention_grads(scalars, rows_mine, rows_other, blocks, halves, queries, queries_other, out_grad, out_grad_other, head, heads):
    chips, tokens, part = rows_mine.shape
    seqs, length, query_width = queries.shape
    repeat = query_width // (2 * heads * HD)
    inv_root = (chips * part) ** (-0.5)
    far = chips // 2
    half = length // 2
    places = [k for k in range(chips) if k != far]

    def body(s, a_ref, b_ref, qa_ref, qb_ref, ga_ref, gb_ref, *refs):
        block_refs = refs[: len(places)]
        half_refs = refs[len(places) : len(places) + 2]
        out_ref = refs[len(places) + 2]
        far_ref = refs[len(places) + 3]
        step = pl.program_id(0)

        @pl.when(step == 0)
        def _():
            far_ref[: part // 2, :] = half_refs[0][...]
            far_ref[part // 2 :, :] = half_refs[1][...]

        def work(x_ref, q_ref, g_ref):
            acc = dot_nn(x_ref[s[1 + far]], far_ref[...])
            for ref, k in zip(block_refs, places):
                acc = acc + dot_nn(x_ref[s[1 + k]], ref[...])
            kv = (acc * inv_root).astype(BF16)
            keys, values = kv[:, :HD], kv[:, HD:]
            key_grad = jnp.zeros((HD, length), F32)
            value_grad = jnp.zeros((HD, length), F32)
            for r in range(repeat):
                q_all = q_ref[0, :, r * HD : (r + 1) * HD]
                g_all = g_ref[0, :, r * HD : (r + 1) * HD]
                d_parts, p_parts = [], []
                for t in range(2):
                    cols = (t + 1) * half
                    q = q_all[t * half : (t + 1) * half]
                    g = g_all[t * half : (t + 1) * half]
                    scores = dot_nt(q, keys[:cols]) * HD ** (-0.5)
                    spot = lax.broadcasted_iota(jnp.int32, (half, cols), 0) + t * half
                    causal = lax.broadcasted_iota(jnp.int32, (half, cols), 1) <= spot
                    scores = jnp.where(causal, scores, -1e30)
                    highest = jnp.max(scores, axis=-1, keepdims=True)
                    exps = jnp.exp(scores - highest)
                    prob = exps * (1.0 / jnp.sum(exps, axis=-1, keepdims=True))
                    prob_grad = dot_nt(g, values[:cols]).astype(BF16).astype(F32)
                    weighted = prob * prob_grad
                    mean = jnp.sum(weighted, axis=-1, keepdims=True)
                    d_part = ((weighted - prob * mean) * HD ** (-0.5)).astype(BF16)
                    p_part = prob.astype(BF16)
                    if t == 0:
                        d_part = jnp.concatenate([d_part, jnp.zeros((half, length - cols), BF16)], axis=1)
                        p_part = jnp.concatenate([p_part, jnp.zeros((half, length - cols), BF16)], axis=1)
                    d_parts.append(d_part)
                    p_parts.append(p_part)
                key_grad = key_grad + dot_tn(q_all, jnp.concatenate(d_parts, axis=0))
                value_grad = value_grad + dot_tn(g_all, jnp.concatenate(p_parts, axis=0))
            out_ref[:HD, :] = key_grad.astype(BF16)
            out_ref[HD:, :] = value_grad.astype(BF16)

        @pl.when(step < seqs)
        def _():
            work(a_ref, qa_ref, ga_ref)

        @pl.when(step >= seqs)
        def _():
            work(b_ref, qb_ref, gb_ref)

    first = lambda i: jnp.minimum(i, seqs - 1)
    second = lambda i: jnp.maximum(i - seqs, 0)
    rows_spec = lambda pick: pl.BlockSpec((chips, length, part), lambda i, s: (0, pick(i), 0))
    mine_spec = pl.BlockSpec((1, length, repeat * HD), lambda i, s: (first(i), 0, s[0] * heads + head))
    other_spec = pl.BlockSpec((1, length, repeat * HD), lambda i, s: (second(i), 0, head))
    block = whole((part, 2 * HD))
    half_block = whole((part // 2, 2 * HD))
    work_flops = 2 * tokens * chips * part * 2 * HD * 2 + 2 * seqs * repeat * length * length * HD * 8 * 2
    return call(
        body,
        jax.ShapeDtypeStruct((2 * HD, 2 * tokens), BF16),
        [rows_spec(first), rows_spec(second), mine_spec, other_spec, mine_spec, other_spec]
        + [block] * len(places)
        + [half_block] * 2,
        pl.BlockSpec((2 * HD, length), lambda i, s: (0, i)),
        grid=(2 * seqs,),
        scratch=[pltpu.VMEM((part, 2 * HD), BF16)],
        flops=work_flops,
        moved=2 * tokens * chips * part * 2,
        name=f"attend_{head}",
    )(
        scalars, rows_mine, rows_other, queries, queries_other, out_grad, out_grad_other,
        *[blocks[k] for k in places], *halves,
    )


def far_partials(scalars, kv_grad, rows_mine, rows_other, name):
    chips, tokens, part = rows_mine.shape
    inv_root = (chips * part) ** (-0.5)
    far = chips // 2

    def body(s, k_ref, a_ref, b_ref, up_ref, down_ref):
        total = dot_nn(k_ref[:, :tokens], a_ref[0]) + dot_nn(k_ref[:, tokens:], b_ref[0])
        total = total * inv_root
        up_ref[...] = total[:HD].astype(BF16)
        down_ref[...] = total[HD:].astype(BF16)

    rows_spec = pl.BlockSpec((1, tokens, part), lambda i, s: (s[1 + far], 0, 0))
    shape = (HD, part)
    return call(
        body,
        [jax.ShapeDtypeStruct(shape, BF16)] * 2,
        [whole(kv_grad.shape), rows_spec, rows_spec],
        [whole(shape)] * 2,
        flops=2 * 2 * tokens * part * 2 * HD,
        moved=2 * tokens * part * 2,
        name=name,
    )(scalars, kv_grad, rows_mine, rows_other)


def near_partials(scalars, kv_grad, rows_mine, rows_other, up, down, distance, name):
    chips, tokens, part = rows_mine.shape
    inv_root = (chips * part) ** (-0.5)
    is_half = up.shape[0] == HD

    def body(s, k_ref, a_ref, b_ref, ui_ref, di_ref, up_ref, down_ref):
        step = pl.program_id(0)
        total = dot_nn(k_ref[:, :tokens], a_ref[0]) + dot_nn(k_ref[:, tokens:], b_ref[0])
        total = total * inv_root

        @pl.when(step == 0)
        def _():
            if is_half:
                up_ref[:HD, :] = (total[:HD] + ui_ref[...].astype(F32)).astype(BF16)
                up_ref[HD:, :] = total[HD:].astype(BF16)
            else:
                up_ref[...] = (total + ui_ref[...].astype(F32)).astype(BF16)

        @pl.when(step == 1)
        def _():
            if is_half:
                down_ref[:HD, :] = total[:HD].astype(BF16)
                down_ref[HD:, :] = (total[HD:] + di_ref[...].astype(F32)).astype(BF16)
            else:
                down_ref[...] = (total + di_ref[...].astype(F32)).astype(BF16)

    rows_spec = pl.BlockSpec(
        (1, tokens, part), lambda i, s: (jnp.where(i == 0, s[1 + distance], s[1 + chips - distance]), 0, 0)
    )
    shape = (2 * HD, part)
    return call(
        body,
        [jax.ShapeDtypeStruct(shape, BF16)] * 2,
        [whole(kv_grad.shape), rows_spec, rows_spec, whole(up.shape), whole(down.shape)],
        [whole(shape)] * 2,
        grid=(2,),
        flops=2 * 2 * 2 * tokens * part * 2 * HD,
        moved=2 * 2 * tokens * part * 2,
        name=name,
    )(scalars, kv_grad, rows_mine, rows_other, up, down)


def split_packs(values):
    deep = values.shape[0] // 2
    rows = values.shape[1] // 2
    return [
        jnp.concatenate([values[:deep, k * rows : (k + 1) * rows], values[deep:, k * rows : (k + 1) * rows]], axis=1)
        for k in range(2)
    ]


def code_deltas(scalars, kv_grad, rows_mine, rows_other, up, down, delta_start, name):
    chips, tokens, part = rows_mine.shape
    inv_root = (chips * part) ** (-0.5)

    def body(s, k_ref, a_ref, b_ref, ui_ref, di_ref, d_ref, own_ref, core_ref, y_ref, far_ref):
        core = s[0]
        total = dot_nn(k_ref[:, :tokens], a_ref[0]) + dot_nn(k_ref[:, tokens:], b_ref[0])
        total = total * inv_root + ui_ref[...].astype(F32) + di_ref[...].astype(F32)
        delta = d_ref[...] + inner_rate * total
        scales, coded = [], []
        for kv in range(2):
            piece = delta[kv * HD : (kv + 1) * HD]
            scale = (jnp.max(jnp.abs(piece), axis=0, keepdims=True) + scale_eps).astype(BF16).astype(F32)
            scales.append(scale)
            coded.append(piece / scale)
        grads = split_packs(total)
        codes = split_packs(jnp.concatenate(coded, axis=0))
        levels = split_packs(jnp.concatenate(scales, axis=0))
        for mine, wide_ref, thin_ref in ((True, own_ref, y_ref), (False, core_ref, far_ref)):
            first = (core == 0) if mine else (core == 1)
            grad = jnp.where(first, grads[0], grads[1]).astype(BF16)
            code = jnp.where(first, codes[0], codes[1]).astype(BF16)
            level = jnp.where(first, levels[0], levels[1])
            level = jnp.broadcast_to(level, (SCALE_ROWS, part)).astype(BF16)
            wide_ref[:HD, :] = code
            wide_ref[HD : HD + SCALE_ROWS, :] = level
            wide_ref[HD + SCALE_ROWS :, :] = grad
            thin_ref[:HD, :] = code
            thin_ref[HD:, :] = level

    rows_spec = pl.BlockSpec((1, tokens, part), lambda i, s: (s[1], 0, 0))
    wide, thin = (2 * HD + SCALE_ROWS, part), (HD + SCALE_ROWS, part)
    return call(
        body,
        [jax.ShapeDtypeStruct(shape, BF16) for shape in (wide, wide, thin, thin)],
        [whole(kv_grad.shape), rows_spec, rows_spec, whole(up.shape), whole(down.shape), whole(delta_start.shape)],
        [whole(wide), whole(wide), whole(thin), whole(thin)],
        flops=2 * 2 * tokens * part * 2 * HD,
        moved=2 * tokens * part * 2,
        name=name,
    )(scalars, kv_grad, rows_mine, rows_other, up, down, delta_start)


def finish(scalars, weight, outer, momentum, grads, codes, heads):
    rows, cols = weight.shape
    groups = len(codes[0][0])
    packs = []
    for h in range(heads):
        for side in range(2):
            packs.append(grads[h][side])
            packs.extend(codes[h][side])

    def body(s, w_ref, k_ref, m_ref, *refs):
        pack_refs = refs[: len(packs)]
        blend_ref, outer_ref, moment_ref = refs[len(packs) :]
        at = 0
        for h in range(heads):
            for side in range(2):
                grad_ref = pack_refs[at]
                code_refs = pack_refs[at + 1 : at + 1 + groups]
                at += 1 + groups
                core = s[0] if side == 0 else 1 - s[0]
                for kv in range(2):
                    lanes = slice(kv * rows, (kv + 1) * rows)
                    grad = grad_ref[HD + SCALE_ROWS :, lanes].astype(F32).T
                    total = jnp.zeros((HD, rows), F32)
                    for ref in code_refs:
                        total = total + ref[:HD, lanes].astype(F32) * ref[HD : HD + 1, lanes].astype(F32)
                    average = (total / groups).T
                    where = pl.ds(columns_of(core, h, kv, heads, cols // 2), HD)
                    fresh = w_ref[:, where].astype(F32) - inner_rate * grad
                    moment = momentum_decay * m_ref[:, where] + average
                    stepped = k_ref[:, where] - outer_rate * (momentum_decay * moment + average)
                    moment_ref[:, where] = moment
                    outer_ref[:, where] = stepped
                    blend_ref[:, where] = (blend_share * fresh + (1.0 - blend_share) * stepped).astype(BF16)

    full = whole((rows, cols))
    return call(
        body,
        [
            jax.ShapeDtypeStruct((rows, cols), BF16),
            jax.ShapeDtypeStruct((rows, cols), F32),
            jax.ShapeDtypeStruct((rows, cols), F32),
        ],
        [full] * 3 + [whole(p.shape) for p in packs],
        [full] * 3,
        moved=rows * cols * 24,
        name="finish",
    )(scalars, weight, outer, momentum, *packs)


def local(hidden, norm_gain, queries, out_grad, kv_inner, kv_outer, momentum):
    count = lax.axis_size("fsdp")
    groups = lax.axis_size("group")
    index = lax.axis_index("fsdp")
    group = lax.axis_index("group")
    chips = count // 2
    far = chips // 2
    ring = ring_order(chips)
    place = {chip: at for at, chip in enumerate(ring)}
    walks = np.array([[ring[(place[j] + k) % chips] for k in range(chips)] for j in range(chips)], np.int32)
    core = index % 2
    scalars = jnp.concatenate([core[None].astype(jnp.int32), jnp.asarray(walks)[index // 2]])

    def around(shift):
        return [(2 * j + c, 2 * ring[(place[j] + shift) % chips] + c) for j in range(chips) for c in range(2)]

    up = functools.partial(lax.ppermute, axis_name="fsdp", perm=around(1))
    down = functools.partial(lax.ppermute, axis_name="fsdp", perm=around(-1))
    swap = functools.partial(lax.ppermute, axis_name="fsdp", perm=[(i, i ^ 1) for i in range(count)])

    def across(values, shift, flip):
        pairs = [
            (g * count + i, (g + shift) % groups * count + (i ^ flip)) for g in range(groups) for i in range(count)
        ]
        return lax.ppermute(values, ("group", "fsdp"), pairs)

    weight = kv_inner[0]
    rows, cols = weight.shape
    heads = cols // 2 // HD // 2
    seqs, length, width = hidden.shape[1:]
    half_width = queries.shape[-1] // 2

    received = swap(pick_columns(scalars, weight, heads, "pick_inner"))
    own = own_blocks(scalars, weight, received, heads)

    blocks = [{0: own[h]} for h in range(heads)]
    halves = [None] * heads
    part = 2 * rows
    ups, downs = list(own), list(own)
    for step in range(1, far + 1):
        for h in range(heads):
            if step < far:
                ups[h], downs[h] = up(ups[h]), down(downs[h])
                blocks[h][chips - step], blocks[h][step] = ups[h], downs[h]
            else:
                halves[h] = (up(ups[h][: part // 2]), down(downs[h][part // 2 :]))

    rows_mine = norm_rows(scalars, hidden.reshape(seqs * length, width), norm_gain, chips)
    rows_other = swap(rows_mine)
    at = ((1 - core) * half_width).astype(jnp.int32)
    queries_other = swap(lax.dynamic_slice_in_dim(queries[0], at, half_width, axis=2))
    out_grad_other = swap(lax.dynamic_slice_in_dim(out_grad[0], at, half_width, axis=2))
    outer_other = swap(pick_columns(scalars, kv_outer, heads, "pick_outer"))
    deltas = start_deltas(scalars, own, kv_outer, outer_other, heads)

    kv_grad = [
        attention_grads(
            scalars, rows_mine, rows_other, blocks[h], halves[h],
            queries[0], queries_other, out_grad[0], out_grad_other, h, heads,
        )
        for h in range(heads)
    ]

    grads, codes = [], []
    for h in range(heads):
        going_up, going_down = far_partials(scalars, kv_grad[h], rows_mine, rows_other, f"far_{h}")
        for distance in range(far - 1, 0, -1):
            going_up, going_down = near_partials(
                scalars, kv_grad[h], rows_mine, rows_other, up(going_up), down(going_down), distance, f"near_{h}_{distance}"
            )
        own_pack, core_pack, thin_own, thin_core = code_deltas(
            scalars, kv_grad[h], rows_mine, rows_other, up(going_up), down(going_down), deltas[h], f"code_{h}"
        )
        from_core = swap(core_pack)
        mine = [own_pack] + [across(thin_own, k, 0) for k in range(1, groups)]
        theirs = [from_core] + [across(thin_core, k, 1) for k in range(1, groups)]
        if groups > 2:
            deep = HD + SCALE_ROWS
            ordered = []
            for packs in (mine, theirs):
                stacked = jnp.stack([p[:deep] for p in packs])
                ordered.append([stacked[(group - g) % groups] for g in range(groups)])
            mine_codes, their_codes = ordered
        else:
            mine_codes, their_codes = mine, theirs
        grads.append((own_pack, from_core))
        codes.append((mine_codes, their_codes))

    blended, outer_new, momentum_new = finish(scalars, weight, kv_outer, momentum, grads, codes, heads)
    return (blended[None], outer_new, momentum_new)


def solution(mesh):
    in_specs = (
        P("group", "fsdp", None, None),
        P(),
        P("group", "fsdp", None, None),
        P("group", "fsdp", None, None),
        P("group", "fsdp", None),
        P("fsdp", None),
        P("fsdp", None),
    )
    out_specs = (P("group", "fsdp", None), P("fsdp", None), P("fsdp", None))
    return jax.shard_map(local, mesh=mesh, in_specs=in_specs, out_specs=out_specs, check_vma=False)
```

time: 313 us -> 226 us (0.72)
  waiting for transfers between devices: 208 us -> 60.7 us
  Pallas kernels: 0 us -> 111 us
  matrix products: 43.3 us -> 0 us
  starting transfers between devices: 0.12 us -> 37.7 us
  other arithmetic: 27.1 us -> 0.61 us
  between operations: 14 us -> 0.97 us
  blocking collectives: 4.36 us -> 0 us
    reduce_scatter x1 -> x0, waiting for transfers between devices: 117 us -> none  [local(): lax.psum_scatter(grad_term(rows_in, kv_grad, inv_root).astype(jnp.bfloat1...]
    pallas_call x0 -> x18, Pallas kernels: none -> 111 us  [the longest x2 42.4 us: attention_grads(): call(body, jax.ShapeDtypeStruct((2 * HD, 2 * tokens), BF16), [rows_spec(f...]
    all_gather x2 -> x0, waiting for transfers between devices: 90 us -> none  [the longest x1 70.6 us: local(): lax.all_gather(local_weights, 'fsdp', axis=0, tiled=True)]
    ppermute x0 -> x43, waiting for transfers between devices: none -> 60.7 us  [the longest x12 36.5 us: local(): ups[h], downs[h] = (up(ups[h]), down(downs[h]))]
    dot_general x6 -> x0, matrix products: 43.3 us -> none  [the longest x2 13 us: attend(): jnp.einsum('sgrlm,smgd->slgrd', prob_rows, value_h, preferred_element_typ...]
    ppermute x0 -> x43, starting transfers between devices: none -> 37.7 us  [the longest x12 13.2 us: local(): ups[h], downs[h] = (up(ups[h]), down(downs[h]))]
    convert_element_type x5 -> x0, other arithmetic: 13.1 us -> none  [the longest x2 11.6 us: normed_rows(): (looked * lax.rsqrt(mean_sq + norm_eps) * norm_gain).astype(jnp.bfloat16)]
    reduce_sum x2 -> x0, other arithmetic: 6.14 us -> none  [the longest x1 3.59 us: normed_rows(): mean_sq = jnp.mean(looked * looked, axis=-1, keepdims=True)]
  transfers between devices with their start and end apart: 3 -> 43, of which waited for: 3 -> 16; matrix products, arithmetic and copies ran while one was open for 7% -> 0% of each run, Pallas kernels for 0% -> 43%
where the time goes in v1:
time: 226 us
  Pallas kernels  111 us (49%)
  waiting for transfers between devices  60.7 us (27%)
  starting transfers between devices  37.7 us (17%)
  local copies, waits for them, and re-layouts  15.1 us (7%)
    pallas_call x2, Pallas kernels, attention_grads(): call(body, jax.ShapeDtypeStruct((2 * HD, 2 * tokens), BF16), [rows_spec(f...  42.4 us
    ppermute x12, waiting for transfers between devices, local(): ups[h], downs[h] = (up(ups[h]), down(downs[h]))  36.5 us
    pallas_call x6, Pallas kernels, near_partials(): call(body, [jax.ShapeDtypeStruct(shape, BF16)] * 2, [whole(kv_grad.shape)...  26.7 us
    unnamed x90, local copies, waits for them, and re-layouts  14.2 us
    ppermute x12, starting transfers between devices, local(): ups[h], downs[h] = (up(ups[h]), down(downs[h]))  13.2 us
    ppermute x8, starting transfers between devices, local(): up(going_up)  12.7 us
    ppermute x4, waiting for transfers between devices, across(): return lax.ppermute(values, ('group', 'fsdp'), pairs)  12.5 us
    pallas_call x2, Pallas kernels, code_deltas(): call(body, [jax.ShapeDtypeStruct(shape, BF16) for shape in (wide, wide, t...  8.73 us
  transfers between devices with their start and end apart: 43, of which 16 were waited for; matrix products, arithmetic and copies ran while one was open for 0% of the time, Pallas kernels for 43%

profile of v1, /device:TPU:0, one launch (start us, length us, event | category | flops | bytes accessed | tf_op | source)
XLA Modules:
  0.0 225.8 jit_solution(4551917596346458682)
XLA Ops:
  2.0 7.4 %norm.1.a_ref = bf16[8,512,640]{2,1,0:T(8,128)(2,1)} custom-call(s32[9]{0:T(128)} %pad_add_fusion.s, bf16[512,5120]{1,0:T(8,128)(2,1)} %bitcast.20, f32[1,5120]{1,0:T(1,128)} %bitcast.21), custom_call_target="tpu_custom_call" | custom-call | flops 15728640 | bytes 10485760 | tf_op jit(solution)/shard_map/norm/pallas_call | solution.py:81
  12.4 6.3 %collective-permute-done.3.r_ref = bf16[320,512]{1,0:T(8,128)(2,1)S(1)} collective-permute-done((bf16[320,512]{1,0:T(8,128)(2,1)}, bf16[320,512]{1,0:T(8,128)(2,1)S(1)}, u32[]{:S(2)}, u32[]{:S(2)}) %collective-permute-start.3) | collective-permute-done | bytes 327712 | tf_op jit(solution)/shard_map/ppermute | solution.py:462
  27.4 6.5 %collective-permute-done.27.refs_6_ = bf16[640,256]{1,0:T(8,128)(2,1)S(1)} collective-permute-done((bf16[640,256]{1,0:T(8,128)(2,1)}, bf16[640,256]{1,0:T(8,128)(2,1)S(1)}, u32[]{:S(2)}, u32[]{:S(2)}) %collective-permute-start.27) | collective-permute-done | bytes 327712 | tf_op jit(solution)/shard_map/ppermute | solution.py:472
  36.9 4.1 %collective-permute-done.7.refs_6_ = bf16[640,256]{1,0:T(8,128)(2,1)S(1)} collective-permute-done((bf16[640,256]{1,0:T(8,128)(2,1)}, bf16[640,256]{1,0:T(8,128)(2,1)S(1)}, u32[]{:S(2)}, u32[]{:S(2)}) %collective-permute-start.7) | collective-permute-done | bytes 327712 | tf_op jit(solution)/shard_map/ppermute | solution.py:472
  43.2 4.3 %collective-permute-done.28.refs_5_ = bf16[640,256]{1,0:T(8,128)(2,1)S(1)} collective-permute-done((bf16[640,256]{1,0:T(8,128)(2,1)S(1)}, bf16[640,256]{1,0:T(8,128)(2,1)S(1)}, u32[]{:S(2)}, u32[]{:S(2)}) %collective-permute-start.28) | collective-permute-done | bytes 327712 | tf_op jit(solution)/shard_map/ppermute | solution.py:472
  49.5 7.2 %collective-permute-done.8.refs_5_ = bf16[640,256]{1,0:T(8,128)(2,1)S(1)} collective-permute-done((bf16[640,256]{1,0:T(8,128)(2,1)S(1)}, bf16[640,256]{1,0:T(8,128)(2,1)S(1)}, u32[]{:S(2)}, u32[]{:S(2)}) %collective-permute-start.8) | collective-permute-done | bytes 327712 | tf_op jit(solution)/shard_map/ppermute | solution.py:472
  58.8 6.3 %collective-permute-done.29.refs_4_ = bf16[640,256]{1,0:T(8,128)(2,1)S(1)} collective-permute-done((bf16[640,256]{1,0:T(8,128)(2,1)S(1)}, bf16[640,256]{1,0:T(8,128)(2,1)S(1)}, u32[]{:S(2)}, u32[]{:S(2)}) %collective-permute-start.29) | collective-permute-done | bytes 327712 | tf_op jit(solution)/shard_map/ppermute | solution.py:472
  67.1 5.8 %collective-permute-done.9.refs_4_ = bf16[640,256]{1,0:T(8,128)(2,1)S(1)} collective-permute-done((bf16[640,256]{1,0:T(8,128)(2,1)S(1)}, bf16[640,256]{1,0:T(8,128)(2,1)S(1)}, u32[]{:S(2)}, u32[]{:S(2)}) %collective-permute-start.9) | collective-permute-done | bytes 327712 | tf_op jit(solution)/shard_map/ppermute | solution.py:472
  80.3 21.2 %attend_1.1.k_ref = bf16[256,1024]{1,0:T(8,128)(2,1)} custom-call(s32[9]{0:T(128)} %pad_add_fusion.s, bf16[8,512,640]{2,1,0:T(8,128)(2,1)} %norm.1.a_ref, bf16[8,512,640]{2,1,0:T(8,128)(2,1)} %collective-permute-done.b_ref, bf16[2,256,2560]{2,1,0:T(8,128)(2,1)} %bitcast.13, bf16[2,256,1280]{2,1,0:T(8,128)(2,1)} %copy-done.2, bf16[2,256,2560]{2,1,0:T(8,128)(2,1)} %bitcast.15, ...), custom_call_target="tpu_custom_call" | custom-call | flops 5368709120 | bytes 10485760 | tf_op jit(solution)/shard_map/attend_1/pallas_call | solution.py:245
  101.5 3.4 %far_1.1 = (bf16[128,640]{1,0:T(8,128)(2,1)}, bf16[128,640]{1,0:T(8,128)(2,1)}) custom-call(s32[9]{0:T(128)} %pad_add_fusion.s, bf16[256,1024]{1,0:T(8,128)(2,1)} %attend_1.1.k_ref, bf16[8,512,640]{2,1,0:T(8,128)(2,1)} %norm.1.a_ref, bf16[8,512,640]{2,1,0:T(8,128)(2,1)} %collective-permute-done.b_ref), custom_call_target="tpu_custom_call" | custom-call | flops 335544320 | bytes 1310720 | tf_op jit(solution)/shard_map/far_1/pallas_call | solution.py:276
  108.3 21.2 %attend_0.1.k_ref = bf16[256,1024]{1,0:T(8,128)(2,1)} custom-call(s32[9]{0:T(128)} %pad_add_fusion.s, bf16[8,512,640]{2,1,0:T(8,128)(2,1)} %norm.1.a_ref, bf16[8,512,640]{2,1,0:T(8,128)(2,1)} %collective-permute-done.b_ref, bf16[2,256,2560]{2,1,0:T(8,128)(2,1)} %bitcast.14, bf16[2,256,1280]{2,1,0:T(8,128)(2,1)} %copy-done.2, bf16[2,256,2560]{2,1,0:T(8,128)(2,1)} %bitcast.16, ...), custom_call_target="tpu_custom_call" | custom-call | flops 5368709120 | bytes 10485760 | tf_op jit(solution)/shard_map/attend_0/pallas_call | solution.py:245
  129.5 3.4 %far_0.1 = (bf16[128,640]{1,0:T(8,128)(2,1)}, bf16[128,640]{1,0:T(8,128)(2,1)}) custom-call(s32[9]{0:T(128)} %pad_add_fusion.s, bf16[256,1024]{1,0:T(8,128)(2,1)} %attend_0.1.k_ref, bf16[8,512,640]{2,1,0:T(8,128)(2,1)} %norm.1.a_ref, bf16[8,512,640]{2,1,0:T(8,128)(2,1)} %collective-permute-done.b_ref), custom_call_target="tpu_custom_call" | custom-call | flops 335544320 | bytes 1310720 | tf_op jit(solution)/shard_map/far_0/pallas_call | solution.py:276
  136.2 4.3 %near_1_3.1 = (bf16[256,640]{1,0:T(8,128)(2,1)}, bf16[256,640]{1,0:T(8,128)(2,1)}) custom-call(s32[9]{0:T(128)} %pad_add_fusion.s, bf16[256,1024]{1,0:T(8,128)(2,1)} %attend_1.1.k_ref, bf16[8,512,640]{2,1,0:T(8,128)(2,1)} %norm.1.a_ref, bf16[8,512,640]{2,1,0:T(8,128)(2,1)} %collective-permute-done.b_ref, bf16[128,640]{1,0:T(8,128)(2,1)} %copy-done.40, ...), custom_call_target="tpu_custom_call" | custom-call | flops 671088640 | bytes 2621440 | tf_op jit(solution)/shard_map/near_1_3/pallas_call | solution.py:317
  143.9 4.4 %near_0_3.1 = (bf16[256,640]{1,0:T(8,128)(2,1)}, bf16[256,640]{1,0:T(8,128)(2,1)}) custom-call(s32[9]{0:T(128)} %pad_add_fusion.s, bf16[256,1024]{1,0:T(8,128)(2,1)} %attend_0.1.k_ref, bf16[8,512,640]{2,1,0:T(8,128)(2,1)} %norm.1.a_ref, bf16[8,512,640]{2,1,0:T(8,128)(2,1)} %collective-permute-done.b_ref, bf16[128,640]{1,0:T(8,128)(2,1)} %copy-done.42, ...), custom_call_target="tpu_custom_call" | custom-call | flops 671088640 | bytes 2621440 | tf_op jit(solution)/shard_map/near_0_3/pallas_call | solution.py:317
  153.7 4.5 %near_1_2.1 = (bf16[256,640]{1,0:T(8,128)(2,1)}, bf16[256,640]{1,0:T(8,128)(2,1)}) custom-call(s32[9]{0:T(128)} %pad_add_fusion.s, bf16[256,1024]{1,0:T(8,128)(2,1)} %attend_1.1.k_ref, bf16[8,512,640]{2,1,0:T(8,128)(2,1)} %norm.1.a_ref, bf16[8,512,640]{2,1,0:T(8,128)(2,1)} %collective-permute-done.b_ref, bf16[256,640]{1,0:T(8,128)(2,1)} %copy-done.19, ...), custom_call_target="tpu_custom_call" | custom-call | flops 671088640 | bytes 2621440 | tf_op jit(solution)/shard_map/near_1_2/pallas_call | solution.py:317
  161.6 4.5 %near_0_2.1 = (bf16[256,640]{1,0:T(8,128)(2,1)}, bf16[256,640]{1,0:T(8,128)(2,1)}) custom-call(s32[9]{0:T(128)} %pad_add_fusion.s, bf16[256,1024]{1,0:T(8,128)(2,1)} %attend_0.1.k_ref, bf16[8,512,640]{2,1,0:T(8,128)(2,1)} %norm.1.a_ref, bf16[8,512,640]{2,1,0:T(8,128)(2,1)} %collective-permute-done.b_ref, bf16[256,640]{1,0:T(8,128)(2,1)} %copy-done.20, ...), custom_call_target="tpu_custom_call" | custom-call | flops 671088640 | bytes 2621440 | tf_op jit(solution)/shard_map/near_0_2/pallas_call | solution.py:317
  172.5 4.5 %near_1_1.1 = (bf16[256,640]{1,0:T(8,128)(2,1)}, bf16[256,640]{1,0:T(8,128)(2,1)}) custom-call(s32[9]{0:T(128)} %pad_add_fusion.s, bf16[256,1024]{1,0:T(8,128)(2,1)} %attend_1.1.k_ref, bf16[8,512,640]{2,1,0:T(8,128)(2,1)} %norm.1.a_ref, bf16[8,512,640]{2,1,0:T(8,128)(2,1)} %collective-permute-done.b_ref, bf16[256,640]{1,0:T(8,128)(2,1)} %copy-done.15, ...), custom_call_target="tpu_custom_call" | custom-call | flops 671088640 | bytes 2621440 | tf_op jit(solution)/shard_map/near_1_1/pallas_call | solution.py:317
  180.5 4.5 %near_0_1.1 = (bf16[256,640]{1,0:T(8,128)(2,1)}, bf16[256,640]{1,0:T(8,128)(2,1)}) custom-call(s32[9]{0:T(128)} %pad_add_fusion.s, bf16[256,1024]{1,0:T(8,128)(2,1)} %attend_0.1.k_ref, bf16[8,512,640]{2,1,0:T(8,128)(2,1)} %norm.1.a_ref, bf16[8,512,640]{2,1,0:T(8,128)(2,1)} %collective-permute-done.b_ref, bf16[256,640]{1,0:T(8,128)(2,1)} %copy-done.16, ...), custom_call_target="tpu_custom_call" | custom-call | flops 671088640 | bytes 2621440 | tf_op jit(solution)/shard_map/near_0_1/pallas_call | solution.py:317
  187.9 3.6 %start_deltas.1 = (f32[256,640]{1,0:T(8,128)}, f32[256,640]{1,0:T(8,128)}) custom-call(s32[9]{0:T(128)} %pad_add_fusion.s, f32[320,1024]{1,0:T(8,128)} %k_ref.1, f32[320,512]{1,0:T(8,128)} %copy-done.10, bf16[640,256]{1,0:T(8,128)(2,1)} %get-tuple-element.34.refs_0_, bf16[640,256]{1,0:T(8,128)(2,1)} %get-tuple-element.43.refs_1_.refs_0_), custom_call_target="tpu_custom_call" | custom-call | bytes 4587520 | tf_op jit(solution)/shard_map/start_deltas/pallas_call | solution.py:160
  192.4 4.3 %code_1.1 = (bf16[272,640]{1,0:T(8,128)(2,1)}, bf16[272,640]{1,0:T(8,128)(2,1)}, bf16[144,640]{1,0:T(8,128)(2,1)}, bf16[144,640]{1,0:T(8,128)(2,1)}) custom-call(s32[9]{0:T(128)} %pad_add_fusion.s, bf16[256,1024]{1,0:T(8,128)(2,1)} %attend_1.1.k_ref, bf16[8,512,640]{2,1,0:T(8,128)(2,1)} %norm.1.a_ref, bf16[8,512,640]{2,1,0:T(8,128)(2,1)} %collective-permute-done.b_ref, ...), custom_call_target="tpu_custom_call" | custom-call | flops 335544320 | bytes 1310720 | tf_op jit(solution)/shard_map/code_1/pallas_call | solution.py:370
  199.0 4.4 %code_0.1 = (bf16[272,640]{1,0:T(8,128)(2,1)}, bf16[272,640]{1,0:T(8,128)(2,1)}, bf16[144,640]{1,0:T(8,128)(2,1)}, bf16[144,640]{1,0:T(8,128)(2,1)}) custom-call(s32[9]{0:T(128)} %pad_add_fusion.s, bf16[256,1024]{1,0:T(8,128)(2,1)} %attend_0.1.k_ref, bf16[8,512,640]{2,1,0:T(8,128)(2,1)} %norm.1.a_ref, bf16[8,512,640]{2,1,0:T(8,128)(2,1)} %collective-permute-done.b_ref, ...), custom_call_target="tpu_custom_call" | custom-call | flops 335544320 | bytes 1310720 | tf_op jit(solution)/shard_map/code_0/pallas_call | solution.py:370
  205.6 4.6 %collective-permute-done.42.refs_11_ = bf16[144,640]{1,0:T(8,128)(2,1)S(1)} collective-permute-done((bf16[144,640]{1,0:T(8,128)(2,1)S(1)}, bf16[144,640]{1,0:T(8,128)(2,1)S(1)}, u32[]{:S(2)}, u32[]{:S(2)}) %collective-permute-start.42) | collective-permute-done | bytes 184352 | tf_op jit(solution)/shard_map/ppermute | solution.py:454
  210.2 4.7 %collective-permute-done.21.refs_2_ = bf16[144,640]{1,0:T(8,128)(2,1)S(1)} collective-permute-done((bf16[144,640]{1,0:T(8,128)(2,1)}, bf16[144,640]{1,0:T(8,128)(2,1)S(1)}, u32[]{:S(2)}, u32[]{:S(2)}) %collective-permute-start.21) | collective-permute-done | bytes 184352 | tf_op jit(solution)/shard_map/ppermute | solution.py:454
  219.0 6.8 %finish.1 = (bf16[320,1024]{1,0:T(8,128)(2,1)}, f32[320,1024]{1,0:T(8,128)}, f32[320,1024]{1,0:T(8,128)}) custom-call(s32[9]{0:T(128)} %pad_add_fusion.s, bf16[320,1024]{1,0:T(8,128)(2,1)} %bitcast.19, f32[320,1024]{1,0:T(8,128)} %k_ref.1, f32[320,1024]{1,0:T(8,128)} %m_ref.1, bf16[272,640]{1,0:T(8,128)(2,1)} %get-tuple-element.45.refs_0_.refs_1_, ...), custom_call_target="tpu_custom_call" | custom-call | bytes 7864320 | tf_op jit(solution)/shard_map/finish/pallas_call | solution.py:416
  (178 shorter events, 72.6 us)
Async XLA Ops:
  9.4 70.3 %collective-permute-start = (bf16[8,512,640]{2,1,0:T(8,128)(2,1)}, bf16[8,512,640]{2,1,0:T(8,128)(2,1)}, u32[]{:S(2)}, u32[]{:S(2)}) collective-permute-start(bf16[8,512,640]{2,1,0:T(8,128)(2,1)} %norm.1.a_ref), channel_id=1, source_target_pairs={{0,1},{1,0},{2,3},{3,2},{4,5},{5,4},{6,7},{7,6},{8,9},{9,8},{10,11... | collective-permute-start | bytes 15728648 | tf_op jit(solution)/shard_map/ppermute | solution.py:478
  22.4 11.6 %collective-permute-start.27 = (bf16[640,256]{1,0:T(8,128)(2,1)}, bf16[640,256]{1,0:T(8,128)(2,1)S(1)}, u32[]{:S(2)}, u32[]{:S(2)}) collective-permute-start(bf16[640,256]{1,0:T(8,128)(2,1)} %get-tuple-element.43.refs_1_.refs_0_), channel_id=1, source_target_pairs={{0,4},{1,5},{2,0},{3,1},{4,8},{5,9},{6,2},{7,3},{8,12},{9,13},{10,... | collective-permute-start | bytes 983048 | tf_op jit(solution)/shard_map/ppermute | solution.py:472
  25.3 15.6 %collective-permute-start.7 = (bf16[640,256]{1,0:T(8,128)(2,1)}, bf16[640,256]{1,0:T(8,128)(2,1)S(1)}, u32[]{:S(2)}, u32[]{:S(2)}) collective-permute-start(bf16[640,256]{1,0:T(8,128)(2,1)} %get-tuple-element.34.refs_0_), channel_id=1, source_target_pairs={{0,4},{1,5},{2,0},{3,1},{4,8},{5,9},{6,2},{7,3},{8,12},{9,13},{10,... | collective-permute-start | bytes 983048 | tf_op jit(solution)/shard_map/ppermute | solution.py:472
  27.3 15.8 %collective-permute-start.4 = (bf16[640,256]{1,0:T(8,128)(2,1)}, bf16[640,256]{1,0:T(8,128)(2,1)S(1)}, u32[]{:S(2)}, u32[]{:S(2)}) collective-permute-start(bf16[640,256]{1,0:T(8,128)(2,1)} %get-tuple-element.34.refs_0_), channel_id=1, source_target_pairs={{0,2},{1,3},{2,6},{3,7},{4,0},{5,1},{6,10},{7,11},{8,4},{9,5},{10,... | collective-permute-start | bytes 983048 | tf_op jit(solution)/shard_map/ppermute | solution.py:472
  33.9 13.6 %collective-permute-start.28 = (bf16[640,256]{1,0:T(8,128)(2,1)S(1)}, bf16[640,256]{1,0:T(8,128)(2,1)S(1)}, u32[]{:S(2)}, u32[]{:S(2)}) collective-permute-start(bf16[640,256]{1,0:T(8,128)(2,1)S(1)} %collective-permute-done.27.refs_6_), channel_id=1, source_target_pairs={{0,4},{1,5},{2,0},{3,1},{4,8},{5,9},{6,2},{7,3},{8,12},{9,13},{10,... | collective-permute-start | bytes 983048 | tf_op jit(solution)/shard_map/ppermute | solution.py:472
  36.1 13.2 %collective-permute-start.25 = (bf16[640,256]{1,0:T(8,128)(2,1)S(1)}, bf16[640,256]{1,0:T(8,128)(2,1)S(1)}, u32[]{:S(2)}, u32[]{:S(2)}) collective-permute-start(bf16[640,256]{1,0:T(8,128)(2,1)S(1)} %collective-permute-done.24.refs_1_), channel_id=1, source_target_pairs={{0,2},{1,3},{2,6},{3,7},{4,0},{5,1},{6,10},{7,11},{8,4},{9,5},{10,... | collective-permute-start | bytes 983048 | tf_op jit(solution)/shard_map/ppermute | solution.py:472
  41.0 34.1 %collective-permute-start.1 = (bf16[2,256,1280]{2,1,0:T(8,128)(2,1)S(1)}, bf16[2,256,1280]{2,1,0:T(8,128)(2,1)S(1)}, u32[]{:S(2)}, u32[]{:S(2)}) collective-permute-start(bf16[2,256,1280]{2,1,0:T(8,128)(2,1)S(1)} %dynamic-slice_bitcast_fusion.1), channel_id=1, source_target_pairs={{0,1},{1,0},{2,3},{3,2},{4,5},{5,4},{6,7},{7,6},{8,9},{9,8},{10,11... | collective-permute-start | bytes 3932168 | tf_op jit(solution)/shard_map/ppermute | solution.py:480
  43.2 33.3 %collective-permute-start.2 = (bf16[2,256,1280]{2,1,0:T(8,128)(2,1)S(1)}, bf16[2,256,1280]{2,1,0:T(8,128)(2,1)S(1)}, u32[]{:S(2)}, u32[]{:S(2)}) collective-permute-start(bf16[2,256,1280]{2,1,0:T(8,128)(2,1)S(1)} %dynamic-slice_bitcast_fusion), channel_id=1, source_target_pairs={{0,1},{1,0},{2,3},{3,2},{4,5},{5,4},{6,7},{7,6},{8,9},{9,8},{10,11... | collective-permute-start | bytes 3932168 | tf_op jit(solution)/shard_map/ppermute | solution.py:481
  75.0 31.9 %collective-permute-start.10 = (bf16[320,256]{1,0:T(8,128)(2,1)S(1)}, bf16[320,256]{1,0:T(8,128)(2,1)S(1)}, u32[]{:S(2)}, u32[]{:S(2)}) collective-permute-start(bf16[320,256]{1,0:T(8,128)(2,1)S(1)} %slice.16), channel_id=1, source_target_pairs={{0,4},{1,5},{2,0},{3,1},{4,8},{5,9},{6,2},{7,3},{8,12},{9,13},{10,... | collective-permute-start | bytes 491528 | tf_op jit(solution)/shard_map/ppermute | solution.py:475
  76.5 30.5 %collective-permute-start.11 = (bf16[320,256]{1,0:T(8,128)(2,1)S(1)}, bf16[320,256]{1,0:T(8,128)(2,1)S(1)}, u32[]{:S(2)}, u32[]{:S(2)}) collective-permute-start(bf16[320,256]{1,0:T(8,128)(2,1)S(1)} %slice.17), channel_id=1, source_target_pairs={{0,2},{1,3},{2,6},{3,7},{4,0},{5,1},{6,10},{7,11},{8,4},{9,5},{10,... | collective-permute-start | bytes 491528 | tf_op jit(solution)/shard_map/ppermute | solution.py:475
  104.9 30.0 %collective-permute-start.32 = (bf16[128,640]{1,0:T(8,128)(2,1)}, bf16[128,640]{1,0:T(8,128)(2,1)S(1)}, u32[]{:S(2)}, u32[]{:S(2)}) collective-permute-start(bf16[128,640]{1,0:T(8,128)(2,1)} %get-tuple-element.49), channel_id=1, source_target_pairs={{0,4},{1,5},{2,0},{3,1},{4,8},{5,9},{6,2},{7,3},{8,12},{9,13},{10,... | collective-permute-start | bytes 491528 | tf_op jit(solution)/shard_map/ppermute | solution.py:498
  106.5 28.4 %collective-permute-start.33 = (bf16[128,640]{1,0:T(8,128)(2,1)}, bf16[128,640]{1,0:T(8,128)(2,1)S(1)}, u32[]{:S(2)}, u32[]{:S(2)}) collective-permute-start(bf16[128,640]{1,0:T(8,128)(2,1)} %get-tuple-element.50), channel_id=1, source_target_pairs={{0,2},{1,3},{2,6},{3,7},{4,0},{5,1},{6,10},{7,11},{8,4},{9,5},{10,... | collective-permute-start | bytes 491528 | tf_op jit(solution)/shard_map/ppermute | solution.py:498
  148.3 11.9 %collective-permute-start.14 = (bf16[256,640]{1,0:T(8,128)(2,1)}, bf16[256,640]{1,0:T(8,128)(2,1)S(1)}, u32[]{:S(2)}, u32[]{:S(2)}) collective-permute-start(bf16[256,640]{1,0:T(8,128)(2,1)} %get-tuple-element.37), channel_id=1, source_target_pairs={{0,4},{1,5},{2,0},{3,1},{4,8},{5,9},{6,2},{7,3},{8,12},{9,13},{10,... | collective-permute-start | bytes 983048 | tf_op jit(solution)/shard_map/ppermute | solution.py:498
  158.1 12.9 %collective-permute-start.36 = (bf16[256,640]{1,0:T(8,128)(2,1)}, bf16[256,640]{1,0:T(8,128)(2,1)S(1)}, u32[]{:S(2)}, u32[]{:S(2)}) collective-permute-start(bf16[256,640]{1,0:T(8,128)(2,1)} %get-tuple-element.53), channel_id=1, source_target_pairs={{0,4},{1,5},{2,0},{3,1},{4,8},{5,9},{6,2},{7,3},{8,12},{9,13},{10,... | collective-permute-start | bytes 983048 | tf_op jit(solution)/shard_map/ppermute | solution.py:498
  166.1 12.9 %collective-permute-start.16 = (bf16[256,640]{1,0:T(8,128)(2,1)}, bf16[256,640]{1,0:T(8,128)(2,1)S(1)}, u32[]{:S(2)}, u32[]{:S(2)}) collective-permute-start(bf16[256,640]{1,0:T(8,128)(2,1)} %get-tuple-element.39), channel_id=1, source_target_pairs={{0,4},{1,5},{2,0},{3,1},{4,8},{5,9},{6,2},{7,3},{8,12},{9,13},{10,... | collective-permute-start | bytes 983048 | tf_op jit(solution)/shard_map/ppermute | solution.py:498
  167.7 11.4 %collective-permute-start.17 = (bf16[256,640]{1,0:T(8,128)(2,1)}, bf16[256,640]{1,0:T(8,128)(2,1)S(1)}, u32[]{:S(2)}, u32[]{:S(2)}) collective-permute-start(bf16[256,640]{1,0:T(8,128)(2,1)} %get-tuple-element.40), channel_id=1, source_target_pairs={{0,2},{1,3},{2,6},{3,7},{4,0},{5,1},{6,10},{7,11},{8,4},{9,5},{10,... | collective-permute-start | bytes 983048 | tf_op jit(solution)/shard_map/ppermute | solution.py:498
  171.0 16.0 %collective-permute-start.20 = (f32[320,512]{1,0:T(8,128)}, f32[320,512]{1,0:T(8,128)S(1)}, u32[]{:S(2)}, u32[]{:S(2)}) collective-permute-start(f32[320,512]{1,0:T(8,128)} %pick_outer.1), channel_id=1, source_target_pairs={{0,1},{1,0},{2,3},{3,2},{4,5},{5,4},{6,7},{7,6},{8,9},{9,8},{10,11... | collective-permute-start | bytes 1966088 | tf_op jit(solution)/shard_map/ppermute | solution.py:482
  177.0 14.5 %collective-permute-start.38 = (bf16[256,640]{1,0:T(8,128)(2,1)}, bf16[256,640]{1,0:T(8,128)(2,1)S(1)}, u32[]{:S(2)}, u32[]{:S(2)}) collective-permute-start(bf16[256,640]{1,0:T(8,128)(2,1)} %get-tuple-element.55), channel_id=1, source_target_pairs={{0,4},{1,5},{2,0},{3,1},{4,8},{5,9},{6,2},{7,3},{8,12},{9,13},{10,... | collective-permute-start | bytes 983048 | tf_op jit(solution)/shard_map/ppermute | solution.py:501
  178.6 12.9 %collective-permute-start.39 = (bf16[256,640]{1,0:T(8,128)(2,1)}, bf16[256,640]{1,0:T(8,128)(2,1)S(1)}, u32[]{:S(2)}, u32[]{:S(2)}) collective-permute-start(bf16[256,640]{1,0:T(8,128)(2,1)} %get-tuple-element.56), channel_id=1, source_target_pairs={{0,2},{1,3},{2,6},{3,7},{4,0},{5,1},{6,10},{7,11},{8,4},{9,5},{10,... | collective-permute-start | bytes 983048 | tf_op jit(solution)/shard_map/ppermute | solution.py:501
  185.0 13.2 %collective-permute-start.18 = (bf16[256,640]{1,0:T(8,128)(2,1)}, bf16[256,640]{1,0:T(8,128)(2,1)S(1)}, u32[]{:S(2)}, u32[]{:S(2)}) collective-permute-start(bf16[256,640]{1,0:T(8,128)(2,1)} %get-tuple-element.41), channel_id=1, source_target_pairs={{0,4},{1,5},{2,0},{3,1},{4,8},{5,9},{6,2},{7,3},{8,12},{9,13},{10,... | collective-permute-start | bytes 983048 | tf_op jit(solution)/shard_map/ppermute | solution.py:501
  186.6 11.6 %collective-permute-start.19 = (bf16[256,640]{1,0:T(8,128)(2,1)}, bf16[256,640]{1,0:T(8,128)(2,1)S(1)}, u32[]{:S(2)}, u32[]{:S(2)}) collective-permute-start(bf16[256,640]{1,0:T(8,128)(2,1)} %get-tuple-element.42), channel_id=1, source_target_pairs={{0,2},{1,3},{2,6},{3,7},{4,0},{5,1},{6,10},{7,11},{8,4},{9,5},{10,... | collective-permute-start | bytes 983048 | tf_op jit(solution)/shard_map/ppermute | solution.py:501
  196.7 21.4 %collective-permute-start.41 = (bf16[272,640]{1,0:T(8,128)(2,1)}, bf16[272,640]{1,0:T(8,128)(2,1)S(1)}, u32[]{:S(2)}, u32[]{:S(2)}) collective-permute-start(bf16[272,640]{1,0:T(8,128)(2,1)} %get-tuple-element.60), channel_id=1, source_target_pairs={{0,1},{1,0},{2,3},{3,2},{4,5},{5,4},{6,7},{7,6},{8,9},{9,8},{10,11... | collective-permute-start | bytes 1044488 | tf_op jit(solution)/shard_map/ppermute | solution.py:503
  203.4 14.7 %collective-permute-start.22 = (bf16[272,640]{1,0:T(8,128)(2,1)}, bf16[272,640]{1,0:T(8,128)(2,1)S(1)}, u32[]{:S(2)}, u32[]{:S(2)}) collective-permute-start(bf16[272,640]{1,0:T(8,128)(2,1)} %get-tuple-element.47), channel_id=1, source_target_pairs={{0,1},{1,0},{2,3},{3,2},{4,5},{5,4},{6,7},{7,6},{8,9},{9,8},{10,11... | collective-permute-start | bytes 1044488 | tf_op jit(solution)/shard_map/ppermute | solution.py:503
  205.6 12.5 %collective-permute-start.23 = (bf16[144,640]{1,0:T(8,128)(2,1)}, bf16[144,640]{1,0:T(8,128)(2,1)S(1)}, u32[]{:S(2)}, u32[]{:S(2)}) collective-permute-start(bf16[144,640]{1,0:T(8,128)(2,1)} %get-tuple-element.48), channel_id=1, source_target_pairs={{0,17},{1,16},{2,19},{3,18},{4,21},{5,20},{6,23},{7,22},{8,25},{9,... | collective-permute-start | bytes 552968 | tf_op jit(solution)/shard_map/ppermute | solution.py:454
  (64 other events, 614.3 us)

commit v2 on v1

v2 whole, which is shorter than its diff:
```python
import functools

import jax
import jax.numpy as jnp
import numpy as np
from jax import lax
from jax.experimental import pallas as pl
from jax.experimental.pallas import tpu as pltpu
from jax.sharding import PartitionSpec as P

HD = 128

inner_rate = 0.25
outer_rate = 0.7
momentum_decay = 0.9
blend_share = 0.5
norm_eps = 1e-06
scale_eps = 1e-06

F32 = jnp.float32
BF16 = jnp.bfloat16
VMEM_LIMIT = 62 * 1024 * 1024
SCALE_ROWS = 16


def ring_order(count):
    return list(range(0, count, 2)) + list(range(1, count, 2))[::-1]


def call(body, out_shape, in_specs, out_specs, grid=(1,), scratch=(), flops=0, moved=0, aliases=None, name=None):
    return pl.pallas_call(
        body,
        out_shape=out_shape,
        grid_spec=pltpu.PrefetchScalarGridSpec(
            num_scalar_prefetch=1,
            grid=grid,
            in_specs=in_specs,
            out_specs=out_specs,
            scratch_shapes=list(scratch),
        ),
        compiler_params=pltpu.CompilerParams(
            vmem_limit_bytes=VMEM_LIMIT, dimension_semantics=("arbitrary",) * len(grid)
        ),
        cost_estimate=pl.CostEstimate(flops=int(flops), bytes_accessed=int(moved), transcendentals=0),
        input_output_aliases=aliases or {},
        name=name,
    )


def whole(shape):
    zeros = (0,) * len(shape)
    return pl.BlockSpec(shape, lambda i, s: zeros)


def dot_nn(a, b):
    return lax.dot_general(a, b, (((1,), (0,)), ((), ())), preferred_element_type=F32)


def dot_nt(a, b):
    return lax.dot_general(a, b, (((1,), (1,)), ((), ())), preferred_element_type=F32)


def dot_tn(a, b):
    return lax.dot_general(a, b, (((0,), (0,)), ((), ())), preferred_element_type=F32)


def norm_rows(scalars, hidden_rows, norm_gain, chips):
    tokens, width = hidden_rows.shape
    part = width // chips
    tile = 128

    def body(s, x_ref, g_ref, o_ref):
        total = jnp.zeros((tile, 1), F32)
        for b in range(chips):
            x = x_ref[:, b * part : (b + 1) * part].astype(F32)
            total = total + jnp.sum(x * x, axis=-1, keepdims=True)
        factor = lax.rsqrt(total * (1.0 / width) + norm_eps)
        for b in range(chips):
            x = x_ref[:, b * part : (b + 1) * part].astype(F32)
            o_ref[b] = (x * factor * g_ref[:, b * part : (b + 1) * part]).astype(BF16)

    return call(
        body,
        jax.ShapeDtypeStruct((chips, tokens, part), BF16),
        [pl.BlockSpec((tile, width), lambda i, s: (i, 0)), whole((1, width))],
        pl.BlockSpec((chips, tile, part), lambda i, s: (0, i, 0)),
        grid=(tokens // tile,),
        flops=tokens * width * 6,
        moved=tokens * width * 4,
        name="norm",
    )(scalars, hidden_rows, norm_gain.reshape(1, width))


def columns_of(core, head, kv, heads, kv_width):
    return pl.multiple_of(kv * kv_width + (core * heads + head) * HD, HD)


def own_blocks(scalars, weight, received, heads):
    rows, cols = weight.shape

    def body(s, w_ref, r_ref, *o_refs):
        core = s[0]
        mine = pl.multiple_of(core * rows, 16)
        theirs = pl.multiple_of((1 - core) * rows, 16)
        for h in range(heads):
            for kv in range(2):
                there = pl.ds(columns_of(core, h, kv, heads, cols // 2), HD)
                lanes = slice(kv * HD, (kv + 1) * HD)
                o_refs[h][pl.ds(mine, rows), lanes] = w_ref[:, there]
                o_refs[h][pl.ds(theirs, rows), lanes] = r_ref[:, there]

    shape = (2 * rows, 2 * HD)
    return call(
        body,
        [jax.ShapeDtypeStruct(shape, weight.dtype)] * heads,
        [whole((rows, cols))] * 2,
        [whole(shape)] * heads,
        moved=rows * cols * 6,
        name="own_blocks",
    )(scalars, weight, received)


def start_deltas(scalars, blocks, outer, received, heads):
    rows, cols = outer.shape

    def body(s, o_ref, r_ref, *refs):
        core = s[0]
        for h in range(heads):
            block_ref, out_ref = refs[h], refs[heads + h]
            for kv in range(2):
                there = pl.ds(columns_of(core, h, kv, heads, cols // 2), HD)
                mine = o_ref[:, there]
                theirs = r_ref[:, there]
                first = jnp.where(core == 0, mine, theirs)
                second = jnp.where(core == 0, theirs, mine)
                both = jnp.concatenate([first, second], axis=0)
                both = both - block_ref[:, kv * HD : (kv + 1) * HD].astype(F32)
                out_ref[kv * HD : (kv + 1) * HD, :] = both.T

    return call(
        body,
        [jax.ShapeDtypeStruct((2 * HD, 2 * rows), F32)] * heads,
        [whole((rows, cols))] * 2 + [whole((2 * rows, 2 * HD))] * heads,
        [whole((2 * HD, 2 * rows))] * heads,
        moved=rows * cols * 14,
        name="start_deltas",
    )(scalars, outer, received, *blocks)


def project_part(scalars, rows_mine, rows_other, blocks, base, acc, name):
    chips, tokens, part = rows_mine.shape
    count = len(blocks)

    def body(s, a_ref, b_ref, *refs):
        block_refs = refs[:count]
        acc_ref = refs[count] if acc is not None else None
        out_ref, held, sems = refs[-3:]
        copies = []
        for k in range(count):
            for side, ref in enumerate((a_ref, b_ref)):
                copies.append(pltpu.make_async_copy(ref.at[s[1 + base + k]], held.at[k, side], sems.at[k, side]))
        for copy in copies:
            copy.start()
        for k in range(count):
            for side in range(2):
                copies[2 * k + side].wait()
                here = slice(side * tokens, (side + 1) * tokens)
                product = dot_nn(held[k, side], block_refs[k][...])
                if k > 0:
                    product = product + out_ref[here, :]
                elif acc is not None:
                    product = product + acc_ref[here, :]
                out_ref[here, :] = product

    shape = (2 * tokens, 2 * HD)
    any_spec = pl.BlockSpec(memory_space=pl.ANY)
    inputs = [rows_mine, rows_other, *blocks] + ([acc] if acc is not None else [])
    return call(
        body,
        jax.ShapeDtypeStruct(shape, F32),
        [any_spec, any_spec] + [whole(b.shape) for b in blocks] + ([whole(shape)] if acc is not None else []),
        whole(shape),
        scratch=[pltpu.VMEM((count, 2, tokens, part), BF16), pltpu.SemaphoreType.DMA((count, 2))],
        flops=2 * 2 * tokens * part * 2 * HD * count,
        moved=2 * tokens * part * 2 * count,
        name=name,
    )(scalars, *inputs)


def attention_grads(scalars, acc, rows_mine, rows_other, blocks, halves, base, queries, queries_other, out_grad, out_grad_other, head, heads):
    chips, tokens, part = rows_mine.shape
    seqs, length, query_width = queries.shape
    repeat = query_width // (2 * heads * HD)
    inv_root = (chips * part) ** (-0.5)
    half = length // 2
    count = len(blocks)
    last = chips - 1
    two_power = HD ** (-0.5) * 1.4426950408889634

    def body(s, acc_ref, qa_ref, qb_ref, ga_ref, gb_ref, fa_ref, fb_ref, *refs):
        row_refs = (refs[: count + 1], refs[count + 1 : 2 * count + 2])
        refs = refs[2 * count + 2 :]
        block_refs, half_refs = refs[:count], refs[count : count + 2]
        out_ref, up_ref, down_ref, far_ref, grad_ref = refs[count + 2 :]
        step = pl.program_id(0)

        @pl.when(step == 0)
        def _():
            far_ref[: part // 2, :] = half_refs[0][...]
            far_ref[part // 2 :, :] = half_refs[1][...]

        def work(x_refs, q_ref, g_ref):
            total = acc_ref[...]
            for ref, block_ref in zip(x_refs, list(block_refs) + [far_ref]):
                total = total + dot_nn(ref[0], block_ref[...])
            kv = (total * inv_root).astype(BF16)
            keys, values = kv[:, :HD], kv[:, HD:]
            found = []
            for t in range(2):
                cols = (t + 1) * half
                rows_of = slice(t * half, (t + 1) * half)
                q = jnp.concatenate([q_ref[0, rows_of, r * HD : (r + 1) * HD] for r in range(repeat)], axis=0)
                g = jnp.concatenate([g_ref[0, rows_of, r * HD : (r + 1) * HD] for r in range(repeat)], axis=0)
                scores = dot_nt(q, keys[:cols]) * two_power
                spot = lax.broadcasted_iota(jnp.int32, (half, cols), 0) + t * half
                causal = lax.broadcasted_iota(jnp.int32, (half, cols), 1) <= spot
                causal = jnp.concatenate([causal.astype(F32)] * repeat, axis=0) > 0.0
                scores = jnp.where(causal, scores, -1e30)
                highest = jnp.max(scores, axis=-1, keepdims=True)
                exps = jnp.exp2(scores - highest)
                prob = exps * (1.0 / jnp.sum(exps, axis=-1, keepdims=True))
                prob_grad = dot_nt(g, values[:cols]).astype(BF16).astype(F32)
                weighted = prob * prob_grad
                mean = jnp.sum(weighted, axis=-1, keepdims=True)
                score_grad = (weighted - prob * mean).astype(BF16)
                found.append((dot_tn(q, score_grad), dot_tn(g, prob.astype(BF16))))
            for at, factor in ((0, HD ** (-0.5)), (1, 1.0)):
                grad_rows = slice(at * HD, (at + 1) * HD)
                early, late = found[0][at], found[1][at]
                grad = jnp.concatenate([(late[:, :half] + early) * factor, late[:, half:] * factor], axis=1).astype(BF16)
                out_ref[grad_rows, :] = grad
                grad_ref[step, grad_rows, :] = grad

        @pl.when(step < seqs)
        def _():
            work(row_refs[0], qa_ref, ga_ref)

        @pl.when(step >= seqs)
        def _():
            work(row_refs[1], qb_ref, gb_ref)

        @pl.when(step == 2 * seqs - 1)
        def _():
            total = jnp.zeros((2 * HD, part), F32)
            for at in range(seqs):
                here = slice(at * length, (at + 1) * length)
                total = total + dot_nn(grad_ref[at], fa_ref[0, here, :]) + dot_nn(grad_ref[seqs + at], fb_ref[0, here, :])
            total = total * inv_root
            up_ref[...] = total[:HD].astype(BF16)
            down_ref[...] = total[HD:].astype(BF16)

    first = lambda i: jnp.minimum(i, seqs - 1)
    second = lambda i: jnp.maximum(i - seqs, 0)

    def rows_spec(pick, place):
        return pl.BlockSpec((1, length, part), lambda i, s: (s[1 + place], pick(i), 0))

    mine_spec = pl.BlockSpec((1, length, repeat * HD), lambda i, s: (first(i), 0, s[0] * heads + head))
    other_spec = pl.BlockSpec((1, length, repeat * HD), lambda i, s: (second(i), 0, head))
    far_spec = pl.BlockSpec((1, tokens, part), lambda i, s: (s[1 + last], 0, 0))
    places = [base + k for k in range(count)] + [last]
    half_shape = (HD, part)
    work_flops = 2 * tokens * part * 2 * HD * 2 * len(places) + 2 * seqs * repeat * length * length * HD * 8 * 4
    return call(
        body,
        [jax.ShapeDtypeStruct((2 * HD, 2 * tokens), BF16)] + [jax.ShapeDtypeStruct(half_shape, BF16)] * 2,
        [pl.BlockSpec((length, 2 * HD), lambda i, s: (i, 0)), mine_spec, other_spec, mine_spec, other_spec, far_spec, far_spec]
        + [rows_spec(first, p) for p in places]
        + [rows_spec(second, p) for p in places]
        + [whole(b.shape) for b in blocks]
        + [whole(h.shape) for h in halves],
        [pl.BlockSpec((2 * HD, length), lambda i, s: (0, i)), whole(half_shape), whole(half_shape)],
        grid=(2 * seqs,),
        scratch=[pltpu.VMEM((part, 2 * HD), BF16), pltpu.VMEM((2 * seqs, 2 * HD, length), BF16)],
        flops=work_flops,
        moved=2 * tokens * part * 2 * len(places),
        name=f"attend_{head}",
    )(
        scalars, acc, queries, queries_other, out_grad, out_grad_other, rows_mine, rows_other,
        *[rows_mine] * len(places), *[rows_other] * len(places), *blocks, *halves,
    )


def partials(scalars, kv_grad, rows_mine, rows_other, name):
    chips, tokens, part = rows_mine.shape
    inv_root = (chips * part) ** (-0.5)
    count = chips - 1

    def body(s, k_ref, a_ref, b_ref, out_ref, held, done, in_sems, out_sems):
        copies = {}
        for k in reversed(range(count)):
            for side, ref in enumerate((a_ref, b_ref)):
                copies[k, side] = pltpu.make_async_copy(ref.at[s[1 + k]], held.at[k, side], in_sems.at[k, side])
                copies[k, side].start()
        leaving = []
        for k in reversed(range(count)):
            copies[k, 0].wait()
            copies[k, 1].wait()
            total = dot_nn(k_ref[:, :tokens], held[k, 0]) + dot_nn(k_ref[:, tokens:], held[k, 1])
            done[k] = (total * inv_root).astype(BF16)
            leaving.append(pltpu.make_async_copy(done.at[k], out_ref.at[k], out_sems.at[k]))
            leaving[-1].start()
        for copy in leaving:
            copy.wait()

    any_spec = pl.BlockSpec(memory_space=pl.ANY)
    shape = (count, 2 * HD, part)
    return call(
        body,
        jax.ShapeDtypeStruct(shape, BF16),
        [whole(kv_grad.shape), any_spec, any_spec],
        any_spec,
        scratch=[
            pltpu.VMEM((count, 2, tokens, part), BF16),
            pltpu.VMEM(shape, BF16),
            pltpu.SemaphoreType.DMA((count, 2)),
            pltpu.SemaphoreType.DMA((count,)),
        ],
        flops=2 * 2 * tokens * part * 2 * HD * count,
        moved=2 * tokens * part * 2 * count,
        name=name,
    )(scalars, kv_grad, rows_mine, rows_other)


def add_partials(scalars, own, up, down, distance, name):
    part = own.shape[-1]
    is_half = up.shape[0] == HD
    at = 2 * distance - 1

    def body(s, ou_ref, od_ref, ui_ref, di_ref, up_ref, down_ref):
        mine_up, mine_down = ou_ref[0].astype(F32), od_ref[0].astype(F32)
        if is_half:
            keys = pl.program_id(0) == 0
            up_ref[...] = jnp.where(keys, mine_up + ui_ref[...].astype(F32), mine_up).astype(BF16)
            down_ref[...] = jnp.where(keys, mine_down, mine_down + di_ref[...].astype(F32)).astype(BF16)
        else:
            up_ref[...] = (mine_up + ui_ref[...].astype(F32)).astype(BF16)
            down_ref[...] = (mine_down + di_ref[...].astype(F32)).astype(BF16)

    block = (HD, part)
    came = whole(block) if is_half else pl.BlockSpec(block, lambda i, s: (i, 0))
    shape = jax.ShapeDtypeStruct((2 * HD, part), BF16)
    return call(
        body,
        [shape] * 2,
        [
            pl.BlockSpec((1, HD, part), lambda i, s: (at, i, 0)),
            pl.BlockSpec((1, HD, part), lambda i, s: (at + 1, i, 0)),
            came,
            came,
        ],
        [pl.BlockSpec(block, lambda i, s: (i, 0))] * 2,
        grid=(2,),
        moved=2 * HD * part * 12,
        name=name,
    )(scalars, own, own, up, down)


def split_packs(values):
    deep = values.shape[0] // 2
    rows = values.shape[1] // 2
    return [
        jnp.concatenate([values[:deep, k * rows : (k + 1) * rows], values[deep:, k * rows : (k + 1) * rows]], axis=1)
        for k in range(2)
    ]


def code_deltas(scalars, own, up, down, delta_start, name):
    part = own.shape[-1]

    def body(s, g_ref, ui_ref, di_ref, d_ref, own_ref, core_ref, y_ref, far_ref):
        core = s[0]
        total = g_ref[0].astype(F32) + ui_ref[...].astype(F32) + di_ref[...].astype(F32)
        delta = d_ref[...] + inner_rate * total
        scales, coded = [], []
        for kv in range(2):
            piece = delta[kv * HD : (kv + 1) * HD]
            scale = (jnp.max(jnp.abs(piece), axis=0, keepdims=True) + scale_eps).astype(BF16).astype(F32)
            scales.append(scale)
            coded.append(piece / scale)
        grads = split_packs(total)
        codes = split_packs(jnp.concatenate(coded, axis=0))
        levels = split_packs(jnp.concatenate(scales, axis=0))
        for mine, wide_ref, thin_ref in ((True, own_ref, y_ref), (False, core_ref, far_ref)):
            first = (core == 0) if mine else (core == 1)
            grad = jnp.where(first, grads[0], grads[1]).astype(BF16)
            code = jnp.where(first, codes[0], codes[1]).astype(BF16)
            level = jnp.where(first, levels[0], levels[1])
            level = jnp.broadcast_to(level, (SCALE_ROWS, part)).astype(BF16)
            wide_ref[:HD, :] = code
            wide_ref[HD : HD + SCALE_ROWS, :] = level
            wide_ref[HD + SCALE_ROWS :, :] = grad
            thin_ref[:HD, :] = code
            thin_ref[HD:, :] = level

    wide, thin = (2 * HD + SCALE_ROWS, part), (HD + SCALE_ROWS, part)
    return call(
        body,
        [jax.ShapeDtypeStruct(shape, BF16) for shape in (wide, wide, thin, thin)],
        [
            pl.BlockSpec((1, 2 * HD, part), lambda i, s: (0, 0, 0)),
            whole(up.shape),
            whole(down.shape),
            whole(delta_start.shape),
        ],
        [whole(wide), whole(wide), whole(thin), whole(thin)],
        moved=2 * HD * part * 16,
        name=name,
    )(scalars, own, up, down, delta_start)


def finish(scalars, weight, outer, momentum, grads, codes, before, head, heads):
    rows, cols = weight.shape
    groups = len(codes[0])
    packs = [*codes[0], grads[0], *codes[1], grads[1]]
    kept = [] if before is None else list(before)

    def body(s, w_ref, k_ref, m_ref, *refs):
        pack_refs = refs[: len(packs)]
        blend_ref, outer_ref, moment_ref = refs[len(packs) + len(kept) :]
        step = pl.program_id(0)
        for side in range(2):
            code_refs = pack_refs[side * (groups + 1) : side * (groups + 1) + groups]
            grad_ref = pack_refs[side * (groups + 1) + groups]
            for kv in range(2):

                @pl.when(step == 2 * side + kv)
                def _():
                    lanes = slice(kv * rows, (kv + 1) * rows)
                    grad = grad_ref[HD + SCALE_ROWS :, lanes].astype(F32).T
                    total = jnp.zeros((HD, rows), F32)
                    for ref in code_refs:
                        total = total + ref[:HD, lanes].astype(F32) * ref[HD : HD + 1, lanes].astype(F32)
                    average = (total / groups).T
                    fresh = w_ref[...].astype(F32) - inner_rate * grad
                    moment = momentum_decay * m_ref[...] + average
                    stepped = k_ref[...] - outer_rate * (momentum_decay * moment + average)
                    moment_ref[...] = moment
                    outer_ref[...] = stepped
                    blend_ref[...] = (blend_share * fresh + (1.0 - blend_share) * stepped).astype(BF16)

    block = pl.BlockSpec(
        (rows, HD), lambda i, s: (0, i % 2 * 2 * heads + jnp.where(i < 2, s[0], 1 - s[0]) * heads + head)
    )
    any_spec = pl.BlockSpec(memory_space=pl.ANY)
    return call(
        body,
        [
            jax.ShapeDtypeStruct((rows, cols), BF16),
            jax.ShapeDtypeStruct((rows, cols), F32),
            jax.ShapeDtypeStruct((rows, cols), F32),
        ],
        [block] * 3 + [whole(p.shape) for p in packs] + [any_spec] * len(kept),
        [block] * 3,
        grid=(4,),
        moved=rows * cols * 12,
        aliases={4 + len(packs) + k: k for k in range(len(kept))},
        name=f"finish_{head}",
    )(scalars, weight, outer, momentum, *packs, *kept)


def local(hidden, norm_gain, queries, out_grad, kv_inner, kv_outer, momentum):
    count = lax.axis_size("fsdp")
    groups = lax.axis_size("group")
    index = lax.axis_index("fsdp")
    group = lax.axis_index("group")
    chips = count // 2
    far = chips // 2
    ring = ring_order(chips)
    place = {chip: at for at, chip in enumerate(ring)}
    order = [0] + [k % chips for step in range(1, far) for k in (step, -step)] + [far]
    walks = np.array([[ring[(place[j] + k) % chips] for k in order] for j in range(chips)], np.int32)
    core = index % 2
    scalars = jnp.concatenate([core[None].astype(jnp.int32), jnp.asarray(walks)[index // 2]])

    def around(shift):
        return [(2 * j + c, 2 * ring[(place[j] + shift) % chips] + c) for j in range(chips) for c in range(2)]

    up = functools.partial(lax.ppermute, axis_name="fsdp", perm=around(1))
    down = functools.partial(lax.ppermute, axis_name="fsdp", perm=around(-1))
    swap = functools.partial(lax.ppermute, axis_name="fsdp", perm=[(i, i ^ 1) for i in range(count)])

    def across(values, shift, flip):
        pairs = [
            (g * count + i, (g + shift) % groups * count + (i ^ flip)) for g in range(groups) for i in range(count)
        ]
        return lax.ppermute(values, ("group", "fsdp"), pairs)

    weight = kv_inner[0]
    rows, cols = weight.shape
    heads = cols // 2 // HD // 2
    seqs, length, width = hidden.shape[1:]
    half_width = queries.shape[-1] // 2
    part = 2 * rows

    own = own_blocks(scalars, weight, swap(weight), heads)
    hidden, queries, out_grad, outer_held, own = lax.optimization_barrier((hidden, queries, out_grad, kv_outer, own))

    blocks = [[own[h]] for h in range(heads)]
    halves = [None] * heads
    ups, downs = list(own), list(own)
    for step in range(1, far + 1):
        for h in range(heads):
            if step < far:
                ups[h], downs[h] = up(ups[h]), down(downs[h])
                blocks[h] += [downs[h], ups[h]]
            else:
                halves[h] = (up(ups[h][: part // 2]), down(downs[h][part // 2 :]))

    rows_mine = norm_rows(scalars, hidden.reshape(seqs * length, width), norm_gain, chips)
    rows_other = swap(rows_mine)
    at = ((1 - core) * half_width).astype(jnp.int32)
    queries_other = swap(lax.dynamic_slice_in_dim(queries[0], at, half_width, axis=2))
    out_grad_other = swap(lax.dynamic_slice_in_dim(out_grad[0], at, half_width, axis=2))
    deltas = start_deltas(scalars, own, outer_held, swap(outer_held), heads)

    kv_grad, far_up, far_down = [None] * heads, [None] * heads, [None] * heads
    accs = [None] * heads
    bounds = [0, 3] + [2 * step + 1 for step in range(2, far - 1)]
    for base, end in zip(bounds, bounds[1:]):
        for h in range(heads):
            accs[h] = project_part(scalars, rows_mine, rows_other, blocks[h][base:end], base, accs[h], f"project_{h}_{base}")
    accs, deltas = lax.optimization_barrier((accs, deltas))
    for h in range(heads):
        kv_grad[h], far_up[h], far_down[h] = attention_grads(
            scalars, accs[h], rows_mine, rows_other, blocks[h][bounds[-1] :], halves[h], bounds[-1],
            queries[0], queries_other, out_grad[0], out_grad_other, h, heads,
        )

    outs = None
    for h in range(heads):
        sums = partials(scalars, kv_grad[h], rows_mine, rows_other, f"partials_{h}")
        going_up, going_down = far_up[h], far_down[h]
        for distance in range(far - 1, 0, -1):
            going_up, going_down = add_partials(
                scalars, sums, up(going_up), down(going_down), distance, f"add_{h}_{distance}"
            )
        own_pack, core_pack, thin_own, thin_core = code_deltas(
            scalars, sums, up(going_up), down(going_down), deltas[h], f"code_{h}"
        )
        from_core = swap(core_pack)
        mine = [own_pack] + [across(thin_own, k, 0) for k in range(1, groups)]
        theirs = [from_core] + [across(thin_core, k, 1) for k in range(1, groups)]
        if groups > 2:
            deep = HD + SCALE_ROWS
            ordered = []
            for packs in (mine, theirs):
                stacked = jnp.stack([p[:deep] for p in packs])
                ordered.append([stacked[(group - g) % groups] for g in range(groups)])
            mine, theirs = ordered
        outs = finish(
            scalars, weight, kv_outer, momentum, (own_pack, from_core), (mine, theirs), outs, h, heads
        )

    blended, outer_new, momentum_new = outs
    return (blended[None], outer_new, momentum_new)


def solution(mesh):
    in_specs = (
        P("group", "fsdp", None, None),
        P(),
        P("group", "fsdp", None, None),
        P("group", "fsdp", None, None),
        P("group", "fsdp", None),
        P("fsdp", None),
        P("fsdp", None),
    )
    out_specs = (P("group", "fsdp", None), P("fsdp", None), P("fsdp", None))
    return jax.shard_map(local, mesh=mesh, in_specs=in_specs, out_specs=out_specs, check_vma=False)
```

time: 226 us -> 241 us (1.066)
  Pallas kernels: 111 us -> 120 us
  local copies, waits for them, and re-layouts: 15.1 us -> 20.6 us
    ppermute x12, waiting for transfers between devices: 36.5 us -> 45.8 us  [local(): ups[h], downs[h] = (up(ups[h]), down(downs[h]))]
    ppermute x4, waiting for transfers between devices: 12.5 us -> 5.49 us  [across(): return lax.ppermute(values, ('group', 'fsdp'), pairs)]
    pallas_call x12 -> x14, Pallas kernels: 81.3 us -> 88 us  [the longest x2 28.9 us: attention_grads(): call(body, [jax.ShapeDtypeStruct((2 * HD, 2 * tokens), BF16)] + [jax.Shap...]
    ppermute x2, waiting for transfers between devices: 6.35 us -> 0.65 us  [the longest x1 0.65 us: local(): own = own_blocks(scalars, weight, swap(weight), heads)]
    pallas_call x1 -> x2, Pallas kernels: 6.78 us -> 10.9 us  [finish(): call(body, [jax.ShapeDtypeStruct((rows, cols), BF16), jax.ShapeDtypeStruc...]
    ppermute x8, waiting for transfers between devices: 2.09 us -> 5.17 us  [local(): down(going_down)]
    slice x4, local copies, waits for them, and re-layouts: 0.05 us -> 2.76 us  [local(): halves[h] = (up(ups[h][:part // 2]), down(downs[h][part // 2:]))]
    ppermute x4, waiting for transfers between devices: 2.54 us -> 0.01 us  [local(): halves[h] = (up(ups[h][:part // 2]), down(downs[h][part // 2:]))]
  transfers between devices with their start and end apart: 43 -> 43, of which waited for: 16 -> 19; matrix products, arithmetic and copies ran while one was open for 0% -> 3% of each run, Pallas kernels for 43% -> 43%
where the time goes in v2:
time: 241 us; the launch traced here: 240 us
  Pallas kernels  120 us (50%)
  waiting for transfers between devices  59.4 us (25%)
  starting transfers between devices  38.2 us (16%)
  local copies, waits for them, and re-layouts  20.6 us (9%)
    ppermute x12, waiting for transfers between devices, local(): ups[h], downs[h] = (up(ups[h]), down(downs[h]))  45.8 us
    pallas_call x2, Pallas kernels, attention_grads(): call(body, [jax.ShapeDtypeStruct((2 * HD, 2 * tokens), BF16)] + [jax.Shap...  28.9 us
    pallas_call x4, Pallas kernels, project_part(): call(body, jax.ShapeDtypeStruct(shape, F32), [any_spec, any_spec] + [whol...  26.2 us
    pallas_call x6, Pallas kernels, add_partials(): call(body, [shape] * 2, [pl.BlockSpec((1, HD, part), lambda i, s: (at, i,...  16.9 us
    pallas_call x2, Pallas kernels, partials(): call(body, jax.ShapeDtypeStruct(shape, BF16), [whole(kv_grad.shape), any_...  15.9 us
    unnamed x88, local copies, waits for them, and re-layouts  13.5 us
    ppermute x12, starting transfers between devices, local(): ups[h], downs[h] = (up(ups[h]), down(downs[h]))  12.6 us
    pallas_call x2, Pallas kernels, finish(): call(body, [jax.ShapeDtypeStruct((rows, cols), BF16), jax.ShapeDtypeStruc...  10.9 us
  transfers between devices with their start and end apart: 43, of which 19 were waited for; matrix products, arithmetic and copies ran while one was open for 3% of the time, Pallas kernels for 43%

profile of v2, /device:TPU:0, one launch (start us, length us, event | category | flops | bytes accessed | tf_op | source)
XLA Modules:
  0.0 239.7 jit_solution(13910651744144626024)
XLA Ops:
  3.9 3.0 %own_blocks.1 = (bf16[640,256]{1,0:T(8,128)(2,1)}, bf16[640,256]{1,0:T(8,128)(2,1)}) custom-call(s32[9]{0:T(128)} %pad_add_fusion.s, bf16[320,1024]{1,0:T(8,128)(2,1)} %bitcast.18, bf16[320,1024]{1,0:T(8,128)(2,1)} %copy-done.11), custom_call_target="tpu_custom_call" | custom-call | bytes 1966080 | tf_op jit(solution)/shard_map/own_blocks/pallas_call | solution.py:113
  6.9 7.4 %norm.1.a_ref.fa_ref.refs_0_.refs_1_.refs_2_ = bf16[8,512,640]{2,1,0:T(8,128)(2,1)} custom-call(s32[9]{0:T(128)} %pad_add_fusion.s, bf16[512,5120]{1,0:T(8,128)(2,1)} %bitcast.21, f32[1,5120]{1,0:T(1,128)} %bitcast.23), custom_call_target="tpu_custom_call" | custom-call | flops 15728640 | bytes 10485760 | tf_op jit(solution)/shard_map/norm/pallas_call | solution.py:82
  19.5 6.5 %collective-permute-done.6.refs_1_ = bf16[640,256]{1,0:T(8,128)(2,1)S(1)} collective-permute-done((bf16[640,256]{1,0:T(8,128)(2,1)S(1)}, bf16[640,256]{1,0:T(8,128)(2,1)S(1)}, u32[]{:S(2)}, u32[]{:S(2)}) %collective-permute-start.6) | collective-permute-done | bytes 327712 | tf_op jit(solution)/shard_map/ppermute | solution.py:515
  28.0 6.9 %collective-permute-done.8.refs_2_ = bf16[640,256]{1,0:T(8,128)(2,1)S(1)} collective-permute-done((bf16[640,256]{1,0:T(8,128)(2,1)S(1)}, bf16[640,256]{1,0:T(8,128)(2,1)S(1)}, u32[]{:S(2)}, u32[]{:S(2)}) %collective-permute-start.8) | collective-permute-done | bytes 327712 | tf_op jit(solution)/shard_map/ppermute | solution.py:515
  35.1 4.7 %collective-permute-done.7.refs_0_ = bf16[640,256]{1,0:T(8,128)(2,1)} collective-permute-done((bf16[640,256]{1,0:T(8,128)(2,1)S(1)}, bf16[640,256]{1,0:T(8,128)(2,1)}, u32[]{:S(2)}, u32[]{:S(2)}) %collective-permute-start.7) | collective-permute-done | bytes 327712 | tf_op jit(solution)/shard_map/ppermute | solution.py:515
  45.8 3.2 %collective-permute-done.9.refs_1_ = bf16[640,256]{1,0:T(8,128)(2,1)S(1)} collective-permute-done((bf16[640,256]{1,0:T(8,128)(2,1)S(1)}, bf16[640,256]{1,0:T(8,128)(2,1)S(1)}, u32[]{:S(2)}, u32[]{:S(2)}) %collective-permute-start.9) | collective-permute-done | bytes 327712 | tf_op jit(solution)/shard_map/ppermute | solution.py:515
  49.5 5.6 %collective-permute-done.29.refs_7_ = bf16[640,256]{1,0:T(8,128)(2,1)S(1)} collective-permute-done((bf16[640,256]{1,0:T(8,128)(2,1)}, bf16[640,256]{1,0:T(8,128)(2,1)S(1)}, u32[]{:S(2)}, u32[]{:S(2)}) %collective-permute-start.29) | collective-permute-done | bytes 327712 | tf_op jit(solution)/shard_map/ppermute | solution.py:515
  56.7 7.3 %collective-permute-done.28.refs_6_ = bf16[640,256]{1,0:T(8,128)(2,1)S(1)} collective-permute-done((bf16[640,256]{1,0:T(8,128)(2,1)S(1)}, bf16[640,256]{1,0:T(8,128)(2,1)S(1)}, u32[]{:S(2)}, u32[]{:S(2)}) %collective-permute-start.28) | collective-permute-done | bytes 327712 | tf_op jit(solution)/shard_map/ppermute | solution.py:515
  64.7 7.2 %collective-permute-done.14.refs_7_ = bf16[640,256]{1,0:T(8,128)(2,1)S(1)} collective-permute-done((bf16[640,256]{1,0:T(8,128)(2,1)S(1)}, bf16[640,256]{1,0:T(8,128)(2,1)S(1)}, u32[]{:S(2)}, u32[]{:S(2)}) %collective-permute-start.14) | collective-permute-done | bytes 327712 | tf_op jit(solution)/shard_map/ppermute | solution.py:515
  75.5 3.7 %collective-permute-done.13.refs_6_ = bf16[640,256]{1,0:T(8,128)(2,1)S(1)} collective-permute-done((bf16[640,256]{1,0:T(8,128)(2,1)}, bf16[640,256]{1,0:T(8,128)(2,1)S(1)}, u32[]{:S(2)}, u32[]{:S(2)}) %collective-permute-start.13) | collective-permute-done | bytes 327712 | tf_op jit(solution)/shard_map/ppermute | solution.py:515
  83.0 3.9 %start_deltas.1 = (f32[256,640]{1,0:T(8,128)}, f32[256,640]{1,0:T(8,128)}) custom-call(s32[9]{0:T(128)} %pad_add_fusion.s, f32[320,1024]{1,0:T(8,128)} %k_ref.3, f32[320,1024]{1,0:T(8,128)} %copy-done.6, bf16[640,256]{1,0:T(8,128)(2,1)} %get-tuple-element.52.refs_0_, bf16[640,256]{1,0:T(8,128)(2,1)} %get-tuple-element.53.refs_0_.refs_1_), custom_call_target="tpu_custom_call" | custom-call | bytes 4587520 | tf_op jit(solution)/shard_map/start_deltas/pallas_call | solution.py:140
  88.3 6.8 %project_1_0.1.refs_2_ = f32[1024,256]{1,0:T(8,128)} custom-call(s32[9]{0:T(128)} %pad_add_fusion.s, bf16[8,512,640]{2,1,0:T(8,128)(2,1)} %norm.1.a_ref.fa_ref.refs_0_.refs_1_.refs_2_, bf16[8,512,640]{2,1,0:T(8,128)(2,1)} %collective-permute-done.1.b_ref.fb_ref.refs_3_.refs_4_.refs_5_, bf16[640,256]{1,0:T(8,128)(2,1)} %get-tuple-element.53.refs_0_.refs_1_, ...), custom_call_target="tpu_custom_call" | custom-call | flops 1006632960 | bytes 3932160 | tf_op jit(solution)/shard_map/project_1_0/pallas_call | solution.py:178
  95.1 6.3 %project_1_3.1.acc_ref = f32[1024,256]{1,0:T(8,128)} custom-call(s32[9]{0:T(128)} %pad_add_fusion.s, bf16[8,512,640]{2,1,0:T(8,128)(2,1)} %norm.1.a_ref.fa_ref.refs_0_.refs_1_.refs_2_, bf16[8,512,640]{2,1,0:T(8,128)(2,1)} %collective-permute-done.1.b_ref.fb_ref.refs_3_.refs_4_.refs_5_, bf16[640,256]{1,0:T(8,128)(2,1)} %collective-permute-done.7.refs_0_, ...), custom_call_target="tpu_custom_call" | custom-call | flops 671088640 | bytes 2621440 | tf_op jit(solution)/shard_map/project_1_3/pallas_call | solution.py:178
  101.4 6.8 %project_0_0.1.refs_2_ = f32[1024,256]{1,0:T(8,128)} custom-call(s32[9]{0:T(128)} %pad_add_fusion.s, bf16[8,512,640]{2,1,0:T(8,128)(2,1)} %norm.1.a_ref.fa_ref.refs_0_.refs_1_.refs_2_, bf16[8,512,640]{2,1,0:T(8,128)(2,1)} %collective-permute-done.1.b_ref.fb_ref.refs_3_.refs_4_.refs_5_, bf16[640,256]{1,0:T(8,128)(2,1)} %get-tuple-element.52.refs_0_, ...), custom_call_target="tpu_custom_call" | custom-call | flops 1006632960 | bytes 3932160 | tf_op jit(solution)/shard_map/project_0_0/pallas_call | solution.py:178
  108.2 6.4 %project_0_3.1.acc_ref = f32[1024,256]{1,0:T(8,128)} custom-call(s32[9]{0:T(128)} %pad_add_fusion.s, bf16[8,512,640]{2,1,0:T(8,128)(2,1)} %norm.1.a_ref.fa_ref.refs_0_.refs_1_.refs_2_, bf16[8,512,640]{2,1,0:T(8,128)(2,1)} %collective-permute-done.1.b_ref.fb_ref.refs_3_.refs_4_.refs_5_, bf16[640,256]{1,0:T(8,128)(2,1)} %copy-done.16, ...), custom_call_target="tpu_custom_call" | custom-call | flops 671088640 | bytes 2621440 | tf_op jit(solution)/shard_map/project_0_3/pallas_call | solution.py:178
  116.0 14.4 %attend_0.1 = (bf16[256,1024]{1,0:T(8,128)(2,1)}, bf16[128,640]{1,0:T(8,128)(2,1)}, bf16[128,640]{1,0:T(8,128)(2,1)}) custom-call(s32[9]{0:T(128)} %pad_add_fusion.s, f32[1024,256]{1,0:T(8,128)} %project_0_3.1.acc_ref, bf16[2,256,2560]{2,1,0:T(8,128)(2,1)} %bitcast.13, bf16[2,256,1280]{2,1,0:T(8,128)(2,1)} %collective-permute-done.11.qb_ref, ...), custom_call_target="tpu_custom_call" | custom-call | flops 6375342080 | bytes 3932160 | tf_op jit(solution)/shard_map/attend_0/pallas_call | solution.py:274
  133.9 14.5 %attend_1.1 = (bf16[256,1024]{1,0:T(8,128)(2,1)}, bf16[128,640]{1,0:T(8,128)(2,1)}, bf16[128,640]{1,0:T(8,128)(2,1)}) custom-call(s32[9]{0:T(128)} %pad_add_fusion.s, f32[1024,256]{1,0:T(8,128)} %project_1_3.1.acc_ref, bf16[2,256,2560]{2,1,0:T(8,128)(2,1)} %bitcast.14, bf16[2,256,1280]{2,1,0:T(8,128)(2,1)} %collective-permute-done.11.qb_ref, ...), custom_call_target="tpu_custom_call" | custom-call | flops 6375342080 | bytes 3932160 | tf_op jit(solution)/shard_map/attend_1/pallas_call | solution.py:274
  150.5 8.0 %partials_0.1.ou_ref.od_ref.g_ref = bf16[7,256,640]{2,1,0:T(8,128)(2,1)} custom-call(s32[9]{0:T(128)} %pad_add_fusion.s, bf16[256,1024]{1,0:T(8,128)(2,1)} %get-tuple-element.75.k_ref, bf16[8,512,640]{2,1,0:T(8,128)(2,1)} %norm.1.a_ref.fa_ref.refs_0_.refs_1_.refs_2_, bf16[8,512,640]{2,1,0:T(8,128)(2,1)} %collective-permute-done.1.b_ref.fb_ref.refs_3_.refs_4_.refs_5_), custom_call_target="tpu_custom_call" | custom-call | flops 2348810240 | bytes 9175040 | tf_op jit(solution)/shard_map/partials_0/pallas_call | solution.py:318
  164.6 8.0 %partials_1.1.ou_ref.od_ref.g_ref = bf16[7,256,640]{2,1,0:T(8,128)(2,1)} custom-call(s32[9]{0:T(128)} %pad_add_fusion.s, bf16[256,1024]{1,0:T(8,128)(2,1)} %get-tuple-element.60.k_ref, bf16[8,512,640]{2,1,0:T(8,128)(2,1)} %norm.1.a_ref.fa_ref.refs_0_.refs_1_.refs_2_, bf16[8,512,640]{2,1,0:T(8,128)(2,1)} %collective-permute-done.1.b_ref.fb_ref.refs_3_.refs_4_.refs_5_), custom_call_target="tpu_custom_call" | custom-call | flops 2348810240 | bytes 9175040 | tf_op jit(solution)/shard_map/partials_1/pallas_call | solution.py:318
  209.5 3.4 %code_0.1 = (bf16[272,640]{1,0:T(8,128)(2,1)}, bf16[272,640]{1,0:T(8,128)(2,1)}, bf16[144,640]{1,0:T(8,128)(2,1)}, bf16[144,640]{1,0:T(8,128)(2,1)}) custom-call(s32[9]{0:T(128)} %pad_add_fusion.s, bf16[7,256,640]{2,1,0:T(8,128)(2,1)} %partials_0.1.ou_ref.od_ref.g_ref, bf16[256,640]{1,0:T(8,128)(2,1)} %copy-done.20, bf16[256,640]{1,0:T(8,128)(2,1)} %copy-done.26, ...), custom_call_target="tpu_custom_call" | custom-call | bytes 2621440 | tf_op jit(solution)/shard_map/code_0/pallas_call | solution.py:407
  215.0 3.4 %code_1.1 = (bf16[272,640]{1,0:T(8,128)(2,1)}, bf16[272,640]{1,0:T(8,128)(2,1)}, bf16[144,640]{1,0:T(8,128)(2,1)}, bf16[144,640]{1,0:T(8,128)(2,1)}) custom-call(s32[9]{0:T(128)} %pad_add_fusion.s, bf16[7,256,640]{2,1,0:T(8,128)(2,1)} %partials_1.1.ou_ref.od_ref.g_ref, bf16[256,640]{1,0:T(8,128)(2,1)} %copy-done.18, bf16[256,640]{1,0:T(8,128)(2,1)} %copy-done.21, ...), custom_call_target="tpu_custom_call" | custom-call | bytes 2621440 | tf_op jit(solution)/shard_map/code_1/pallas_call | solution.py:407
  221.7 3.9 %collective-permute-done.42.refs_4_ = bf16[144,640]{1,0:T(8,128)(2,1)S(1)} collective-permute-done((bf16[144,640]{1,0:T(8,128)(2,1)S(1)}, bf16[144,640]{1,0:T(8,128)(2,1)S(1)}, u32[]{:S(2)}, u32[]{:S(2)}) %collective-permute-start.42) | collective-permute-done | bytes 184352 | tf_op jit(solution)/shard_map/ppermute | solution.py:497
  226.4 5.4 %finish_0.1 = (bf16[320,1024]{1,0:T(8,128)(2,1)}, f32[320,1024]{1,0:T(8,128)}, f32[320,1024]{1,0:T(8,128)}) custom-call(s32[9]{0:T(128)} %pad_add_fusion.s, bf16[320,1024]{1,0:T(8,128)(2,1)} %bitcast.19, f32[320,1024]{1,0:T(8,128)} %k_ref.3, f32[320,1024]{1,0:T(8,128)} %m_ref.3, bf16[272,640]{1,0:T(8,128)(2,1)} %get-tuple-element.85.refs_0_.refs_2_, ...), custom_call_target="tpu_custom_call" | custom-call | bytes 3932160 | tf_op jit(solution)/shard_map/finish_0/pallas_call | solution.py:456
  234.2 5.4 %finish_1.1 = (bf16[320,1024]{1,0:T(8,128)(2,1)}, f32[320,1024]{1,0:T(8,128)}, f32[320,1024]{1,0:T(8,128)}) custom-call(s32[9]{0:T(128)} %pad_add_fusion.s, bf16[320,1024]{1,0:T(8,128)(2,1)} %bitcast.20, f32[320,1024]{1,0:T(8,128)} %k_ref.3, f32[320,1024]{1,0:T(8,128)} %m_ref.3, ...), custom_call_target="tpu_custom_call", output_to_operand_aliasing={{0}: (10, {}), {1}: (11, {}), {2}: (12, {})} | custom-call | bytes 3932160 | tf_op jit(solution)/shard_map/finish_1/pallas_call | solution.py:456
  (179 shorter events, 86.9 us)
Async XLA Ops:
  14.3 72.6 %collective-permute-start.1 = (bf16[8,512,640]{2,1,0:T(8,128)(2,1)}, bf16[8,512,640]{2,1,0:T(8,128)(2,1)}, u32[]{:S(2)}, u32[]{:S(2)}) collective-permute-start(bf16[8,512,640]{2,1,0:T(8,128)(2,1)} %norm.1.a_ref.fa_ref.refs_0_.refs_1_.refs_2_), channel_id=1, source_target_pairs={{0,1},{1,0},{2,3},{3,2},{4,5},{5,4},{6,7},{7,6},{8,9},{9,8},{10,11... | collective-permute-start | bytes 15728648 | tf_op jit(solution)/shard_map/ppermute | solution.py:521
  17.5 17.4 %collective-permute-start.8 = (bf16[640,256]{1,0:T(8,128)(2,1)S(1)}, bf16[640,256]{1,0:T(8,128)(2,1)S(1)}, u32[]{:S(2)}, u32[]{:S(2)}) collective-permute-start(bf16[640,256]{1,0:T(8,128)(2,1)S(1)} %copy-done.5), channel_id=1, source_target_pairs={{0,4},{1,5},{2,0},{3,1},{4,8},{5,9},{6,2},{7,3},{8,12},{9,13},{10,... | collective-permute-start | bytes 983048 | tf_op jit(solution)/shard_map/ppermute | solution.py:515
  19.4 15.5 %collective-permute-start.2 = (bf16[640,256]{1,0:T(8,128)(2,1)S(1)}, bf16[640,256]{1,0:T(8,128)(2,1)S(1)}, u32[]{:S(2)}, u32[]{:S(2)}) collective-permute-start(bf16[640,256]{1,0:T(8,128)(2,1)S(1)} %copy-done.4), channel_id=1, source_target_pairs={{0,2},{1,3},{2,6},{3,7},{4,0},{5,1},{6,10},{7,11},{8,4},{9,5},{10,... | collective-permute-start | bytes 983048 | tf_op jit(solution)/shard_map/ppermute | solution.py:515
  25.9 13.8 %collective-permute-start.7 = (bf16[640,256]{1,0:T(8,128)(2,1)S(1)}, bf16[640,256]{1,0:T(8,128)(2,1)}, u32[]{:S(2)}, u32[]{:S(2)}) collective-permute-start(bf16[640,256]{1,0:T(8,128)(2,1)S(1)} %collective-permute-done.6.refs_1_), channel_id=1, source_target_pairs={{0,2},{1,3},{2,6},{3,7},{4,0},{5,1},{6,10},{7,11},{8,4},{9,5},{10,... | collective-permute-start | bytes 983048 | tf_op jit(solution)/shard_map/ppermute | solution.py:515
  27.9 14.1 %collective-permute-start.5 = (bf16[640,256]{1,0:T(8,128)(2,1)S(1)}, bf16[640,256]{1,0:T(8,128)(2,1)}, u32[]{:S(2)}, u32[]{:S(2)}) collective-permute-start(bf16[640,256]{1,0:T(8,128)(2,1)S(1)} %collective-permute-done.4.refs_2_), channel_id=1, source_target_pairs={{0,4},{1,5},{2,0},{3,1},{4,8},{5,9},{6,2},{7,3},{8,12},{9,13},{10,... | collective-permute-start | bytes 983048 | tf_op jit(solution)/shard_map/ppermute | solution.py:515
  34.9 46.3 %collective-permute-start.10 = (f32[320,1024]{1,0:T(8,128)S(1)}, f32[320,1024]{1,0:T(8,128)S(1)}, u32[]{:S(2)}, u32[]{:S(2)}) collective-permute-start(f32[320,1024]{1,0:T(8,128)S(1)} %copy-done.1), channel_id=1, source_target_pairs={{0,1},{1,0},{2,3},{3,2},{4,5},{5,4},{6,7},{7,6},{8,9},{9,8},{10,11... | collective-permute-start | bytes 3932168 | tf_op jit(solution)/shard_map/ppermute | solution.py:525
  34.9 14.0 %collective-permute-start.9 = (bf16[640,256]{1,0:T(8,128)(2,1)S(1)}, bf16[640,256]{1,0:T(8,128)(2,1)S(1)}, u32[]{:S(2)}, u32[]{:S(2)}) collective-permute-start(bf16[640,256]{1,0:T(8,128)(2,1)S(1)} %collective-permute-done.8.refs_2_), channel_id=1, source_target_pairs={{0,4},{1,5},{2,0},{3,1},{4,8},{5,9},{6,2},{7,3},{8,12},{9,13},{10,... | collective-permute-start | bytes 983048 | tf_op jit(solution)/shard_map/ppermute | solution.py:515
  42.0 13.1 %collective-permute-start.29 = (bf16[640,256]{1,0:T(8,128)(2,1)}, bf16[640,256]{1,0:T(8,128)(2,1)S(1)}, u32[]{:S(2)}, u32[]{:S(2)}) collective-permute-start(bf16[640,256]{1,0:T(8,128)(2,1)} %collective-permute-done.5.refs_1_), channel_id=1, source_target_pairs={{0,4},{1,5},{2,0},{3,1},{4,8},{5,9},{6,2},{7,3},{8,12},{9,13},{10,... | collective-permute-start | bytes 983048 | tf_op jit(solution)/shard_map/ppermute | solution.py:515
  48.9 66.4 %collective-permute-start.11 = (bf16[2,256,1280]{2,1,0:T(8,128)(2,1)}, bf16[2,256,1280]{2,1,0:T(8,128)(2,1)}, u32[]{:S(2)}, u32[]{:S(2)}) collective-permute-start(bf16[2,256,1280]{2,1,0:T(8,128)(2,1)} %dynamic-slice_bitcast_fusion.1), channel_id=1, source_target_pairs={{0,1},{1,0},{2,3},{3,2},{4,5},{5,4},{6,7},{7,6},{8,9},{9,8},{10,11... | collective-permute-start | bytes 3932168 | tf_op jit(solution)/shard_map/ppermute | solution.py:523
  49.2 66.2 %collective-permute-start.12 = (bf16[2,256,1280]{2,1,0:T(8,128)(2,1)}, bf16[2,256,1280]{2,1,0:T(8,128)(2,1)}, u32[]{:S(2)}, u32[]{:S(2)}) collective-permute-start(bf16[2,256,1280]{2,1,0:T(8,128)(2,1)} %dynamic-slice_bitcast_fusion), channel_id=1, source_target_pairs={{0,1},{1,0},{2,3},{3,2},{4,5},{5,4},{6,7},{7,6},{8,9},{9,8},{10,11... | collective-permute-start | bytes 3932168 | tf_op jit(solution)/shard_map/ppermute | solution.py:524
  79.2 35.4 %collective-permute-start.30 = (bf16[320,256]{1,0:T(8,128)(2,1)}, bf16[320,256]{1,0:T(8,128)(2,1)}, u32[]{:S(2)}, u32[]{:S(2)}) collective-permute-start(bf16[320,256]{1,0:T(8,128)(2,1)} %slice.18), channel_id=1, source_target_pairs={{0,4},{1,5},{2,0},{3,1},{4,8},{5,9},{6,2},{7,3},{8,12},{9,13},{10,... | collective-permute-start | bytes 491528 | tf_op jit(solution)/shard_map/ppermute | solution.py:518
  82.3 33.0 %collective-permute-start.31 = (bf16[320,256]{1,0:T(8,128)(2,1)}, bf16[320,256]{1,0:T(8,128)(2,1)S(1)}, u32[]{:S(2)}, u32[]{:S(2)}) collective-permute-start(bf16[320,256]{1,0:T(8,128)(2,1)} %slice.19), channel_id=1, source_target_pairs={{0,2},{1,3},{2,6},{3,7},{4,0},{5,1},{6,10},{7,11},{8,4},{9,5},{10,... | collective-permute-start | bytes 491528 | tf_op jit(solution)/shard_map/ppermute | solution.py:518
  86.9 45.6 %collective-permute-start.15 = (bf16[320,256]{1,0:T(8,128)(2,1)S(1)}, bf16[320,256]{1,0:T(8,128)(2,1)S(1)}, u32[]{:S(2)}, u32[]{:S(2)}) collective-permute-start(bf16[320,256]{1,0:T(8,128)(2,1)S(1)} %copy-done.38), channel_id=1, source_target_pairs={{0,4},{1,5},{2,0},{3,1},{4,8},{5,9},{6,2},{7,3},{8,12},{9,13},{10,... | collective-permute-start | bytes 491528 | tf_op jit(solution)/shard_map/ppermute | solution.py:518
  114.6 17.9 %collective-permute-start.16 = (bf16[320,256]{1,0:T(8,128)(2,1)S(1)}, bf16[320,256]{1,0:T(8,128)(2,1)S(1)}, u32[]{:S(2)}, u32[]{:S(2)}) collective-permute-start(bf16[320,256]{1,0:T(8,128)(2,1)S(1)} %copy-done.39), channel_id=1, source_target_pairs={{0,2},{1,3},{2,6},{3,7},{4,0},{5,1},{6,10},{7,11},{8,4},{9,5},{10,... | collective-permute-start | bytes 491528 | tf_op jit(solution)/shard_map/ppermute | solution.py:518
  130.5 28.0 %collective-permute-start.32 = (bf16[128,640]{1,0:T(8,128)(2,1)}, bf16[128,640]{1,0:T(8,128)(2,1)S(1)}, u32[]{:S(2)}, u32[]{:S(2)}) collective-permute-start(bf16[128,640]{1,0:T(8,128)(2,1)} %get-tuple-element.76), channel_id=1, source_target_pairs={{0,4},{1,5},{2,0},{3,1},{4,8},{5,9},{6,2},{7,3},{8,12},{9,13},{10,... | collective-permute-start | bytes 491528 | tf_op jit(solution)/shard_map/ppermute | solution.py:546
  132.0 26.4 %collective-permute-start.33 = (bf16[128,640]{1,0:T(8,128)(2,1)}, bf16[128,640]{1,0:T(8,128)(2,1)S(1)}, u32[]{:S(2)}, u32[]{:S(2)}) collective-permute-start(bf16[128,640]{1,0:T(8,128)(2,1)} %get-tuple-element.77), channel_id=1, source_target_pairs={{0,2},{1,3},{2,6},{3,7},{4,0},{5,1},{6,10},{7,11},{8,4},{9,5},{10,... | collective-permute-start | bytes 491528 | tf_op jit(solution)/shard_map/ppermute | solution.py:546
  148.4 24.2 %collective-permute-start.17 = (bf16[128,640]{1,0:T(8,128)(2,1)}, bf16[128,640]{1,0:T(8,128)(2,1)S(1)}, u32[]{:S(2)}, u32[]{:S(2)}) collective-permute-start(bf16[128,640]{1,0:T(8,128)(2,1)} %get-tuple-element.61), channel_id=1, source_target_pairs={{0,4},{1,5},{2,0},{3,1},{4,8},{5,9},{6,2},{7,3},{8,12},{9,13},{10,... | collective-permute-start | bytes 491528 | tf_op jit(solution)/shard_map/ppermute | solution.py:546
  149.9 22.7 %collective-permute-start.18 = (bf16[128,640]{1,0:T(8,128)(2,1)}, bf16[128,640]{1,0:T(8,128)(2,1)S(1)}, u32[]{:S(2)}, u32[]{:S(2)}) collective-permute-start(bf16[128,640]{1,0:T(8,128)(2,1)} %get-tuple-element.62), channel_id=1, source_target_pairs={{0,2},{1,3},{2,6},{3,7},{4,0},{5,1},{6,10},{7,11},{8,4},{9,5},{10,... | collective-permute-start | bytes 491528 | tf_op jit(solution)/shard_map/ppermute | solution.py:546
  162.6 16.1 %collective-permute-start.34 = (bf16[256,640]{1,0:T(8,128)(2,1)}, bf16[256,640]{1,0:T(8,128)(2,1)S(1)}, u32[]{:S(2)}, u32[]{:S(2)}) collective-permute-start(bf16[256,640]{1,0:T(8,128)(2,1)} %get-tuple-element.78), channel_id=1, source_target_pairs={{0,4},{1,5},{2,0},{3,1},{4,8},{5,9},{6,2},{7,3},{8,12},{9,13},{10,... | collective-permute-start | bytes 983048 | tf_op jit(solution)/shard_map/ppermute | solution.py:546
  164.0 14.7 %collective-permute-start.35 = (bf16[256,640]{1,0:T(8,128)(2,1)}, bf16[256,640]{1,0:T(8,128)(2,1)S(1)}, u32[]{:S(2)}, u32[]{:S(2)}) collective-permute-start(bf16[256,640]{1,0:T(8,128)(2,1)} %get-tuple-element.79), channel_id=1, source_target_pairs={{0,2},{1,3},{2,6},{3,7},{4,0},{5,1},{6,10},{7,11},{8,4},{9,5},{10,... | collective-permute-start | bytes 983048 | tf_op jit(solution)/shard_map/ppermute | solution.py:546
  213.5 12.0 %collective-permute-start.41 = (bf16[272,640]{1,0:T(8,128)(2,1)}, bf16[272,640]{1,0:T(8,128)(2,1)S(1)}, u32[]{:S(2)}, u32[]{:S(2)}) collective-permute-start(bf16[272,640]{1,0:T(8,128)(2,1)} %get-tuple-element.87), channel_id=1, source_target_pairs={{0,1},{1,0},{2,3},{3,2},{4,5},{5,4},{6,7},{7,6},{8,9},{9,8},{10,11... | collective-permute-start | bytes 1044488 | tf_op jit(solution)/shard_map/ppermute | solution.py:551
  218.4 15.1 %collective-permute-start.26 = (bf16[272,640]{1,0:T(8,128)(2,1)}, bf16[272,640]{1,0:T(8,128)(2,1)S(1)}, u32[]{:S(2)}, u32[]{:S(2)}) collective-permute-start(bf16[272,640]{1,0:T(8,128)(2,1)} %get-tuple-element.72), channel_id=1, source_target_pairs={{0,1},{1,0},{2,3},{3,2},{4,5},{5,4},{6,7},{7,6},{8,9},{9,8},{10,11... | collective-permute-start | bytes 1044488 | tf_op jit(solution)/shard_map/ppermute | solution.py:551
  219.9 11.9 %collective-permute-start.25 = (bf16[144,640]{1,0:T(8,128)(2,1)}, bf16[144,640]{1,0:T(8,128)(2,1)S(1)}, u32[]{:S(2)}, u32[]{:S(2)}) collective-permute-start(bf16[144,640]{1,0:T(8,128)(2,1)} %get-tuple-element.71), channel_id=1, source_target_pairs={{0,16},{1,17},{2,18},{3,19},{4,20},{5,21},{6,22},{7,23},{8,24},{9,... | collective-permute-start | bytes 552968 | tf_op jit(solution)/shard_map/ppermute | solution.py:497
  220.6 12.9 %collective-permute-start.27 = (bf16[144,640]{1,0:T(8,128)(2,1)}, bf16[144,640]{1,0:T(8,128)(2,1)S(1)}, u32[]{:S(2)}, u32[]{:S(2)}) collective-permute-start(bf16[144,640]{1,0:T(8,128)(2,1)} %get-tuple-element.73), channel_id=1, source_target_pairs={{0,17},{1,16},{2,19},{3,18},{4,21},{5,20},{6,23},{7,22},{8,25},{9,... | collective-permute-start | bytes 552968 | tf_op jit(solution)/shard_map/ppermute | solution.py:497
  (63 other events, 456.9 us)

commit v3 on v2

v3 whole, which is shorter than its diff:
```python
import functools

import jax
import jax.numpy as jnp
import numpy as np
from jax import lax
from jax.experimental import pallas as pl
from jax.experimental.pallas import tpu as pltpu
from jax.sharding import PartitionSpec as P

HD = 128

inner_rate = 0.25
outer_rate = 0.7
momentum_decay = 0.9
blend_share = 0.5
norm_eps = 1e-06
scale_eps = 1e-06

F32 = jnp.float32
BF16 = jnp.bfloat16
VMEM_LIMIT = 62 * 1024 * 1024
SCALE_ROWS = 16


def ring_order(count):
    return list(range(0, count, 2)) + list(range(1, count, 2))[::-1]


def call(body, out_shape, in_specs, out_specs, grid=(1,), scratch=(), flops=0, moved=0, aliases=None, name=None):
    return pl.pallas_call(
        body,
        out_shape=out_shape,
        grid_spec=pltpu.PrefetchScalarGridSpec(
            num_scalar_prefetch=1,
            grid=grid,
            in_specs=in_specs,
            out_specs=out_specs,
            scratch_shapes=list(scratch),
        ),
        compiler_params=pltpu.CompilerParams(
            vmem_limit_bytes=VMEM_LIMIT, dimension_semantics=("arbitrary",) * len(grid)
        ),
        cost_estimate=pl.CostEstimate(flops=int(flops), bytes_accessed=int(moved), transcendentals=0),
        input_output_aliases=aliases or {},
        name=name,
    )


def whole(shape):
    zeros = (0,) * len(shape)
    return pl.BlockSpec(shape, lambda i, s: zeros)


def dot_nn(a, b):
    return lax.dot_general(a, b, (((1,), (0,)), ((), ())), preferred_element_type=F32)


def dot_nt(a, b):
    return lax.dot_general(a, b, (((1,), (1,)), ((), ())), preferred_element_type=F32)


def dot_tn(a, b):
    return lax.dot_general(a, b, (((0,), (0,)), ((), ())), preferred_element_type=F32)


def norm_rows(scalars, hidden_rows, norm_gain, chips):
    tokens, width = hidden_rows.shape
    part = width // chips
    tile = 128

    def body(s, x_ref, g_ref, o_ref):
        total = jnp.zeros((tile, 1), F32)
        for b in range(chips):
            x = x_ref[:, b * part : (b + 1) * part].astype(F32)
            total = total + jnp.sum(x * x, axis=-1, keepdims=True)
        factor = lax.rsqrt(total * (1.0 / width) + norm_eps)
        for b in range(chips):
            x = x_ref[:, b * part : (b + 1) * part].astype(F32)
            o_ref[b] = (x * factor * g_ref[:, b * part : (b + 1) * part]).astype(BF16)

    return call(
        body,
        jax.ShapeDtypeStruct((chips, tokens, part), BF16),
        [pl.BlockSpec((tile, width), lambda i, s: (i, 0)), whole((1, width))],
        pl.BlockSpec((chips, tile, part), lambda i, s: (0, i, 0)),
        grid=(tokens // tile,),
        flops=tokens * width * 6,
        moved=tokens * width * 4,
        name="norm",
    )(scalars, hidden_rows, norm_gain.reshape(1, width))


def columns_of(core, head, kv, heads, kv_width):
    return pl.multiple_of(kv * kv_width + (core * heads + head) * HD, HD)


def own_blocks(scalars, weight, received, heads):
    rows, cols = weight.shape

    def body(s, w_ref, r_ref, *o_refs):
        core = s[0]
        mine = pl.multiple_of(core * rows, 16)
        theirs = pl.multiple_of((1 - core) * rows, 16)
        for h in range(heads):
            for kv in range(2):
                there = pl.ds(columns_of(core, h, kv, heads, cols // 2), HD)
                lanes = slice(kv * HD, (kv + 1) * HD)
                o_refs[h][pl.ds(mine, rows), lanes] = w_ref[:, there]
                o_refs[h][pl.ds(theirs, rows), lanes] = r_ref[:, there]

    shape = (2 * rows, 2 * HD)
    return call(
        body,
        [jax.ShapeDtypeStruct(shape, weight.dtype)] * heads,
        [whole((rows, cols))] * 2,
        [whole(shape)] * heads,
        moved=rows * cols * 6,
        name="own_blocks",
    )(scalars, weight, received)


def start_deltas(scalars, blocks, outer, received, heads):
    rows, cols = outer.shape

    def body(s, o_ref, r_ref, *refs):
        core = s[0]
        for h in range(heads):
            block_ref, out_ref = refs[h], refs[heads + h]
            for kv in range(2):
                there = pl.ds(columns_of(core, h, kv, heads, cols // 2), HD)
                mine = o_ref[:, there]
                theirs = r_ref[:, there]
                first = jnp.where(core == 0, mine, theirs)
                second = jnp.where(core == 0, theirs, mine)
                both = jnp.concatenate([first, second], axis=0)
                both = both - block_ref[:, kv * HD : (kv + 1) * HD].astype(F32)
                out_ref[kv * HD : (kv + 1) * HD, :] = both.T

    return call(
        body,
        [jax.ShapeDtypeStruct((2 * HD, 2 * rows), F32)] * heads,
        [whole((rows, cols))] * 2 + [whole((2 * rows, 2 * HD))] * heads,
        [whole((2 * HD, 2 * rows))] * heads,
        moved=rows * cols * 14,
        name="start_deltas",
    )(scalars, outer, received, *blocks)


def group_step(scalars, rows_mine, rows_other, blocks, halves, queries, queries_other, out_grad, out_grad_other, heads):
    chips, tokens, part = rows_mine.shape
    seqs, length, query_width = queries.shape
    own_width = query_width // 2
    repeat = own_width // (heads * HD)
    inv_root = (chips * part) ** (-0.5)
    half = length // 2
    last = chips - 1
    two_power = HD ** (-0.5) * 1.4426950408889634
    wide = 2 * HD

    def body(s, a_ref, b_ref, qa_ref, qb_ref, ga_ref, gb_ref, *refs):
        block_refs = [refs[h * last : (h + 1) * last] for h in range(heads)]
        half_refs = [refs[heads * last + 2 * h : heads * last + 2 * h + 2] for h in range(heads)]
        refs = refs[heads * (last + 2) :]
        sum_refs, up_refs, down_refs = refs[:heads], refs[heads : 2 * heads], refs[2 * heads : 3 * heads]
        held, w_held, q_held, g_held, acc, grads, done = refs[3 * heads : 3 * heads + 7]
        row_sems, w_sems, q_sems, out_sems = refs[3 * heads + 7 :]

        waits = []
        for k in range(chips):
            wait = []
            for side, ref in enumerate((a_ref, b_ref)):
                wait.append(pltpu.make_async_copy(ref.at[s[1 + k]], held.at[k, side], row_sems.at[k, side]))
            for h in range(heads):
                if k < last:
                    wait.append(pltpu.make_async_copy(block_refs[h][k], w_held.at[h, k], w_sems.at[h, k]))
                else:
                    for at in range(2):
                        there = w_held.at[h, k, pl.ds(at * (part // 2), part // 2)]
                        wait.append(pltpu.make_async_copy(half_refs[h][at], there, w_sems.at[h, k + at]))
            waits.append(wait)
        mine = pl.ds(pl.multiple_of(s[0] * own_width, HD), own_width)
        pairs = (
            (qa_ref.at[:, :, mine], q_held.at[pl.ds(0, seqs)]),
            (ga_ref.at[:, :, mine], g_held.at[pl.ds(0, seqs)]),
            (qb_ref.at[:, :, mine], q_held.at[pl.ds(seqs, seqs)]),
            (gb_ref.at[:, :, mine], g_held.at[pl.ds(seqs, seqs)]),
        )
        query_waits = [pltpu.make_async_copy(x, y, q_sems.at[k]) for k, (x, y) in enumerate(pairs)]
        for wait in waits:
            for copy in wait:
                copy.start()
        for copy in query_waits:
            copy.start()

        for k in range(chips):
            for copy in waits[k]:
                copy.wait()
            for h in range(heads):
                for side in range(2):
                    here = slice(side * tokens, (side + 1) * tokens)
                    product = dot_nn(held[k, side], w_held[h, k])
                    acc[h, here, :] = product if k == 0 else acc[h, here, :] + product
        for copy in query_waits:
            copy.wait()

        def one(at, carry):
            token = pl.ds(pl.multiple_of(at * length, length), length)
            for h in range(heads):
                kv = (acc[h, token, :] * inv_root).astype(BF16)
                keys, values = kv[:, :HD], kv[:, HD:]
                found = []
                for t in range(2):
                    upto = (t + 1) * half
                    rows_of = slice(t * half, upto)
                    lanes = [slice((h * repeat + r) * HD, (h * repeat + r + 1) * HD) for r in range(repeat)]
                    q = jnp.concatenate([q_held[at, rows_of, x] for x in lanes], axis=0)
                    g = jnp.concatenate([g_held[at, rows_of, x] for x in lanes], axis=0)
                    scores = dot_nt(keys[:upto], q) * two_power
                    causal = lax.broadcasted_iota(jnp.int32, (half, half), 0) <= lax.broadcasted_iota(
                        jnp.int32, (half, half), 1
                    )
                    causal = jnp.concatenate([causal.astype(F32)] * repeat, axis=1) > 0.0
                    end = jnp.where(causal, scores[upto - half :], -1e30)
                    scores = end if t == 0 else jnp.concatenate([scores[:half], end], axis=0)
                    highest = jnp.max(scores, axis=0, keepdims=True)
                    exps = jnp.exp2(scores - highest)
                    prob = exps * (1.0 / jnp.sum(exps, axis=0, keepdims=True))
                    prob_grad = dot_nt(values[:upto], g).astype(BF16).astype(F32)
                    weighted = prob * prob_grad
                    mean = jnp.sum(weighted, axis=0, keepdims=True)
                    score_grad = (weighted - prob * mean).astype(BF16)
                    found.append((dot_nn(score_grad, q), dot_nn(prob.astype(BF16), g)))
                for kv_at, factor in ((0, HD ** (-0.5)), (1, 1.0)):
                    early, late = found[0][kv_at], found[1][kv_at]
                    grad = jnp.concatenate([(late[:half] + early) * factor, late[half:] * factor], axis=0)
                    grads[h * wide + kv_at * HD : h * wide + (kv_at + 1) * HD, token] = grad.T.astype(BF16)
            return carry

        lax.fori_loop(0, 2 * seqs, one, 0)

        leaving = []
        for k in [last] + list(range(last))[::-1]:
            total = dot_nn(grads[:, :tokens], held[k, 0]) + dot_nn(grads[:, tokens:], held[k, 1])
            total = (total * inv_root).astype(BF16)
            for h in range(heads):
                done[h, k] = total[h * wide : (h + 1) * wide]
                if k < last:
                    leaving.append(pltpu.make_async_copy(done.at[h, k], sum_refs[h].at[k], out_sems.at[h, k]))
                else:
                    for at, ref in enumerate((up_refs[h], down_refs[h])):
                        there = done.at[h, k, pl.ds(at * HD, HD)]
                        leaving.append(pltpu.make_async_copy(there, ref, out_sems.at[h, k + at]))
            for copy in leaving[-heads if k < last else -2 * heads :]:
                copy.start()
        for copy in leaving:
            copy.wait()

    any_spec = pl.BlockSpec(memory_space=pl.ANY)
    inputs = [rows_mine, rows_other, queries, queries_other, out_grad, out_grad_other]
    for h in range(heads):
        inputs += blocks[h]
    for h in range(heads):
        inputs += halves[h]
    flops = 2 * 2 * tokens * chips * part * wide * heads * 2 + heads * 2 * seqs * repeat * length * length * HD * 16
    outs = call(
        body,
        [jax.ShapeDtypeStruct((last, wide, part), BF16)] * heads + [jax.ShapeDtypeStruct((HD, part), BF16)] * (2 * heads),
        [any_spec] * len(inputs),
        [any_spec] * (3 * heads),
        scratch=[
            pltpu.VMEM((chips, 2, tokens, part), BF16),
            pltpu.VMEM((heads, chips, part, wide), BF16),
            pltpu.VMEM((2 * seqs, length, own_width), BF16),
            pltpu.VMEM((2 * seqs, length, own_width), BF16),
            pltpu.VMEM((heads, 2 * tokens, wide), F32),
            pltpu.VMEM((heads * wide, 2 * tokens), BF16),
            pltpu.VMEM((heads, chips, wide, part), BF16),
            pltpu.SemaphoreType.DMA((chips, 2)),
            pltpu.SemaphoreType.DMA((heads, chips + 1)),
            pltpu.SemaphoreType.DMA((4,)),
            pltpu.SemaphoreType.DMA((heads, chips + 1)),
        ],
        flops=flops,
        moved=2 * tokens * chips * part * 6,
        name="group_step",
    )(scalars, *inputs)
    return outs[:heads], outs[heads : 2 * heads], outs[2 * heads :]


def add_partials(scalars, own, up, down, distance, name):
    part = own.shape[-1]
    is_half = up.shape[0] == HD
    at = 2 * distance - 1

    def body(s, ou_ref, od_ref, ui_ref, di_ref, up_ref, down_ref):
        mine_up, mine_down = ou_ref[0].astype(F32), od_ref[0].astype(F32)
        if is_half:
            keys = pl.program_id(0) == 0
            up_ref[...] = jnp.where(keys, mine_up + ui_ref[...].astype(F32), mine_up).astype(BF16)
            down_ref[...] = jnp.where(keys, mine_down, mine_down + di_ref[...].astype(F32)).astype(BF16)
        else:
            up_ref[...] = (mine_up + ui_ref[...].astype(F32)).astype(BF16)
            down_ref[...] = (mine_down + di_ref[...].astype(F32)).astype(BF16)

    block = (HD, part)
    came = whole(block) if is_half else pl.BlockSpec(block, lambda i, s: (i, 0))
    shape = jax.ShapeDtypeStruct((2 * HD, part), BF16)
    return call(
        body,
        [shape] * 2,
        [
            pl.BlockSpec((1, HD, part), lambda i, s: (at, i, 0)),
            pl.BlockSpec((1, HD, part), lambda i, s: (at + 1, i, 0)),
            came,
            came,
        ],
        [pl.BlockSpec(block, lambda i, s: (i, 0))] * 2,
        grid=(2,),
        moved=2 * HD * part * 12,
        name=name,
    )(scalars, own, own, up, down)


def split_packs(values):
    deep = values.shape[0] // 2
    rows = values.shape[1] // 2
    return [
        jnp.concatenate([values[:deep, k * rows : (k + 1) * rows], values[deep:, k * rows : (k + 1) * rows]], axis=1)
        for k in range(2)
    ]


def code_deltas(scalars, own, up, down, delta_start, name):
    part = own.shape[-1]

    def body(s, g_ref, ui_ref, di_ref, d_ref, own_ref, core_ref, y_ref, far_ref):
        core = s[0]
        total = g_ref[0].astype(F32) + ui_ref[...].astype(F32) + di_ref[...].astype(F32)
        delta = d_ref[...] + inner_rate * total
        scales, coded = [], []
        for kv in range(2):
            piece = delta[kv * HD : (kv + 1) * HD]
            scale = (jnp.max(jnp.abs(piece), axis=0, keepdims=True) + scale_eps).astype(BF16).astype(F32)
            scales.append(scale)
            coded.append(piece / scale)
        grads = split_packs(total)
        codes = split_packs(jnp.concatenate(coded, axis=0))
        levels = split_packs(jnp.concatenate(scales, axis=0))
        for mine, wide_ref, thin_ref in ((True, own_ref, y_ref), (False, core_ref, far_ref)):
            first = (core == 0) if mine else (core == 1)
            grad = jnp.where(first, grads[0], grads[1]).astype(BF16)
            code = jnp.where(first, codes[0], codes[1]).astype(BF16)
            level = jnp.where(first, levels[0], levels[1])
            level = jnp.broadcast_to(level, (SCALE_ROWS, part)).astype(BF16)
            wide_ref[:HD, :] = code
            wide_ref[HD : HD + SCALE_ROWS, :] = level
            wide_ref[HD + SCALE_ROWS :, :] = grad
            thin_ref[:HD, :] = code
            thin_ref[HD:, :] = level

    wide, thin = (2 * HD + SCALE_ROWS, part), (HD + SCALE_ROWS, part)
    return call(
        body,
        [jax.ShapeDtypeStruct(shape, BF16) for shape in (wide, wide, thin, thin)],
        [
            pl.BlockSpec((1, 2 * HD, part), lambda i, s: (0, 0, 0)),
            whole(up.shape),
            whole(down.shape),
            whole(delta_start.shape),
        ],
        [whole(wide), whole(wide), whole(thin), whole(thin)],
        moved=2 * HD * part * 16,
        name=name,
    )(scalars, own, up, down, delta_start)


def finish(scalars, weight, outer, momentum, grads, codes, before, head, heads):
    rows, cols = weight.shape
    groups = len(codes[0])
    packs = [*codes[0], grads[0], *codes[1], grads[1]]
    kept = [] if before is None else list(before)
    count = len(packs)

    def body(s, w_ref, k_ref, m_ref, *refs):
        pack_refs = refs[:count]
        out_refs = refs[count + len(kept) : count + len(kept) + 3]
        refs = refs[count + len(kept) + 3 :]
        pack_held = refs[:count]
        w_held, k_held, m_held, blend, stepped, moved, pack_sems, in_sems, out_sems = refs[count:]

        def columns(at):
            core = s[0] if at < 2 else 1 - s[0]
            return pl.ds(columns_of(core, head, at % 2, heads, cols // 2), HD)

        pack_waits = [pltpu.make_async_copy(x, y, pack_sems.at[k]) for k, (x, y) in enumerate(zip(pack_refs, pack_held))]
        waits = []
        for at in range(4):
            held = ((w_ref, w_held), (k_ref, k_held), (m_ref, m_held))
            waits.append([pltpu.make_async_copy(x.at[:, columns(at)], y.at[at], in_sems.at[at, k]) for k, (x, y) in enumerate(held)])
        for copy in pack_waits[: count // 2] + waits[0] + waits[1] + pack_waits[count // 2 :] + waits[2] + waits[3]:
            copy.start()
        leaving = []
        for at in range(4):
            side, kv = at // 2, at % 2
            own = range(side * (groups + 1), (side + 1) * (groups + 1))
            if kv == 0:
                for k in own:
                    pack_waits[k].wait()
            lanes = slice(kv * rows, (kv + 1) * rows)
            grad = pack_held[own[-1]][HD + SCALE_ROWS :, lanes].astype(F32).T
            total = jnp.zeros((HD, rows), F32)
            for k in own[:-1]:
                total = total + pack_held[k][:HD, lanes].astype(F32) * pack_held[k][HD : HD + 1, lanes].astype(F32)
            average = (total / groups).T
            for copy in waits[at]:
                copy.wait()
            fresh = w_held[at].astype(F32) - inner_rate * grad
            moment = momentum_decay * m_held[at] + average
            new = k_held[at] - outer_rate * (momentum_decay * moment + average)
            moved[at] = moment
            stepped[at] = new
            blend[at] = (blend_share * fresh + (1.0 - blend_share) * new).astype(BF16)
            for k, (x, y) in enumerate(zip((blend, stepped, moved), out_refs)):
                leaving.append(pltpu.make_async_copy(x.at[at], y.at[:, columns(at)], out_sems.at[at, k]))
                leaving[-1].start()
        for copy in leaving:
            copy.wait()

    any_spec = pl.BlockSpec(memory_space=pl.ANY)
    return call(
        body,
        [
            jax.ShapeDtypeStruct((rows, cols), BF16),
            jax.ShapeDtypeStruct((rows, cols), F32),
            jax.ShapeDtypeStruct((rows, cols), F32),
        ],
        [any_spec] * (3 + count + len(kept)),
        [any_spec] * 3,
        scratch=[pltpu.VMEM(p.shape, BF16) for p in packs]
        + [pltpu.VMEM((4, rows, HD), t) for t in (BF16, F32, F32, BF16, F32, F32)]
        + [
            pltpu.SemaphoreType.DMA((count,)),
            pltpu.SemaphoreType.DMA((4, 3)),
            pltpu.SemaphoreType.DMA((4, 3)),
        ],
        moved=rows * cols * 12,
        aliases={4 + count + k: k for k in range(len(kept))},
        name=f"finish_{head}",
    )(scalars, weight, outer, momentum, *packs, *kept)


def local(hidden, norm_gain, queries, out_grad, kv_inner, kv_outer, momentum):
    count = lax.axis_size("fsdp")
    groups = lax.axis_size("group")
    index = lax.axis_index("fsdp")
    group = lax.axis_index("group")
    chips = count // 2
    far = chips // 2
    ring = ring_order(chips)
    place = {chip: at for at, chip in enumerate(ring)}
    order = [0] + [k % chips for step in range(1, far) for k in (step, -step)] + [far]
    walks = np.array([[ring[(place[j] + k) % chips] for k in order] for j in range(chips)], np.int32)
    core = index % 2
    scalars = jnp.concatenate([core[None].astype(jnp.int32), jnp.asarray(walks)[index // 2]])

    def around(shift):
        return [(2 * j + c, 2 * ring[(place[j] + shift) % chips] + c) for j in range(chips) for c in range(2)]

    up = functools.partial(lax.ppermute, axis_name="fsdp", perm=around(1))
    down = functools.partial(lax.ppermute, axis_name="fsdp", perm=around(-1))
    swap = functools.partial(lax.ppermute, axis_name="fsdp", perm=[(i, i ^ 1) for i in range(count)])

    def across(values, shift, flip):
        pairs = [
            (g * count + i, (g + shift) % groups * count + (i ^ flip)) for g in range(groups) for i in range(count)
        ]
        return lax.ppermute(values, ("group", "fsdp"), pairs)

    weight = kv_inner[0]
    rows, cols = weight.shape
    heads = cols // 2 // HD // 2
    seqs, length, width = hidden.shape[1:]
    part = 2 * rows

    own = own_blocks(scalars, weight, swap(weight), heads)

    tied = lax.optimization_barrier
    own, outer_other, queries_other = tied((own, swap(kv_outer), swap(queries[0])))
    out_grad_other = swap(tied((out_grad[0], own))[0])
    rows_mine = norm_rows(scalars, tied((hidden, own))[0].reshape(seqs * length, width), norm_gain, chips)

    blocks = [[own[h]] for h in range(heads)]
    halves = [None] * heads
    ups, downs = list(own), list(own)
    for step in range(1, far + 1):
        for h in range(heads):
            if step < far:
                ups[h], downs[h] = up(ups[h]), down(downs[h])
                blocks[h] += [downs[h], ups[h]]
            else:
                halves[h] = (up(ups[h][: part // 2]), down(downs[h][part // 2 :]))
        if step == 1:
            rows_other = swap(tied((rows_mine, out_grad_other, ups, downs))[0])
    deltas = start_deltas(scalars, own, kv_outer, outer_other, heads)

    rows_mine, deltas = lax.optimization_barrier((rows_mine, deltas))
    sums, far_up, far_down = group_step(
        scalars, rows_mine, rows_other, blocks, halves, queries[0], queries_other, out_grad[0], out_grad_other, heads
    )

    outs = None
    for h in range(heads):
        going_up, going_down = far_up[h], far_down[h]
        for distance in range(far - 1, 0, -1):
            going_up, going_down = add_partials(
                scalars, sums[h], up(going_up), down(going_down), distance, f"add_{h}_{distance}"
            )
        own_pack, core_pack, thin_own, thin_core = code_deltas(
            scalars, sums[h], up(going_up), down(going_down), deltas[h], f"code_{h}"
        )
        from_core = swap(core_pack)
        mine = [own_pack] + [across(thin_own, k, 0) for k in range(1, groups)]
        theirs = [from_core] + [across(thin_core, k, 1) for k in range(1, groups)]
        if groups > 2:
            deep = HD + SCALE_ROWS
            ordered = []
            for packs in (mine, theirs):
                stacked = jnp.stack([p[:deep] for p in packs])
                ordered.append([stacked[(group - g) % groups] for g in range(groups)])
            mine, theirs = ordered
        outs = finish(
            scalars, weight, kv_outer, momentum, (own_pack, from_core), (mine, theirs), outs, h, heads
        )

    blended, outer_new, momentum_new = outs
    return (blended[None], outer_new, momentum_new)


def solution(mesh):
    in_specs = (
        P("group", "fsdp", None, None),
        P(),
        P("group", "fsdp", None, None),
        P("group", "fsdp", None, None),
        P("group", "fsdp", None),
        P("fsdp", None),
        P("fsdp", None),
    )
    out_specs = (P("group", "fsdp", None), P("fsdp", None), P("fsdp", None))
    return jax.shard_map(local, mesh=mesh, in_specs=in_specs, out_specs=out_specs, check_vma=False)
```

time: 241 us -> 182 us (0.76)
  Pallas kernels: 120 us -> 73.1 us
  local copies, waits for them, and re-layouts: 20.6 us -> 9.74 us
    pallas_call x8 -> x1, Pallas kernels: 71.1 us -> 26.3 us  [group_step(): call(body, [jax.ShapeDtypeStruct((last, wide, part), BF16)] * heads + [ja...]
    ppermute x12, waiting for transfers between devices: 45.8 us -> 28.9 us  [local(): ups[h], downs[h] = (up(ups[h]), down(downs[h]))]
    ppermute x8, waiting for transfers between devices: 2.26 us -> 8.69 us  [local(): up(going_up)]
    ppermute x1, waiting for transfers between devices: 0.65 us -> 5.64 us  [local(): own = own_blocks(scalars, weight, swap(weight), heads)]
    unnamed x88 -> x70, local copies, waits for them, and re-layouts: 13.5 us -> 9 us
    dynamic_slice x2 -> x0, local copies, waits for them, and re-layouts: 3.61 us -> none  [the longest x1 2.46 us: local(): lax.dynamic_slice_in_dim(queries[0], at, half_width, axis=2)]
    slice x4, local copies, waits for them, and re-layouts: 2.76 us -> 0.05 us  [local(): halves[h] = (up(ups[h][:part // 2]), down(downs[h][part // 2:]))]
  transfers between devices with their start and end apart: 43 -> 43, of which waited for: 19 -> 23; matrix products, arithmetic and copies ran while one was open for 3% -> 1% of each run, Pallas kernels for 43% -> 23%
where the time goes in v3:
time: 182 us
  Pallas kernels  73.1 us (40%)
  waiting for transfers between devices  58 us (32%)
  starting transfers between devices  39 us (21%)
  local copies, waits for them, and re-layouts  9.74 us (5%)
    ppermute x12, waiting for transfers between devices, local(): ups[h], downs[h] = (up(ups[h]), down(downs[h]))  28.9 us
    pallas_call x1, Pallas kernels, group_step(): call(body, [jax.ShapeDtypeStruct((last, wide, part), BF16)] * heads + [ja...  26.3 us
    pallas_call x6, Pallas kernels, add_partials(): call(body, [shape] * 2, [pl.BlockSpec((1, HD, part), lambda i, s: (at, i,...  16.9 us
    ppermute x12, starting transfers between devices, local(): ups[h], downs[h] = (up(ups[h]), down(downs[h]))  12.9 us
    pallas_call x2, Pallas kernels, finish(): call(body, [jax.ShapeDtypeStruct((rows, cols), BF16), jax.ShapeDtypeStruc...  9.17 us
    ppermute x8, starting transfers between devices, local(): up(going_up)  9.09 us
    unnamed x70, local copies, waits for them, and re-layouts  9 us
    ppermute x8, waiting for transfers between devices, local(): up(going_up)  8.69 us
  transfers between devices with their start and end apart: 43, of which 23 were waited for; matrix products, arithmetic and copies ran while one was open for 1% of the time, Pallas kernels for 23%

profile of v3, /device:TPU:0, one launch (start us, length us, event | category | flops | bytes accessed | tf_op | source)
XLA Modules:
  0.0 181.6 jit_solution(775330896620353384)
XLA Ops:
  3.0 5.6 %collective-permute-done.r_ref = bf16[320,1024]{1,0:T(8,128)(2,1)S(1)} collective-permute-done((bf16[320,1024]{1,0:T(8,128)(2,1)}, bf16[320,1024]{1,0:T(8,128)(2,1)S(1)}, u32[]{:S(2)}, u32[]{:S(2)}) %collective-permute-start) | collective-permute-done | bytes 655392 | tf_op jit(solution)/shard_map/ppermute | solution.py:486
  9.5 3.0 %own_blocks.1 = (bf16[640,256]{1,0:T(8,128)(2,1)}, bf16[640,256]{1,0:T(8,128)(2,1)}) custom-call(s32[9]{0:T(128)} %pad_add_fusion.s, bf16[320,1024]{1,0:T(8,128)(2,1)} %bitcast.10, bf16[320,1024]{1,0:T(8,128)(2,1)} %copy-done.3), custom_call_target="tpu_custom_call" | custom-call | bytes 1966080 | tf_op jit(solution)/shard_map/own_blocks/pallas_call | solution.py:113
  12.8 2.6 %collective-permute-start.6 = (bf16[640,256]{1,0:T(8,128)(2,1)}, bf16[640,256]{1,0:T(8,128)(2,1)S(1)}, u32[]{:S(2)}, u32[]{:S(2)}) collective-permute-start(bf16[640,256]{1,0:T(8,128)(2,1)} %get-tuple-element.51.refs_0_), channel_id=1, source_target_pairs={{0,2},{1,3},{2,6},{3,7},{4,0},{5,1},{6,10},{7,11},{8,4},{9,5},{10,... | collective-permute-start | bytes 983048 | tf_op jit(solution)/shard_map/ppermute | solution.py:499
  17.6 7.3 %norm.1.a_ref = bf16[8,512,640]{2,1,0:T(8,128)(2,1)} custom-call(s32[9]{0:T(128)} %pad_add_fusion.s, bf16[512,5120]{1,0:T(8,128)(2,1)} %bitcast.13, f32[1,5120]{1,0:T(1,128)} %bitcast.15), custom_call_target="tpu_custom_call" | custom-call | flops 15728640 | bytes 10485760 | tf_op jit(solution)/shard_map/norm/pallas_call | solution.py:82
  26.3 4.9 %collective-permute-done.7.refs_8_ = bf16[640,256]{1,0:T(8,128)(2,1)} collective-permute-done((bf16[640,256]{1,0:T(8,128)(2,1)}, bf16[640,256]{1,0:T(8,128)(2,1)}, u32[]{:S(2)}, u32[]{:S(2)}) %collective-permute-start.7) | collective-permute-done | bytes 327712 | tf_op jit(solution)/shard_map/ppermute | solution.py:499
  36.6 6.5 %collective-permute-done.9.refs_3_ = bf16[640,256]{1,0:T(8,128)(2,1)S(1)} collective-permute-done((bf16[640,256]{1,0:T(8,128)(2,1)S(1)}, bf16[640,256]{1,0:T(8,128)(2,1)S(1)}, u32[]{:S(2)}, u32[]{:S(2)}) %collective-permute-start.9) | collective-permute-done | bytes 327712 | tf_op jit(solution)/shard_map/ppermute | solution.py:499
  45.1 5.0 %collective-permute-done.13.refs_10_ = bf16[640,256]{1,0:T(8,128)(2,1)S(1)} collective-permute-done((bf16[640,256]{1,0:T(8,128)(2,1)}, bf16[640,256]{1,0:T(8,128)(2,1)S(1)}, u32[]{:S(2)}, u32[]{:S(2)}) %collective-permute-start.13) | collective-permute-done | bytes 327712 | tf_op jit(solution)/shard_map/ppermute | solution.py:499
  52.1 4.9 %collective-permute-done.11.refs_5_ = bf16[640,256]{1,0:T(8,128)(2,1)S(1)} collective-permute-done((bf16[640,256]{1,0:T(8,128)(2,1)S(1)}, bf16[640,256]{1,0:T(8,128)(2,1)S(1)}, u32[]{:S(2)}, u32[]{:S(2)}) %collective-permute-start.11) | collective-permute-done | bytes 327712 | tf_op jit(solution)/shard_map/ppermute | solution.py:499
  59.2 4.8 %collective-permute-done.15.refs_12_ = bf16[640,256]{1,0:T(8,128)(2,1)S(1)} collective-permute-done((bf16[640,256]{1,0:T(8,128)(2,1)S(1)}, bf16[640,256]{1,0:T(8,128)(2,1)S(1)}, u32[]{:S(2)}, u32[]{:S(2)}) %collective-permute-start.15) | collective-permute-done | bytes 327712 | tf_op jit(solution)/shard_map/ppermute | solution.py:499
  66.5 3.8 %start_deltas.1 = (f32[256,640]{1,0:T(8,128)}, f32[256,640]{1,0:T(8,128)}) custom-call(s32[9]{0:T(128)} %pad_add_fusion.s, f32[320,1024]{1,0:T(8,128)} %k_ref.3, f32[320,1024]{1,0:T(8,128)} %copy-done.2, bf16[640,256]{1,0:T(8,128)(2,1)} %get-tuple-element.51.refs_0_, bf16[640,256]{1,0:T(8,128)(2,1)} %get-tuple-element.52.refs_1_.refs_7_), custom_call_target="tpu_custom_call" | custom-call | bytes 4587520 | tf_op jit(solution)/shard_map/start_deltas/pallas_call | solution.py:140
  72.2 26.3 %group_step.1 = (bf16[7,256,640]{2,1,0:T(8,128)(2,1)}, bf16[7,256,640]{2,1,0:T(8,128)(2,1)}, bf16[128,640]{1,0:T(8,128)(2,1)}, bf16[128,640]{1,0:T(8,128)(2,1)},...) custom-call(s32[9]{0:T(128)} %pad_add_fusion.s, bf16[8,512,640]{2,1,0:T(8,128)(2,1)} %norm.1.a_ref, ...), custom_call_target="tpu_custom_call" | custom-call | flops 16106127360 | bytes 31457280 | tf_op jit(solution)/shard_map/group_step/pallas_call | solution.py:266
  102.5 3.0 %collective-permute-done.32.ui_ref = bf16[128,640]{1,0:T(8,128)(2,1)S(1)} collective-permute-done((bf16[128,640]{1,0:T(8,128)(2,1)}, bf16[128,640]{1,0:T(8,128)(2,1)S(1)}, u32[]{:S(2)}, u32[]{:S(2)}) %collective-permute-start.32) | collective-permute-done | bytes 163872 | tf_op jit(solution)/shard_map/ppermute | solution.py:517
  106.4 2.7 %add_0_3.1 = (bf16[256,640]{1,0:T(8,128)(2,1)}, bf16[256,640]{1,0:T(8,128)(2,1)}) custom-call(s32[9]{0:T(128)} %pad_add_fusion.s, bf16[7,256,640]{2,1,0:T(8,128)(2,1)} %get-tuple-element.75.ou_ref.od_ref.g_ref, bf16[7,256,640]{2,1,0:T(8,128)(2,1)} %get-tuple-element.75.ou_ref.od_ref.g_ref, bf16[128,640]{1,0:T(8,128)(2,1)} %copy-done.22, ...), custom_call_target="tpu_custom_call" | custom-call | bytes 1966080 | tf_op jit(solution)/shard_map/add_0_3/pallas_call | solution.py:309
  111.9 2.7 %add_1_3.1 = (bf16[256,640]{1,0:T(8,128)(2,1)}, bf16[256,640]{1,0:T(8,128)(2,1)}) custom-call(s32[9]{0:T(128)} %pad_add_fusion.s, bf16[7,256,640]{2,1,0:T(8,128)(2,1)} %get-tuple-element.61.ou_ref.od_ref.g_ref, bf16[7,256,640]{2,1,0:T(8,128)(2,1)} %get-tuple-element.61.ou_ref.od_ref.g_ref, bf16[128,640]{1,0:T(8,128)(2,1)} %copy-done.20, ...), custom_call_target="tpu_custom_call" | custom-call | bytes 1966080 | tf_op jit(solution)/shard_map/add_1_3/pallas_call | solution.py:309
  116.7 2.9 %collective-permute-done.34.ui_ref = bf16[256,640]{1,0:T(8,128)(2,1)S(1)} collective-permute-done((bf16[256,640]{1,0:T(8,128)(2,1)}, bf16[256,640]{1,0:T(8,128)(2,1)S(1)}, u32[]{:S(2)}, u32[]{:S(2)}) %collective-permute-start.34) | collective-permute-done | bytes 327712 | tf_op jit(solution)/shard_map/ppermute | solution.py:517
  121.2 2.8 %add_0_2.1 = (bf16[256,640]{1,0:T(8,128)(2,1)}, bf16[256,640]{1,0:T(8,128)(2,1)}) custom-call(s32[9]{0:T(128)} %pad_add_fusion.s, bf16[7,256,640]{2,1,0:T(8,128)(2,1)} %get-tuple-element.75.ou_ref.od_ref.g_ref, bf16[7,256,640]{2,1,0:T(8,128)(2,1)} %get-tuple-element.75.ou_ref.od_ref.g_ref, bf16[256,640]{1,0:T(8,128)(2,1)} %copy-done.7, ...), custom_call_target="tpu_custom_call" | custom-call | bytes 1966080 | tf_op jit(solution)/shard_map/add_0_2/pallas_call | solution.py:309
  128.3 2.8 %add_1_2.1 = (bf16[256,640]{1,0:T(8,128)(2,1)}, bf16[256,640]{1,0:T(8,128)(2,1)}) custom-call(s32[9]{0:T(128)} %pad_add_fusion.s, bf16[7,256,640]{2,1,0:T(8,128)(2,1)} %get-tuple-element.61.ou_ref.od_ref.g_ref, bf16[7,256,640]{2,1,0:T(8,128)(2,1)} %get-tuple-element.61.ou_ref.od_ref.g_ref, bf16[256,640]{1,0:T(8,128)(2,1)} %copy-done.8, ...), custom_call_target="tpu_custom_call" | custom-call | bytes 1966080 | tf_op jit(solution)/shard_map/add_1_2/pallas_call | solution.py:309
  137.0 2.8 %add_0_1.1 = (bf16[256,640]{1,0:T(8,128)(2,1)}, bf16[256,640]{1,0:T(8,128)(2,1)}) custom-call(s32[9]{0:T(128)} %pad_add_fusion.s, bf16[7,256,640]{2,1,0:T(8,128)(2,1)} %get-tuple-element.75.ou_ref.od_ref.g_ref, bf16[7,256,640]{2,1,0:T(8,128)(2,1)} %get-tuple-element.75.ou_ref.od_ref.g_ref, bf16[256,640]{1,0:T(8,128)(2,1)} %copy-done.9, ...), custom_call_target="tpu_custom_call" | custom-call | bytes 1966080 | tf_op jit(solution)/shard_map/add_0_1/pallas_call | solution.py:309
  143.8 2.8 %add_1_1.1 = (bf16[256,640]{1,0:T(8,128)(2,1)}, bf16[256,640]{1,0:T(8,128)(2,1)}) custom-call(s32[9]{0:T(128)} %pad_add_fusion.s, bf16[7,256,640]{2,1,0:T(8,128)(2,1)} %get-tuple-element.61.ou_ref.od_ref.g_ref, bf16[7,256,640]{2,1,0:T(8,128)(2,1)} %get-tuple-element.61.ou_ref.od_ref.g_ref, bf16[256,640]{1,0:T(8,128)(2,1)} %copy-done.10, ...), custom_call_target="tpu_custom_call" | custom-call | bytes 1966080 | tf_op jit(solution)/shard_map/add_1_1/pallas_call | solution.py:309
  151.2 3.4 %code_0.1 = (bf16[272,640]{1,0:T(8,128)(2,1)}, bf16[272,640]{1,0:T(8,128)(2,1)}, bf16[144,640]{1,0:T(8,128)(2,1)}, bf16[144,640]{1,0:T(8,128)(2,1)}) custom-call(s32[9]{0:T(128)} %pad_add_fusion.s, bf16[7,256,640]{2,1,0:T(8,128)(2,1)} %get-tuple-element.75.ou_ref.od_ref.g_ref, bf16[256,640]{1,0:T(8,128)(2,1)} %copy-done.5, bf16[256,640]{1,0:T(8,128)(2,1)} %copy-done.11, ...), custom_call_target="tpu_custom_call" | custom-call | bytes 2621440 | tf_op jit(solution)/shard_map/code_0/pallas_call | solution.py:363
  157.5 3.4 %code_1.1 = (bf16[272,640]{1,0:T(8,128)(2,1)}, bf16[272,640]{1,0:T(8,128)(2,1)}, bf16[144,640]{1,0:T(8,128)(2,1)}, bf16[144,640]{1,0:T(8,128)(2,1)}) custom-call(s32[9]{0:T(128)} %pad_add_fusion.s, bf16[7,256,640]{2,1,0:T(8,128)(2,1)} %get-tuple-element.61.ou_ref.od_ref.g_ref, bf16[256,640]{1,0:T(8,128)(2,1)} %copy-done.4, bf16[256,640]{1,0:T(8,128)(2,1)} %copy-done.6, ...), custom_call_target="tpu_custom_call" | custom-call | bytes 2621440 | tf_op jit(solution)/shard_map/code_1/pallas_call | solution.py:363
  163.4 4.7 %collective-permute-done.42.refs_4_ = bf16[144,640]{1,0:T(8,128)(2,1)S(1)} collective-permute-done((bf16[144,640]{1,0:T(8,128)(2,1)S(1)}, bf16[144,640]{1,0:T(8,128)(2,1)S(1)}, u32[]{:S(2)}, u32[]{:S(2)}) %collective-permute-start.42) | collective-permute-done | bytes 184352 | tf_op jit(solution)/shard_map/ppermute | solution.py:478
  168.9 4.6 %finish_0.1 = (bf16[320,1024]{1,0:T(8,128)(2,1)}, f32[320,1024]{1,0:T(8,128)}, f32[320,1024]{1,0:T(8,128)}) custom-call(s32[9]{0:T(128)} %pad_add_fusion.s, bf16[320,1024]{1,0:T(8,128)(2,1)} %bitcast.11, f32[320,1024]{1,0:T(8,128)} %k_ref.3, f32[320,1024]{1,0:T(8,128)} %m_ref.3, bf16[272,640]{1,0:T(8,128)(2,1)} %get-tuple-element.85.refs_0_.refs_2_, ...), custom_call_target="tpu_custom_call" | custom-call | bytes 3932160 | tf_op jit(solution)/shard_map/finish_0/pallas_call | solution.py:431
  176.8 4.6 %finish_1.1 = (bf16[320,1024]{1,0:T(8,128)(2,1)}, f32[320,1024]{1,0:T(8,128)}, f32[320,1024]{1,0:T(8,128)}) custom-call(s32[9]{0:T(128)} %pad_add_fusion.s, bf16[320,1024]{1,0:T(8,128)(2,1)} %bitcast.12, f32[320,1024]{1,0:T(8,128)} %k_ref.3, f32[320,1024]{1,0:T(8,128)} %m_ref.3, ...), custom_call_target="tpu_custom_call", output_to_operand_aliasing={{0}: (10, {}), {1}: (11, {}), {2}: (12, {})} | custom-call | bytes 3932160 | tf_op jit(solution)/shard_map/finish_1/pallas_call | solution.py:431
  (152 shorter events, 62.5 us)
Async XLA Ops:
  0.6 11.8 %collective-permute-start.2 = (bf16[2,256,2560]{2,1,0:T(8,128)(2,1)}, bf16[2,256,2560]{2,1,0:T(8,128)(2,1)}, u32[]{:S(2)}, u32[]{:S(2)}) collective-permute-start(bf16[2,256,2560]{2,1,0:T(8,128)(2,1)} %bitcast.16), channel_id=1, source_target_pairs={{0,1},{1,0},{2,3},{3,2},{4,5},{5,4},{6,7},{7,6},{8,9},{9,8},{10,11... | collective-permute-start | bytes 7864328 | tf_op jit(solution)/shard_map/ppermute | solution.py:489
  1.1 11.3 %collective-permute-start.1 = (f32[320,1024]{1,0:T(8,128)}, f32[320,1024]{1,0:T(8,128)S(1)}, u32[]{:S(2)}, u32[]{:S(2)}) collective-permute-start(f32[320,1024]{1,0:T(8,128)} %k_ref.3), channel_id=1, source_target_pairs={{0,1},{1,0},{2,3},{3,2},{4,5},{5,4},{6,7},{7,6},{8,9},{9,8},{10,11... | collective-permute-start | bytes 3932168 | tf_op jit(solution)/shard_map/ppermute | solution.py:489
  12.4 20.1 %collective-permute-start.3 = (bf16[2,256,2560]{2,1,0:T(8,128)(2,1)}, bf16[2,256,2560]{2,1,0:T(8,128)(2,1)}, u32[]{:S(2)}, u32[]{:S(2)}) collective-permute-start(bf16[2,256,2560]{2,1,0:T(8,128)(2,1)} %bitcast.18), channel_id=1, source_target_pairs={{0,1},{1,0},{2,3},{3,2},{4,5},{5,4},{6,7},{7,6},{8,9},{9,8},{10,11... | collective-permute-start | bytes 7864328 | tf_op jit(solution)/shard_map/ppermute | solution.py:490
  12.8 12.1 %collective-permute-start.6 = (bf16[640,256]{1,0:T(8,128)(2,1)}, bf16[640,256]{1,0:T(8,128)(2,1)S(1)}, u32[]{:S(2)}, u32[]{:S(2)}) collective-permute-start(bf16[640,256]{1,0:T(8,128)(2,1)} %get-tuple-element.51.refs_0_), channel_id=1, source_target_pairs={{0,2},{1,3},{2,6},{3,7},{4,0},{5,1},{6,10},{7,11},{8,4},{9,5},{10,... | collective-permute-start | bytes 983048 | tf_op jit(solution)/shard_map/ppermute | solution.py:499
  15.5 10.8 %collective-permute-start.4 = (bf16[640,256]{1,0:T(8,128)(2,1)}, bf16[640,256]{1,0:T(8,128)(2,1)S(1)}, u32[]{:S(2)}, u32[]{:S(2)}) collective-permute-start(bf16[640,256]{1,0:T(8,128)(2,1)} %get-tuple-element.51.refs_0_), channel_id=1, source_target_pairs={{0,4},{1,5},{2,0},{3,1},{4,8},{5,9},{6,2},{7,3},{8,12},{9,13},{10,... | collective-permute-start | bytes 983048 | tf_op jit(solution)/shard_map/ppermute | solution.py:499
  15.6 15.6 %collective-permute-start.7 = (bf16[640,256]{1,0:T(8,128)(2,1)}, bf16[640,256]{1,0:T(8,128)(2,1)}, u32[]{:S(2)}, u32[]{:S(2)}) collective-permute-start(bf16[640,256]{1,0:T(8,128)(2,1)} %get-tuple-element.52.refs_1_.refs_7_), channel_id=1, source_target_pairs={{0,2},{1,3},{2,6},{3,7},{4,0},{5,1},{6,10},{7,11},{8,4},{9,5},{10,... | collective-permute-start | bytes 983048 | tf_op jit(solution)/shard_map/ppermute | solution.py:499
  17.5 15.0 %collective-permute-start.5 = (bf16[640,256]{1,0:T(8,128)(2,1)}, bf16[640,256]{1,0:T(8,128)(2,1)}, u32[]{:S(2)}, u32[]{:S(2)}) collective-permute-start(bf16[640,256]{1,0:T(8,128)(2,1)} %get-tuple-element.52.refs_1_.refs_7_), channel_id=1, source_target_pairs={{0,4},{1,5},{2,0},{3,1},{4,8},{5,9},{6,2},{7,3},{8,12},{9,13},{10,... | collective-permute-start | bytes 983048 | tf_op jit(solution)/shard_map/ppermute | solution.py:499
  32.5 39.6 %collective-permute-start.8 = (bf16[8,512,640]{2,1,0:T(8,128)(2,1)}, bf16[8,512,640]{2,1,0:T(8,128)(2,1)}, u32[]{:S(2)}, u32[]{:S(2)}) collective-permute-start(bf16[8,512,640]{2,1,0:T(8,128)(2,1)} %norm.1.a_ref), channel_id=1, source_target_pairs={{0,1},{1,0},{2,3},{3,2},{4,5},{5,4},{6,7},{7,6},{8,9},{9,8},{10,11... | collective-permute-start | bytes 15728648 | tf_op jit(solution)/shard_map/ppermute | solution.py:504
  34.6 15.5 %collective-permute-start.13 = (bf16[640,256]{1,0:T(8,128)(2,1)}, bf16[640,256]{1,0:T(8,128)(2,1)S(1)}, u32[]{:S(2)}, u32[]{:S(2)}) collective-permute-start(bf16[640,256]{1,0:T(8,128)(2,1)} %collective-permute-done.7.refs_8_), channel_id=1, source_target_pairs={{0,2},{1,3},{2,6},{3,7},{4,0},{5,1},{6,10},{7,11},{8,4},{9,5},{10,... | collective-permute-start | bytes 983048 | tf_op jit(solution)/shard_map/ppermute | solution.py:499
  36.1 15.5 %collective-permute-start.14 = (bf16[640,256]{1,0:T(8,128)(2,1)}, bf16[640,256]{1,0:T(8,128)(2,1)S(1)}, u32[]{:S(2)}, u32[]{:S(2)}) collective-permute-start(bf16[640,256]{1,0:T(8,128)(2,1)} %collective-permute-done.5.refs_9_), channel_id=1, source_target_pairs={{0,4},{1,5},{2,0},{3,1},{4,8},{5,9},{6,2},{7,3},{8,12},{9,13},{10,... | collective-permute-start | bytes 983048 | tf_op jit(solution)/shard_map/ppermute | solution.py:499
  43.0 14.0 %collective-permute-start.11 = (bf16[640,256]{1,0:T(8,128)(2,1)S(1)}, bf16[640,256]{1,0:T(8,128)(2,1)S(1)}, u32[]{:S(2)}, u32[]{:S(2)}) collective-permute-start(bf16[640,256]{1,0:T(8,128)(2,1)S(1)} %collective-permute-done.9.refs_3_), channel_id=1, source_target_pairs={{0,2},{1,3},{2,6},{3,7},{4,0},{5,1},{6,10},{7,11},{8,4},{9,5},{10,... | collective-permute-start | bytes 983048 | tf_op jit(solution)/shard_map/ppermute | solution.py:499
  44.6 14.1 %collective-permute-start.12 = (bf16[640,256]{1,0:T(8,128)(2,1)S(1)}, bf16[640,256]{1,0:T(8,128)(2,1)S(1)}, u32[]{:S(2)}, u32[]{:S(2)}) collective-permute-start(bf16[640,256]{1,0:T(8,128)(2,1)S(1)} %collective-permute-done.10.refs_4_), channel_id=1, source_target_pairs={{0,4},{1,5},{2,0},{3,1},{4,8},{5,9},{6,2},{7,3},{8,12},{9,13},{10,... | collective-permute-start | bytes 983048 | tf_op jit(solution)/shard_map/ppermute | solution.py:499
  50.1 14.0 %collective-permute-start.15 = (bf16[640,256]{1,0:T(8,128)(2,1)S(1)}, bf16[640,256]{1,0:T(8,128)(2,1)S(1)}, u32[]{:S(2)}, u32[]{:S(2)}) collective-permute-start(bf16[640,256]{1,0:T(8,128)(2,1)S(1)} %collective-permute-done.13.refs_10_), channel_id=1, source_target_pairs={{0,2},{1,3},{2,6},{3,7},{4,0},{5,1},{6,10},{7,11},{8,4},{9,5},{10,... | collective-permute-start | bytes 983048 | tf_op jit(solution)/shard_map/ppermute | solution.py:499
  51.7 14.1 %collective-permute-start.16 = (bf16[640,256]{1,0:T(8,128)(2,1)S(1)}, bf16[640,256]{1,0:T(8,128)(2,1)S(1)}, u32[]{:S(2)}, u32[]{:S(2)}) collective-permute-start(bf16[640,256]{1,0:T(8,128)(2,1)S(1)} %collective-permute-done.14.refs_11_), channel_id=1, source_target_pairs={{0,4},{1,5},{2,0},{3,1},{4,8},{5,9},{6,2},{7,3},{8,12},{9,13},{10,... | collective-permute-start | bytes 983048 | tf_op jit(solution)/shard_map/ppermute | solution.py:499
  57.1 13.2 %collective-permute-start.18 = (bf16[320,256]{1,0:T(8,128)(2,1)S(1)}, bf16[320,256]{1,0:T(8,128)(2,1)}, u32[]{:S(2)}, u32[]{:S(2)}) collective-permute-start(bf16[320,256]{1,0:T(8,128)(2,1)S(1)} %slice.17), channel_id=1, source_target_pairs={{0,2},{1,3},{2,6},{3,7},{4,0},{5,1},{6,10},{7,11},{8,4},{9,5},{10,... | collective-permute-start | bytes 491528 | tf_op jit(solution)/shard_map/ppermute | solution.py:502
  58.7 11.6 %collective-permute-start.17 = (bf16[320,256]{1,0:T(8,128)(2,1)S(1)}, bf16[320,256]{1,0:T(8,128)(2,1)}, u32[]{:S(2)}, u32[]{:S(2)}) collective-permute-start(bf16[320,256]{1,0:T(8,128)(2,1)S(1)} %slice.16), channel_id=1, source_target_pairs={{0,4},{1,5},{2,0},{3,1},{4,8},{5,9},{6,2},{7,3},{8,12},{9,13},{10,... | collective-permute-start | bytes 491528 | tf_op jit(solution)/shard_map/ppermute | solution.py:502
  114.7 12.0 %collective-permute-start.23 = (bf16[256,640]{1,0:T(8,128)(2,1)}, bf16[256,640]{1,0:T(8,128)(2,1)S(1)}, u32[]{:S(2)}, u32[]{:S(2)}) collective-permute-start(bf16[256,640]{1,0:T(8,128)(2,1)} %get-tuple-element.64), channel_id=1, source_target_pairs={{0,4},{1,5},{2,0},{3,1},{4,8},{5,9},{6,2},{7,3},{8,12},{9,13},{10,... | collective-permute-start | bytes 983048 | tf_op jit(solution)/shard_map/ppermute | solution.py:517
  115.6 11.9 %collective-permute-start.24 = (bf16[256,640]{1,0:T(8,128)(2,1)}, bf16[256,640]{1,0:T(8,128)(2,1)S(1)}, u32[]{:S(2)}, u32[]{:S(2)}) collective-permute-start(bf16[256,640]{1,0:T(8,128)(2,1)} %get-tuple-element.65), channel_id=1, source_target_pairs={{0,2},{1,3},{2,6},{3,7},{4,0},{5,1},{6,10},{7,11},{8,4},{9,5},{10,... | collective-permute-start | bytes 983048 | tf_op jit(solution)/shard_map/ppermute | solution.py:517
  124.1 10.8 %collective-permute-start.36 = (bf16[256,640]{1,0:T(8,128)(2,1)}, bf16[256,640]{1,0:T(8,128)(2,1)S(1)}, u32[]{:S(2)}, u32[]{:S(2)}) collective-permute-start(bf16[256,640]{1,0:T(8,128)(2,1)} %get-tuple-element.80), channel_id=1, source_target_pairs={{0,4},{1,5},{2,0},{3,1},{4,8},{5,9},{6,2},{7,3},{8,12},{9,13},{10,... | collective-permute-start | bytes 983048 | tf_op jit(solution)/shard_map/ppermute | solution.py:517
  131.1 10.8 %collective-permute-start.25 = (bf16[256,640]{1,0:T(8,128)(2,1)}, bf16[256,640]{1,0:T(8,128)(2,1)S(1)}, u32[]{:S(2)}, u32[]{:S(2)}) collective-permute-start(bf16[256,640]{1,0:T(8,128)(2,1)} %get-tuple-element.66), channel_id=1, source_target_pairs={{0,4},{1,5},{2,0},{3,1},{4,8},{5,9},{6,2},{7,3},{8,12},{9,13},{10,... | collective-permute-start | bytes 983048 | tf_op jit(solution)/shard_map/ppermute | solution.py:517
  156.1 12.1 %collective-permute-start.41 = (bf16[272,640]{1,0:T(8,128)(2,1)}, bf16[272,640]{1,0:T(8,128)(2,1)S(1)}, u32[]{:S(2)}, u32[]{:S(2)}) collective-permute-start(bf16[272,640]{1,0:T(8,128)(2,1)} %get-tuple-element.87), channel_id=1, source_target_pairs={{0,1},{1,0},{2,3},{3,2},{4,5},{5,4},{6,7},{7,6},{8,9},{9,8},{10,11... | collective-permute-start | bytes 1044488 | tf_op jit(solution)/shard_map/ppermute | solution.py:522
  160.9 15.1 %collective-permute-start.30 = (bf16[272,640]{1,0:T(8,128)(2,1)}, bf16[272,640]{1,0:T(8,128)(2,1)S(1)}, u32[]{:S(2)}, u32[]{:S(2)}) collective-permute-start(bf16[272,640]{1,0:T(8,128)(2,1)} %get-tuple-element.73), channel_id=1, source_target_pairs={{0,1},{1,0},{2,3},{3,2},{4,5},{5,4},{6,7},{7,6},{8,9},{9,8},{10,11... | collective-permute-start | bytes 1044488 | tf_op jit(solution)/shard_map/ppermute | solution.py:522
  161.6 11.9 %collective-permute-start.29 = (bf16[144,640]{1,0:T(8,128)(2,1)}, bf16[144,640]{1,0:T(8,128)(2,1)S(1)}, u32[]{:S(2)}, u32[]{:S(2)}) collective-permute-start(bf16[144,640]{1,0:T(8,128)(2,1)} %get-tuple-element.72), channel_id=1, source_target_pairs={{0,16},{1,17},{2,18},{3,19},{4,20},{5,21},{6,22},{7,23},{8,24},{9,... | collective-permute-start | bytes 552968 | tf_op jit(solution)/shard_map/ppermute | solution.py:478
  163.1 12.9 %collective-permute-start.31 = (bf16[144,640]{1,0:T(8,128)(2,1)}, bf16[144,640]{1,0:T(8,128)(2,1)S(1)}, u32[]{:S(2)}, u32[]{:S(2)}) collective-permute-start(bf16[144,640]{1,0:T(8,128)(2,1)} %get-tuple-element.74), channel_id=1, source_target_pairs={{0,17},{1,16},{2,19},{3,18},{4,21},{5,20},{6,23},{7,22},{8,25},{9,... | collective-permute-start | bytes 552968 | tf_op jit(solution)/shard_map/ppermute | solution.py:478
  (54 other events, 352.9 us)

commit v4 on v3

--- a/solution.py
+++ b/solution.py
@@ -19,7 +19,7 @@
 
 F32 = jnp.float32
 BF16 = jnp.bfloat16
-VMEM_LIMIT = 62 * 1024 * 1024
+VMEM_LIMIT = 64 * 1024 * 1024 - 65536
 SCALE_ROWS = 16
 
 
@@ -187,13 +187,16 @@
             (gb_ref.at[:, :, mine], g_held.at[pl.ds(seqs, seqs)]),
         )
         query_waits = [pltpu.make_async_copy(x, y, q_sems.at[k]) for k, (x, y) in enumerate(pairs)]
-        for wait in waits:
-            for copy in wait:
+        ahead = 3
+        waits.append(query_waits)
+        for k in range(ahead):
+            for copy in waits[k]:
                 copy.start()
-        for copy in query_waits:
-            copy.start()
 
         for k in range(chips):
+            if k + ahead <= chips:
+                for copy in waits[k + ahead]:
+                    copy.start()
             for copy in waits[k]:
                 copy.wait()
             for h in range(heads):
@@ -483,10 +486,12 @@
     seqs, length, width = hidden.shape[1:]
     part = 2 * rows
 
-    own = own_blocks(scalars, weight, swap(weight), heads)
+    received = swap(weight)
+    own = own_blocks(scalars, weight, received, heads)
 
     tied = lax.optimization_barrier
-    own, outer_other, queries_other = tied((own, swap(kv_outer), swap(queries[0])))
+    own, outer_other = tied((own, swap(kv_outer)))
+    queries_other = swap(tied((queries[0], received))[0])
     out_grad_other = swap(tied((out_grad[0], own))[0])
     rows_mine = norm_rows(scalars, tied((hidden, own))[0].reshape(seqs * length, width), norm_gain, chips)
 
@@ -501,7 +506,7 @@
             else:
                 halves[h] = (up(ups[h][: part // 2]), down(downs[h][part // 2 :]))
         if step == 1:
-            rows_other = swap(tied((rows_mine, out_grad_other, ups, downs))[0])
+            rows_other = swap(tied((rows_mine, queries_other, out_grad_other, ups, downs))[0])
     deltas = start_deltas(scalars, own, kv_outer, outer_other, heads)
 
     rows_mine, deltas = lax.optimization_barrier((rows_mine, deltas))

time: 182 us -> 177 us (0.973)
  waiting for transfers between devices: 58 us -> 53.7 us
  local copies, waits for them, and re-layouts: 9.74 us -> 6.4 us
  starting transfers between devices: 39 us -> 41.8 us
    unnamed x70 -> x16, local copies, waits for them, and re-layouts: 9 us -> 3 us
    ppermute x8, waiting for transfers between devices: 5.8 us -> 9.6 us  [local(): down(going_down)]
    ppermute x8, starting transfers between devices: 9.09 us -> 12.5 us  [local(): up(going_up)]
    ppermute x12, waiting for transfers between devices: 28.9 us -> 25.7 us  [local(): ups[h], downs[h] = (up(ups[h]), down(downs[h]))]
    ppermute x4, waiting for transfers between devices: 5.64 us -> 2.52 us  [the longest x1 2.51 us: local(): received = swap(weight)]
    ppermute x8, starting transfers between devices: 7.17 us -> 4.29 us  [local(): down(going_down)]
    slice x4, local copies, waits for them, and re-layouts: 0.05 us -> 2.7 us  [local(): halves[h] = (up(ups[h][:part // 2]), down(downs[h][part // 2:]))]
    ppermute x12, starting transfers between devices: 12.9 us -> 15.1 us  [local(): ups[h], downs[h] = (up(ups[h]), down(downs[h]))]
  transfers between devices with their start and end apart: 43 -> 43, of which waited for: 23 -> 22; matrix products, arithmetic and copies ran while one was open for 1% -> 2% of each run, Pallas kernels for 23% -> 24%
where the time goes in v4:
time: 177 us; the launch traced here: 176 us
  Pallas kernels  72.8 us (41%)
  waiting for transfers between devices  53.7 us (30%)
  starting transfers between devices  41.8 us (24%)
  local copies, waits for them, and re-layouts  6.4 us (4%)
    pallas_call x1, Pallas kernels, group_step(): call(body, [jax.ShapeDtypeStruct((last, wide, part), BF16)] * heads + [ja...  26 us
    ppermute x12, waiting for transfers between devices, local(): ups[h], downs[h] = (up(ups[h]), down(downs[h]))  25.7 us
    pallas_call x6, Pallas kernels, add_partials(): call(body, [shape] * 2, [pl.BlockSpec((1, HD, part), lambda i, s: (at, i,...  16.8 us
    ppermute x12, starting transfers between devices, local(): ups[h], downs[h] = (up(ups[h]), down(downs[h]))  15.1 us
    ppermute x8, starting transfers between devices, local(): up(going_up)  12.5 us
    ppermute x8, waiting for transfers between devices, local(): down(going_down)  9.6 us
    pallas_call x2, Pallas kernels, finish(): call(body, [jax.ShapeDtypeStruct((rows, cols), BF16), jax.ShapeDtypeStruc...  9.2 us
    ppermute x8, waiting for transfers between devices, local(): up(going_up)  8.25 us
  transfers between devices with their start and end apart: 43, of which 22 were waited for; matrix products, arithmetic and copies ran while one was open for 2% of the time, Pallas kernels for 24%

profile of v4, /device:TPU:0, one launch (start us, length us, event | category | flops | bytes accessed | tf_op | source)
XLA Modules:
  0.0 176.4 jit_solution(1306926854789287484)
XLA Ops:
  2.6 2.5 %collective-permute-done.r_ref = bf16[320,1024]{1,0:T(8,128)(2,1)} collective-permute-done((bf16[320,1024]{1,0:T(8,128)(2,1)}, bf16[320,1024]{1,0:T(8,128)(2,1)}, u32[]{:S(2)}, u32[]{:S(2)}) %collective-permute-start) | collective-permute-done | bytes 655392 | tf_op jit(solution)/shard_map/ppermute | solution.py:489
  5.5 3.0 %own_blocks.1 = (bf16[640,256]{1,0:T(8,128)(2,1)}, bf16[640,256]{1,0:T(8,128)(2,1)}) custom-call(s32[9]{0:T(128)} %pad_add_fusion.s, bf16[320,1024]{1,0:T(8,128)(2,1)} %bitcast.10, bf16[320,1024]{1,0:T(8,128)(2,1)} %collective-permute-done.r_ref), custom_call_target="tpu_custom_call" | custom-call | bytes 1966080 | tf_op jit(solution)/shard_map/own_blocks/pallas_call | solution.py:113
  8.6 2.9 %collective-permute-start.6 = (bf16[640,256]{1,0:T(8,128)(2,1)}, bf16[640,256]{1,0:T(8,128)(2,1)}, u32[]{:S(2)}, u32[]{:S(2)}) collective-permute-start(bf16[640,256]{1,0:T(8,128)(2,1)} %get-tuple-element.51.refs_0_), channel_id=1, source_target_pairs={{0,2},{1,3},{2,6},{3,7},{4,0},{5,1},{6,10},{7,11},{8,4},{9,5},{10,... | collective-permute-start | bytes 983048 | tf_op jit(solution)/shard_map/ppermute | solution.py:504
  13.4 6.9 %collective-permute-done.6.refs_1_ = bf16[640,256]{1,0:T(8,128)(2,1)} collective-permute-done((bf16[640,256]{1,0:T(8,128)(2,1)}, bf16[640,256]{1,0:T(8,128)(2,1)}, u32[]{:S(2)}, u32[]{:S(2)}) %collective-permute-start.6) | collective-permute-done | bytes 327712 | tf_op jit(solution)/shard_map/ppermute | solution.py:504
  22.4 7.3 %norm.1.a_ref = bf16[8,512,640]{2,1,0:T(8,128)(2,1)} custom-call(s32[9]{0:T(128)} %pad_add_fusion.s, bf16[512,5120]{1,0:T(8,128)(2,1)} %bitcast.13, f32[1,5120]{1,0:T(1,128)} %bitcast.15), custom_call_target="tpu_custom_call" | custom-call | flops 15728640 | bytes 10485760 | tf_op jit(solution)/shard_map/norm/pallas_call | solution.py:82
  33.9 6.7 %collective-permute-done.9.refs_3_ = bf16[640,256]{1,0:T(8,128)(2,1)S(1)} collective-permute-done((bf16[640,256]{1,0:T(8,128)(2,1)}, bf16[640,256]{1,0:T(8,128)(2,1)S(1)}, u32[]{:S(2)}, u32[]{:S(2)}) %collective-permute-start.9) | collective-permute-done | bytes 327712 | tf_op jit(solution)/shard_map/ppermute | solution.py:504
  42.6 4.9 %collective-permute-done.13.refs_10_ = bf16[640,256]{1,0:T(8,128)(2,1)S(1)} collective-permute-done((bf16[640,256]{1,0:T(8,128)(2,1)}, bf16[640,256]{1,0:T(8,128)(2,1)S(1)}, u32[]{:S(2)}, u32[]{:S(2)}) %collective-permute-start.13) | collective-permute-done | bytes 327712 | tf_op jit(solution)/shard_map/ppermute | solution.py:504
  49.6 4.9 %collective-permute-done.11.refs_5_ = bf16[640,256]{1,0:T(8,128)(2,1)S(1)} collective-permute-done((bf16[640,256]{1,0:T(8,128)(2,1)S(1)}, bf16[640,256]{1,0:T(8,128)(2,1)S(1)}, u32[]{:S(2)}, u32[]{:S(2)}) %collective-permute-start.11) | collective-permute-done | bytes 327712 | tf_op jit(solution)/shard_map/ppermute | solution.py:504
  66.7 3.8 %start_deltas.1 = (f32[256,640]{1,0:T(8,128)}, f32[256,640]{1,0:T(8,128)}) custom-call(s32[9]{0:T(128)} %pad_add_fusion.s, f32[320,1024]{1,0:T(8,128)} %k_ref.3, f32[320,1024]{1,0:T(8,128)} %collective-permute-done.1.r_ref, bf16[640,256]{1,0:T(8,128)(2,1)} %get-tuple-element.51.refs_0_, bf16[640,256]{1,0:T(8,128)(2,1)} %get-tuple-element.52.refs_1_.refs_7_), custom_call_target="tpu_custom_call" | custom-call | bytes 4587520 | tf_op jit(solution)/shard_map/start_deltas/pallas_call | solution.py:140
  71.3 26.0 %group_step.1 = (bf16[7,256,640]{2,1,0:T(8,128)(2,1)}, bf16[7,256,640]{2,1,0:T(8,128)(2,1)}, bf16[128,640]{1,0:T(8,128)(2,1)}, bf16[128,640]{1,0:T(8,128)(2,1)},...) custom-call(s32[9]{0:T(128)} %pad_add_fusion.s, bf16[8,512,640]{2,1,0:T(8,128)(2,1)} %norm.1.a_ref, ...), custom_call_target="tpu_custom_call" | custom-call | flops 16106127360 | bytes 31457280 | tf_op jit(solution)/shard_map/group_step/pallas_call | solution.py:269
  104.8 2.8 %add_0_3.1 = (bf16[256,640]{1,0:T(8,128)(2,1)}, bf16[256,640]{1,0:T(8,128)(2,1)}) custom-call(s32[9]{0:T(128)} %pad_add_fusion.s, bf16[7,256,640]{2,1,0:T(8,128)(2,1)} %get-tuple-element.75.ou_ref.od_ref.g_ref, bf16[7,256,640]{2,1,0:T(8,128)(2,1)} %get-tuple-element.75.ou_ref.od_ref.g_ref, bf16[128,640]{1,0:T(8,128)(2,1)} %collective-permute-done.32.ui_ref, ...), custom_call_target="tpu_custom_call" | custom-call | bytes 1966080 | tf_op jit(solution)/shard_map/add_0_3/pallas_call | solution.py:312
  109.7 2.7 %add_1_3.1 = (bf16[256,640]{1,0:T(8,128)(2,1)}, bf16[256,640]{1,0:T(8,128)(2,1)}) custom-call(s32[9]{0:T(128)} %pad_add_fusion.s, bf16[7,256,640]{2,1,0:T(8,128)(2,1)} %get-tuple-element.61.ou_ref.od_ref.g_ref, bf16[7,256,640]{2,1,0:T(8,128)(2,1)} %get-tuple-element.61.ou_ref.od_ref.g_ref, bf16[128,640]{1,0:T(8,128)(2,1)} %collective-permute-done.21.ui_ref, ...), custom_call_target="tpu_custom_call" | custom-call | bytes 1966080 | tf_op jit(solution)/shard_map/add_1_3/pallas_call | solution.py:312
  114.4 4.1 %collective-permute-done.34.ui_ref = bf16[256,640]{1,0:T(8,128)(2,1)} collective-permute-done((bf16[256,640]{1,0:T(8,128)(2,1)}, bf16[256,640]{1,0:T(8,128)(2,1)}, u32[]{:S(2)}, u32[]{:S(2)}) %collective-permute-start.34) | collective-permute-done | bytes 327712 | tf_op jit(solution)/shard_map/ppermute | solution.py:522
  120.0 2.8 %add_0_2.1 = (bf16[256,640]{1,0:T(8,128)(2,1)}, bf16[256,640]{1,0:T(8,128)(2,1)}) custom-call(s32[9]{0:T(128)} %pad_add_fusion.s, bf16[7,256,640]{2,1,0:T(8,128)(2,1)} %get-tuple-element.75.ou_ref.od_ref.g_ref, bf16[7,256,640]{2,1,0:T(8,128)(2,1)} %get-tuple-element.75.ou_ref.od_ref.g_ref, bf16[256,640]{1,0:T(8,128)(2,1)} %collective-permute-done.34.ui_ref, ...), custom_call_target="tpu_custom_call" | custom-call | bytes 1966080 | tf_op jit(solution)/shard_map/add_0_2/pallas_call | solution.py:312
  126.9 2.8 %add_1_2.1 = (bf16[256,640]{1,0:T(8,128)(2,1)}, bf16[256,640]{1,0:T(8,128)(2,1)}) custom-call(s32[9]{0:T(128)} %pad_add_fusion.s, bf16[7,256,640]{2,1,0:T(8,128)(2,1)} %get-tuple-element.61.ou_ref.od_ref.g_ref, bf16[7,256,640]{2,1,0:T(8,128)(2,1)} %get-tuple-element.61.ou_ref.od_ref.g_ref, bf16[256,640]{1,0:T(8,128)(2,1)} %collective-permute-done.23.ui_ref, ...), custom_call_target="tpu_custom_call" | custom-call | bytes 1966080 | tf_op jit(solution)/shard_map/add_1_2/pallas_call | solution.py:312
  133.9 2.8 %add_0_1.1 = (bf16[256,640]{1,0:T(8,128)(2,1)}, bf16[256,640]{1,0:T(8,128)(2,1)}) custom-call(s32[9]{0:T(128)} %pad_add_fusion.s, bf16[7,256,640]{2,1,0:T(8,128)(2,1)} %get-tuple-element.75.ou_ref.od_ref.g_ref, bf16[7,256,640]{2,1,0:T(8,128)(2,1)} %get-tuple-element.75.ou_ref.od_ref.g_ref, bf16[256,640]{1,0:T(8,128)(2,1)} %collective-permute-done.36.ui_ref, ...), custom_call_target="tpu_custom_call" | custom-call | bytes 1966080 | tf_op jit(solution)/shard_map/add_0_1/pallas_call | solution.py:312
  136.8 2.5 %collective-permute-start.38 = (bf16[256,640]{1,0:T(8,128)(2,1)}, bf16[256,640]{1,0:T(8,128)(2,1)}, u32[]{:S(2)}, u32[]{:S(2)}) collective-permute-start(bf16[256,640]{1,0:T(8,128)(2,1)} %get-tuple-element.82), channel_id=1, source_target_pairs={{0,4},{1,5},{2,0},{3,1},{4,8},{5,9},{6,2},{7,3},{8,12},{9,13},{10,... | collective-permute-start | bytes 983048 | tf_op jit(solution)/shard_map/ppermute | solution.py:525
  141.9 2.8 %add_1_1.1 = (bf16[256,640]{1,0:T(8,128)(2,1)}, bf16[256,640]{1,0:T(8,128)(2,1)}) custom-call(s32[9]{0:T(128)} %pad_add_fusion.s, bf16[7,256,640]{2,1,0:T(8,128)(2,1)} %get-tuple-element.61.ou_ref.od_ref.g_ref, bf16[7,256,640]{2,1,0:T(8,128)(2,1)} %get-tuple-element.61.ou_ref.od_ref.g_ref, bf16[256,640]{1,0:T(8,128)(2,1)} %collective-permute-done.25.ui_ref, ...), custom_call_target="tpu_custom_call" | custom-call | bytes 1966080 | tf_op jit(solution)/shard_map/add_1_1/pallas_call | solution.py:312
  147.7 3.4 %code_0.1 = (bf16[272,640]{1,0:T(8,128)(2,1)}, bf16[272,640]{1,0:T(8,128)(2,1)}, bf16[144,640]{1,0:T(8,128)(2,1)}, bf16[144,640]{1,0:T(8,128)(2,1)}) custom-call(s32[9]{0:T(128)} %pad_add_fusion.s, bf16[7,256,640]{2,1,0:T(8,128)(2,1)} %get-tuple-element.75.ou_ref.od_ref.g_ref, bf16[256,640]{1,0:T(8,128)(2,1)} %collective-permute-done.38.ui_ref, ...), custom_call_target="tpu_custom_call" | custom-call | bytes 2621440 | tf_op jit(solution)/shard_map/code_0/pallas_call | solution.py:366
  153.7 3.4 %code_1.1 = (bf16[272,640]{1,0:T(8,128)(2,1)}, bf16[272,640]{1,0:T(8,128)(2,1)}, bf16[144,640]{1,0:T(8,128)(2,1)}, bf16[144,640]{1,0:T(8,128)(2,1)}) custom-call(s32[9]{0:T(128)} %pad_add_fusion.s, bf16[7,256,640]{2,1,0:T(8,128)(2,1)} %get-tuple-element.61.ou_ref.od_ref.g_ref, bf16[256,640]{1,0:T(8,128)(2,1)} %collective-permute-done.27.ui_ref, ...), custom_call_target="tpu_custom_call" | custom-call | bytes 2621440 | tf_op jit(solution)/shard_map/code_1/pallas_call | solution.py:366
  160.1 3.9 %collective-permute-done.42.refs_4_ = bf16[144,640]{1,0:T(8,128)(2,1)} collective-permute-done((bf16[144,640]{1,0:T(8,128)(2,1)}, bf16[144,640]{1,0:T(8,128)(2,1)}, u32[]{:S(2)}, u32[]{:S(2)}) %collective-permute-start.42) | collective-permute-done | bytes 184352 | tf_op jit(solution)/shard_map/ppermute | solution.py:481
  164.0 4.6 %finish_0.1 = (bf16[320,1024]{1,0:T(8,128)(2,1)}, f32[320,1024]{1,0:T(8,128)}, f32[320,1024]{1,0:T(8,128)}) custom-call(s32[9]{0:T(128)} %pad_add_fusion.s, bf16[320,1024]{1,0:T(8,128)(2,1)} %bitcast.11, f32[320,1024]{1,0:T(8,128)} %k_ref.3, f32[320,1024]{1,0:T(8,128)} %m_ref.3, bf16[272,640]{1,0:T(8,128)(2,1)} %get-tuple-element.85.refs_0_.refs_2_, ...), custom_call_target="tpu_custom_call" | custom-call | bytes 3932160 | tf_op jit(solution)/shard_map/finish_0/pallas_call | solution.py:434
  168.9 2.7 %collective-permute-done.31.refs_4_ = bf16[144,640]{1,0:T(8,128)(2,1)} collective-permute-done((bf16[144,640]{1,0:T(8,128)(2,1)}, bf16[144,640]{1,0:T(8,128)(2,1)}, u32[]{:S(2)}, u32[]{:S(2)}) %collective-permute-start.31) | collective-permute-done | bytes 184352 | tf_op jit(solution)/shard_map/ppermute | solution.py:481
  171.6 4.6 %finish_1.1 = (bf16[320,1024]{1,0:T(8,128)(2,1)}, f32[320,1024]{1,0:T(8,128)}, f32[320,1024]{1,0:T(8,128)}) custom-call(s32[9]{0:T(128)} %pad_add_fusion.s, bf16[320,1024]{1,0:T(8,128)(2,1)} %bitcast.12, f32[320,1024]{1,0:T(8,128)} %k_ref.3, f32[320,1024]{1,0:T(8,128)} %m_ref.3, ...), custom_call_target="tpu_custom_call", output_to_operand_aliasing={{0}: (10, {}), {1}: (11, {}), {2}: (12, {})} | custom-call | bytes 3932160 | tf_op jit(solution)/shard_map/finish_1/pallas_call | solution.py:434
  (98 shorter events, 60.7 us)
Async XLA Ops:
  5.1 24.6 %collective-permute-start.2 = (bf16[2,256,2560]{2,1,0:T(8,128)(2,1)}, bf16[2,256,2560]{2,1,0:T(8,128)(2,1)}, u32[]{:S(2)}, u32[]{:S(2)}) collective-permute-start(bf16[2,256,2560]{2,1,0:T(8,128)(2,1)} %bitcast.16), channel_id=1, source_target_pairs={{0,1},{1,0},{2,3},{3,2},{4,5},{5,4},{6,7},{7,6},{8,9},{9,8},{10,11... | collective-permute-start | bytes 7864328 | tf_op jit(solution)/shard_map/ppermute | solution.py:494
  8.4 21.3 %collective-permute-start.3 = (bf16[2,256,2560]{2,1,0:T(8,128)(2,1)}, bf16[2,256,2560]{2,1,0:T(8,128)(2,1)}, u32[]{:S(2)}, u32[]{:S(2)}) collective-permute-start(bf16[2,256,2560]{2,1,0:T(8,128)(2,1)} %bitcast.18), channel_id=1, source_target_pairs={{0,1},{1,0},{2,3},{3,2},{4,5},{5,4},{6,7},{7,6},{8,9},{9,8},{10,11... | collective-permute-start | bytes 7864328 | tf_op jit(solution)/shard_map/ppermute | solution.py:495
  8.6 11.8 %collective-permute-start.6 = (bf16[640,256]{1,0:T(8,128)(2,1)}, bf16[640,256]{1,0:T(8,128)(2,1)}, u32[]{:S(2)}, u32[]{:S(2)}) collective-permute-start(bf16[640,256]{1,0:T(8,128)(2,1)} %get-tuple-element.51.refs_0_), channel_id=1, source_target_pairs={{0,2},{1,3},{2,6},{3,7},{4,0},{5,1},{6,10},{7,11},{8,4},{9,5},{10,... | collective-permute-start | bytes 983048 | tf_op jit(solution)/shard_map/ppermute | solution.py:504
  11.4 18.2 %collective-permute-start.4 = (bf16[640,256]{1,0:T(8,128)(2,1)}, bf16[640,256]{1,0:T(8,128)(2,1)}, u32[]{:S(2)}, u32[]{:S(2)}) collective-permute-start(bf16[640,256]{1,0:T(8,128)(2,1)} %get-tuple-element.51.refs_0_), channel_id=1, source_target_pairs={{0,4},{1,5},{2,0},{3,1},{4,8},{5,9},{6,2},{7,3},{8,12},{9,13},{10,... | collective-permute-start | bytes 983048 | tf_op jit(solution)/shard_map/ppermute | solution.py:504
  11.5 18.1 %collective-permute-start.7 = (bf16[640,256]{1,0:T(8,128)(2,1)}, bf16[640,256]{1,0:T(8,128)(2,1)}, u32[]{:S(2)}, u32[]{:S(2)}) collective-permute-start(bf16[640,256]{1,0:T(8,128)(2,1)} %get-tuple-element.52.refs_1_.refs_7_), channel_id=1, source_target_pairs={{0,2},{1,3},{2,6},{3,7},{4,0},{5,1},{6,10},{7,11},{8,4},{9,5},{10,... | collective-permute-start | bytes 983048 | tf_op jit(solution)/shard_map/ppermute | solution.py:504
  29.7 41.7 %collective-permute-start.8 = (bf16[8,512,640]{2,1,0:T(8,128)(2,1)}, bf16[8,512,640]{2,1,0:T(8,128)(2,1)}, u32[]{:S(2)}, u32[]{:S(2)}) collective-permute-start(bf16[8,512,640]{2,1,0:T(8,128)(2,1)} %norm.1.a_ref), channel_id=1, source_target_pairs={{0,1},{1,0},{2,3},{3,2},{4,5},{5,4},{6,7},{7,6},{8,9},{9,8},{10,11... | collective-permute-start | bytes 15728648 | tf_op jit(solution)/shard_map/ppermute | solution.py:509
  29.8 10.8 %collective-permute-start.9 = (bf16[640,256]{1,0:T(8,128)(2,1)}, bf16[640,256]{1,0:T(8,128)(2,1)S(1)}, u32[]{:S(2)}, u32[]{:S(2)}) collective-permute-start(bf16[640,256]{1,0:T(8,128)(2,1)} %collective-permute-done.6.refs_1_), channel_id=1, source_target_pairs={{0,2},{1,3},{2,6},{3,7},{4,0},{5,1},{6,10},{7,11},{8,4},{9,5},{10,... | collective-permute-start | bytes 983048 | tf_op jit(solution)/shard_map/ppermute | solution.py:504
  30.8 10.8 %collective-permute-start.10 = (bf16[640,256]{1,0:T(8,128)(2,1)}, bf16[640,256]{1,0:T(8,128)(2,1)S(1)}, u32[]{:S(2)}, u32[]{:S(2)}) collective-permute-start(bf16[640,256]{1,0:T(8,128)(2,1)} %collective-permute-done.4.refs_2_), channel_id=1, source_target_pairs={{0,4},{1,5},{2,0},{3,1},{4,8},{5,9},{6,2},{7,3},{8,12},{9,13},{10,... | collective-permute-start | bytes 983048 | tf_op jit(solution)/shard_map/ppermute | solution.py:504
  31.8 15.7 %collective-permute-start.13 = (bf16[640,256]{1,0:T(8,128)(2,1)}, bf16[640,256]{1,0:T(8,128)(2,1)S(1)}, u32[]{:S(2)}, u32[]{:S(2)}) collective-permute-start(bf16[640,256]{1,0:T(8,128)(2,1)} %collective-permute-done.7.refs_8_), channel_id=1, source_target_pairs={{0,2},{1,3},{2,6},{3,7},{4,0},{5,1},{6,10},{7,11},{8,4},{9,5},{10,... | collective-permute-start | bytes 983048 | tf_op jit(solution)/shard_map/ppermute | solution.py:504
  32.8 15.8 %collective-permute-start.14 = (bf16[640,256]{1,0:T(8,128)(2,1)}, bf16[640,256]{1,0:T(8,128)(2,1)S(1)}, u32[]{:S(2)}, u32[]{:S(2)}) collective-permute-start(bf16[640,256]{1,0:T(8,128)(2,1)} %collective-permute-done.5.refs_9_), channel_id=1, source_target_pairs={{0,4},{1,5},{2,0},{3,1},{4,8},{5,9},{6,2},{7,3},{8,12},{9,13},{10,... | collective-permute-start | bytes 983048 | tf_op jit(solution)/shard_map/ppermute | solution.py:504
  40.5 14.0 %collective-permute-start.11 = (bf16[640,256]{1,0:T(8,128)(2,1)S(1)}, bf16[640,256]{1,0:T(8,128)(2,1)S(1)}, u32[]{:S(2)}, u32[]{:S(2)}) collective-permute-start(bf16[640,256]{1,0:T(8,128)(2,1)S(1)} %collective-permute-done.9.refs_3_), channel_id=1, source_target_pairs={{0,2},{1,3},{2,6},{3,7},{4,0},{5,1},{6,10},{7,11},{8,4},{9,5},{10,... | collective-permute-start | bytes 983048 | tf_op jit(solution)/shard_map/ppermute | solution.py:504
  41.6 15.4 %collective-permute-start.12 = (bf16[640,256]{1,0:T(8,128)(2,1)S(1)}, bf16[640,256]{1,0:T(8,128)(2,1)S(1)}, u32[]{:S(2)}, u32[]{:S(2)}) collective-permute-start(bf16[640,256]{1,0:T(8,128)(2,1)S(1)} %collective-permute-done.10.refs_4_), channel_id=1, source_target_pairs={{0,4},{1,5},{2,0},{3,1},{4,8},{5,9},{6,2},{7,3},{8,12},{9,13},{10,... | collective-permute-start | bytes 983048 | tf_op jit(solution)/shard_map/ppermute | solution.py:504
  47.6 14.0 %collective-permute-start.15 = (bf16[640,256]{1,0:T(8,128)(2,1)S(1)}, bf16[640,256]{1,0:T(8,128)(2,1)S(1)}, u32[]{:S(2)}, u32[]{:S(2)}) collective-permute-start(bf16[640,256]{1,0:T(8,128)(2,1)S(1)} %collective-permute-done.13.refs_10_), channel_id=1, source_target_pairs={{0,2},{1,3},{2,6},{3,7},{4,0},{5,1},{6,10},{7,11},{8,4},{9,5},{10,... | collective-permute-start | bytes 983048 | tf_op jit(solution)/shard_map/ppermute | solution.py:504
  48.6 15.4 %collective-permute-start.16 = (bf16[640,256]{1,0:T(8,128)(2,1)S(1)}, bf16[640,256]{1,0:T(8,128)(2,1)S(1)}, u32[]{:S(2)}, u32[]{:S(2)}) collective-permute-start(bf16[640,256]{1,0:T(8,128)(2,1)S(1)} %collective-permute-done.14.refs_11_), channel_id=1, source_target_pairs={{0,4},{1,5},{2,0},{3,1},{4,8},{5,9},{6,2},{7,3},{8,12},{9,13},{10,... | collective-permute-start | bytes 983048 | tf_op jit(solution)/shard_map/ppermute | solution.py:504
  56.0 14.6 %collective-permute-start.18 = (bf16[320,256]{1,0:T(8,128)(2,1)}, bf16[320,256]{1,0:T(8,128)(2,1)}, u32[]{:S(2)}, u32[]{:S(2)}) collective-permute-start(bf16[320,256]{1,0:T(8,128)(2,1)} %slice.17), channel_id=1, source_target_pairs={{0,2},{1,3},{2,6},{3,7},{4,0},{5,1},{6,10},{7,11},{8,4},{9,5},{10,... | collective-permute-start | bytes 491528 | tf_op jit(solution)/shard_map/ppermute | solution.py:507
  58.4 12.2 %collective-permute-start.17 = (bf16[320,256]{1,0:T(8,128)(2,1)}, bf16[320,256]{1,0:T(8,128)(2,1)}, u32[]{:S(2)}, u32[]{:S(2)}) collective-permute-start(bf16[320,256]{1,0:T(8,128)(2,1)} %slice.16), channel_id=1, source_target_pairs={{0,4},{1,5},{2,0},{3,1},{4,8},{5,9},{6,2},{7,3},{8,12},{9,13},{10,... | collective-permute-start | bytes 491528 | tf_op jit(solution)/shard_map/ppermute | solution.py:507
  107.6 10.9 %collective-permute-start.34 = (bf16[256,640]{1,0:T(8,128)(2,1)}, bf16[256,640]{1,0:T(8,128)(2,1)}, u32[]{:S(2)}, u32[]{:S(2)}) collective-permute-start(bf16[256,640]{1,0:T(8,128)(2,1)} %get-tuple-element.78), channel_id=1, source_target_pairs={{0,4},{1,5},{2,0},{3,1},{4,8},{5,9},{6,2},{7,3},{8,12},{9,13},{10,... | collective-permute-start | bytes 983048 | tf_op jit(solution)/shard_map/ppermute | solution.py:522
  109.2 10.8 %collective-permute-start.35 = (bf16[256,640]{1,0:T(8,128)(2,1)}, bf16[256,640]{1,0:T(8,128)(2,1)}, u32[]{:S(2)}, u32[]{:S(2)}) collective-permute-start(bf16[256,640]{1,0:T(8,128)(2,1)} %get-tuple-element.79), channel_id=1, source_target_pairs={{0,2},{1,3},{2,6},{3,7},{4,0},{5,1},{6,10},{7,11},{8,4},{9,5},{10,... | collective-permute-start | bytes 983048 | tf_op jit(solution)/shard_map/ppermute | solution.py:522
  112.4 12.8 %collective-permute-start.23 = (bf16[256,640]{1,0:T(8,128)(2,1)}, bf16[256,640]{1,0:T(8,128)(2,1)}, u32[]{:S(2)}, u32[]{:S(2)}) collective-permute-start(bf16[256,640]{1,0:T(8,128)(2,1)} %get-tuple-element.64), channel_id=1, source_target_pairs={{0,4},{1,5},{2,0},{3,1},{4,8},{5,9},{6,2},{7,3},{8,12},{9,13},{10,... | collective-permute-start | bytes 983048 | tf_op jit(solution)/shard_map/ppermute | solution.py:522
  114.0 13.0 %collective-permute-start.24 = (bf16[256,640]{1,0:T(8,128)(2,1)}, bf16[256,640]{1,0:T(8,128)(2,1)}, u32[]{:S(2)}, u32[]{:S(2)}) collective-permute-start(bf16[256,640]{1,0:T(8,128)(2,1)} %get-tuple-element.65), channel_id=1, source_target_pairs={{0,2},{1,3},{2,6},{3,7},{4,0},{5,1},{6,10},{7,11},{8,4},{9,5},{10,... | collective-permute-start | bytes 983048 | tf_op jit(solution)/shard_map/ppermute | solution.py:522
  129.7 10.8 %collective-permute-start.25 = (bf16[256,640]{1,0:T(8,128)(2,1)}, bf16[256,640]{1,0:T(8,128)(2,1)}, u32[]{:S(2)}, u32[]{:S(2)}) collective-permute-start(bf16[256,640]{1,0:T(8,128)(2,1)} %get-tuple-element.66), channel_id=1, source_target_pairs={{0,4},{1,5},{2,0},{3,1},{4,8},{5,9},{6,2},{7,3},{8,12},{9,13},{10,... | collective-permute-start | bytes 983048 | tf_op jit(solution)/shard_map/ppermute | solution.py:522
  152.6 11.4 %collective-permute-start.41 = (bf16[272,640]{1,0:T(8,128)(2,1)}, bf16[272,640]{1,0:T(8,128)(2,1)}, u32[]{:S(2)}, u32[]{:S(2)}) collective-permute-start(bf16[272,640]{1,0:T(8,128)(2,1)} %get-tuple-element.87), channel_id=1, source_target_pairs={{0,1},{1,0},{2,3},{3,2},{4,5},{5,4},{6,7},{7,6},{8,9},{9,8},{10,11... | collective-permute-start | bytes 1044488 | tf_op jit(solution)/shard_map/ppermute | solution.py:527
  157.1 14.5 %collective-permute-start.30 = (bf16[272,640]{1,0:T(8,128)(2,1)}, bf16[272,640]{1,0:T(8,128)(2,1)}, u32[]{:S(2)}, u32[]{:S(2)}) collective-permute-start(bf16[272,640]{1,0:T(8,128)(2,1)} %get-tuple-element.73), channel_id=1, source_target_pairs={{0,1},{1,0},{2,3},{3,2},{4,5},{5,4},{6,7},{7,6},{8,9},{9,8},{10,11... | collective-permute-start | bytes 1044488 | tf_op jit(solution)/shard_map/ppermute | solution.py:527
  159.2 12.4 %collective-permute-start.31 = (bf16[144,640]{1,0:T(8,128)(2,1)}, bf16[144,640]{1,0:T(8,128)(2,1)}, u32[]{:S(2)}, u32[]{:S(2)}) collective-permute-start(bf16[144,640]{1,0:T(8,128)(2,1)} %get-tuple-element.74), channel_id=1, source_target_pairs={{0,17},{1,16},{2,19},{3,18},{4,21},{5,20},{6,23},{7,22},{8,25},{9,... | collective-permute-start | bytes 552968 | tf_op jit(solution)/shard_map/ppermute | solution.py:481
  (27 other events, 224.8 us)

commit v5 on v4

--- a/solution.py
+++ b/solution.py
@@ -147,7 +147,7 @@
     )(scalars, outer, received, *blocks)
 
 
-def group_step(scalars, rows_mine, rows_other, blocks, halves, queries, queries_other, out_grad, out_grad_other, heads):
+def group_step(scalars, rows_mine, rows_other, blocks, queries, queries_other, out_grad, out_grad_other, heads):
     chips, tokens, part = rows_mine.shape
     seqs, length, query_width = queries.shape
     own_width = query_width // 2
@@ -159,9 +159,8 @@
     wide = 2 * HD
 
     def body(s, a_ref, b_ref, qa_ref, qb_ref, ga_ref, gb_ref, *refs):
-        block_refs = [refs[h * last : (h + 1) * last] for h in range(heads)]
-        half_refs = [refs[heads * last + 2 * h : heads * last + 2 * h + 2] for h in range(heads)]
-        refs = refs[heads * (last + 2) :]
+        block_refs = [refs[h * chips : (h + 1) * chips] for h in range(heads)]
+        refs = refs[heads * chips :]
         sum_refs, up_refs, down_refs = refs[:heads], refs[heads : 2 * heads], refs[2 * heads : 3 * heads]
         held, w_held, q_held, g_held, acc, grads, done = refs[3 * heads : 3 * heads + 7]
         row_sems, w_sems, q_sems, out_sems = refs[3 * heads + 7 :]
@@ -172,12 +171,7 @@
             for side, ref in enumerate((a_ref, b_ref)):
                 wait.append(pltpu.make_async_copy(ref.at[s[1 + k]], held.at[k, side], row_sems.at[k, side]))
             for h in range(heads):
-                if k < last:
-                    wait.append(pltpu.make_async_copy(block_refs[h][k], w_held.at[h, k], w_sems.at[h, k]))
-                else:
-                    for at in range(2):
-                        there = w_held.at[h, k, pl.ds(at * (part // 2), part // 2)]
-                        wait.append(pltpu.make_async_copy(half_refs[h][at], there, w_sems.at[h, k + at]))
+                wait.append(pltpu.make_async_copy(block_refs[h][k], w_held.at[h, k], w_sems.at[h, k]))
             waits.append(wait)
         mine = pl.ds(pl.multiple_of(s[0] * own_width, HD), own_width)
         pairs = (
@@ -263,8 +257,6 @@
     inputs = [rows_mine, rows_other, queries, queries_other, out_grad, out_grad_other]
     for h in range(heads):
         inputs += blocks[h]
-    for h in range(heads):
-        inputs += halves[h]
     flops = 2 * 2 * tokens * chips * part * wide * heads * 2 + heads * 2 * seqs * repeat * length * length * HD * 16
     outs = call(
         body,
@@ -280,7 +272,7 @@
             pltpu.VMEM((heads * wide, 2 * tokens), BF16),
             pltpu.VMEM((heads, chips, wide, part), BF16),
             pltpu.SemaphoreType.DMA((chips, 2)),
-            pltpu.SemaphoreType.DMA((heads, chips + 1)),
+            pltpu.SemaphoreType.DMA((heads, chips)),
             pltpu.SemaphoreType.DMA((4,)),
             pltpu.SemaphoreType.DMA((heads, chips + 1)),
         ],
@@ -496,7 +488,6 @@
     rows_mine = norm_rows(scalars, tied((hidden, own))[0].reshape(seqs * length, width), norm_gain, chips)
 
     blocks = [[own[h]] for h in range(heads)]
-    halves = [None] * heads
     ups, downs = list(own), list(own)
     for step in range(1, far + 1):
         for h in range(heads):
@@ -504,14 +495,14 @@
                 ups[h], downs[h] = up(ups[h]), down(downs[h])
                 blocks[h] += [downs[h], ups[h]]
             else:
-                halves[h] = (up(ups[h][: part // 2]), down(downs[h][part // 2 :]))
+                blocks[h].append(up(ups[h]) if h % 2 == 0 else down(downs[h]))
         if step == 1:
             rows_other = swap(tied((rows_mine, queries_other, out_grad_other, ups, downs))[0])
     deltas = start_deltas(scalars, own, kv_outer, outer_other, heads)
 
     rows_mine, deltas = lax.optimization_barrier((rows_mine, deltas))
     sums, far_up, far_down = group_step(
-        scalars, rows_mine, rows_other, blocks, halves, queries[0], queries_other, out_grad[0], out_grad_other, heads
+        scalars, rows_mine, rows_other, blocks, queries[0], queries_other, out_grad[0], out_grad_other, heads
     )
 
     outs = None

time: 177 us -> 176 us (level)
  waiting for transfers between devices: 53.7 us -> 60.7 us
  local copies, waits for them, and re-layouts: 6.4 us -> 1.42 us
  starting transfers between devices: 41.8 us -> 39.1 us
    ppermute x4 -> x2, waiting for transfers between devices: 0.75 us -> 6.24 us  [local(): blocks[h].append(up(ups[h]) if h % 2 == 0 else down(downs[h]))]
    slice x4 -> x0, local copies, waits for them, and re-layouts: 2.7 us -> none  [local(): halves[h] = (up(ups[h][:part // 2]), down(downs[h][part // 2:]))]
    unnamed x16 -> x4, local copies, waits for them, and re-layouts: 3 us -> 0.73 us
    ppermute x4 -> x2, starting transfers between devices: 4.28 us -> 2.03 us  [local(): blocks[h].append(up(ups[h]) if h % 2 == 0 else down(downs[h]))]
    ppermute x8, waiting for transfers between devices: 8.25 us -> 10.5 us  [local(): up(going_up)]
    ppermute x8, starting transfers between devices: 12.5 us -> 10.4 us  [local(): up(going_up)]
  transfers between devices with their start and end apart: 43 -> 41, of which waited for: 22 -> 22; matrix products, arithmetic and copies ran while one was open for 2% -> 1% of each run, Pallas kernels for 24% -> 24%
where the time goes in v5:
time: 176 us
  Pallas kernels  72.8 us (41%)
  waiting for transfers between devices  60.7 us (34%)
  starting transfers between devices  39.1 us (22%)
    pallas_call x1, Pallas kernels, group_step(): call(body, [jax.ShapeDtypeStruct((last, wide, part), BF16)] * heads + [ja...  26 us
    ppermute x12, waiting for transfers between devices, local(): ups[h], downs[h] = (up(ups[h]), down(downs[h]))  25.7 us
    pallas_call x6, Pallas kernels, add_partials(): call(body, [shape] * 2, [pl.BlockSpec((1, HD, part), lambda i, s: (at, i,...  16.9 us
    ppermute x12, starting transfers between devices, local(): ups[h], downs[h] = (up(ups[h]), down(downs[h]))  15.1 us
    ppermute x8, waiting for transfers between devices, local(): up(going_up)  10.5 us
    ppermute x8, starting transfers between devices, local(): up(going_up)  10.4 us
    pallas_call x2, Pallas kernels, finish(): call(body, [jax.ShapeDtypeStruct((rows, cols), BF16), jax.ShapeDtypeStruc...  9.17 us
    ppermute x8, waiting for transfers between devices, local(): down(going_down)  8.15 us
  transfers between devices with their start and end apart: 41, of which 22 were waited for; matrix products, arithmetic and copies ran while one was open for 1% of the time, Pallas kernels for 24%

profile of v5, /device:TPU:0, one launch (start us, length us, event | category | flops | bytes accessed | tf_op | source)
XLA Modules:
  0.0 175.7 jit_solution(10134754946620309610)
XLA Ops:
  5.5 2.9 %own_blocks.1 = (bf16[640,256]{1,0:T(8,128)(2,1)}, bf16[640,256]{1,0:T(8,128)(2,1)}) custom-call(s32[9]{0:T(128)} %pad_add_fusion.s, bf16[320,1024]{1,0:T(8,128)(2,1)} %bitcast.10, bf16[320,1024]{1,0:T(8,128)(2,1)} %collective-permute-done.r_ref), custom_call_target="tpu_custom_call" | custom-call | bytes 1966080 | tf_op jit(solution)/shard_map/own_blocks/pallas_call | solution.py:113
  8.5 2.9 %collective-permute-start.6 = (bf16[640,256]{1,0:T(8,128)(2,1)}, bf16[640,256]{1,0:T(8,128)(2,1)}, u32[]{:S(2)}, u32[]{:S(2)}) collective-permute-start(bf16[640,256]{1,0:T(8,128)(2,1)} %get-tuple-element.51.refs_0_), channel_id=1, source_target_pairs={{0,2},{1,3},{2,6},{3,7},{4,0},{5,1},{6,10},{7,11},{8,4},{9,5},{10,... | collective-permute-start | bytes 983048 | tf_op jit(solution)/shard_map/ppermute | solution.py:495
  13.4 6.9 %collective-permute-done.6.refs_1_ = bf16[640,256]{1,0:T(8,128)(2,1)} collective-permute-done((bf16[640,256]{1,0:T(8,128)(2,1)}, bf16[640,256]{1,0:T(8,128)(2,1)}, u32[]{:S(2)}, u32[]{:S(2)}) %collective-permute-start.6) | collective-permute-done | bytes 327712 | tf_op jit(solution)/shard_map/ppermute | solution.py:495
  22.4 7.3 %norm.1.a_ref = bf16[8,512,640]{2,1,0:T(8,128)(2,1)} custom-call(s32[9]{0:T(128)} %pad_add_fusion.s, bf16[512,5120]{1,0:T(8,128)(2,1)} %bitcast.13, f32[1,5120]{1,0:T(1,128)} %bitcast.15), custom_call_target="tpu_custom_call" | custom-call | flops 15728640 | bytes 10485760 | tf_op jit(solution)/shard_map/norm/pallas_call | solution.py:82
  33.9 6.7 %collective-permute-done.10.refs_4_ = bf16[640,256]{1,0:T(8,128)(2,1)S(1)} collective-permute-done((bf16[640,256]{1,0:T(8,128)(2,1)}, bf16[640,256]{1,0:T(8,128)(2,1)S(1)}, u32[]{:S(2)}, u32[]{:S(2)}) %collective-permute-start.10) | collective-permute-done | bytes 327712 | tf_op jit(solution)/shard_map/ppermute | solution.py:495
  43.3 6.0 %collective-permute-done.9.refs_3_ = bf16[640,256]{1,0:T(8,128)(2,1)} collective-permute-done((bf16[640,256]{1,0:T(8,128)(2,1)}, bf16[640,256]{1,0:T(8,128)(2,1)}, u32[]{:S(2)}, u32[]{:S(2)}) %collective-permute-start.9) | collective-permute-done | bytes 327712 | tf_op jit(solution)/shard_map/ppermute | solution.py:495
  51.3 3.4 %collective-permute-done.12.refs_6_ = bf16[640,256]{1,0:T(8,128)(2,1)} collective-permute-done((bf16[640,256]{1,0:T(8,128)(2,1)S(1)}, bf16[640,256]{1,0:T(8,128)(2,1)}, u32[]{:S(2)}, u32[]{:S(2)}) %collective-permute-start.12) | collective-permute-done | bytes 327712 | tf_op jit(solution)/shard_map/ppermute | solution.py:495
  56.7 3.8 %start_deltas.1 = (f32[256,640]{1,0:T(8,128)}, f32[256,640]{1,0:T(8,128)}) custom-call(s32[9]{0:T(128)} %pad_add_fusion.s, f32[320,1024]{1,0:T(8,128)} %k_ref.3, f32[320,1024]{1,0:T(8,128)} %collective-permute-done.1.r_ref, bf16[640,256]{1,0:T(8,128)(2,1)} %get-tuple-element.51.refs_0_, bf16[640,256]{1,0:T(8,128)(2,1)} %get-tuple-element.52.refs_1_.refs_8_), custom_call_target="tpu_custom_call" | custom-call | bytes 4587520 | tf_op jit(solution)/shard_map/start_deltas/pallas_call | solution.py:140
  63.3 4.9 %collective-permute-done.13.refs_7_ = bf16[640,256]{1,0:T(8,128)(2,1)} collective-permute-done((bf16[640,256]{1,0:T(8,128)(2,1)}, bf16[640,256]{1,0:T(8,128)(2,1)}, u32[]{:S(2)}, u32[]{:S(2)}) %collective-permute-start.13) | collective-permute-done | bytes 327712 | tf_op jit(solution)/shard_map/ppermute | solution.py:498
  69.6 26.0 %group_step.1 = (bf16[7,256,640]{2,1,0:T(8,128)(2,1)}, bf16[7,256,640]{2,1,0:T(8,128)(2,1)}, bf16[128,640]{1,0:T(8,128)(2,1)}, bf16[128,640]{1,0:T(8,128)(2,1)},...) custom-call(s32[9]{0:T(128)} %pad_add_fusion.s, bf16[8,512,640]{2,1,0:T(8,128)(2,1)} %norm.1.a_ref, ...), custom_call_target="tpu_custom_call" | custom-call | flops 16106127360 | bytes 31457280 | tf_op jit(solution)/shard_map/group_step/pallas_call | solution.py:261
  99.7 3.4 %collective-permute-done.30.ui_ref = bf16[128,640]{1,0:T(8,128)(2,1)} collective-permute-done((bf16[128,640]{1,0:T(8,128)(2,1)}, bf16[128,640]{1,0:T(8,128)(2,1)}, u32[]{:S(2)}, u32[]{:S(2)}) %collective-permute-start.30) | collective-permute-done | bytes 163872 | tf_op jit(solution)/shard_map/ppermute | solution.py:513
  104.4 2.8 %add_0_3.1 = (bf16[256,640]{1,0:T(8,128)(2,1)}, bf16[256,640]{1,0:T(8,128)(2,1)}) custom-call(s32[9]{0:T(128)} %pad_add_fusion.s, bf16[7,256,640]{2,1,0:T(8,128)(2,1)} %get-tuple-element.75.ou_ref.od_ref.g_ref, bf16[7,256,640]{2,1,0:T(8,128)(2,1)} %get-tuple-element.75.ou_ref.od_ref.g_ref, bf16[128,640]{1,0:T(8,128)(2,1)} %collective-permute-done.30.ui_ref, ...), custom_call_target="tpu_custom_call" | custom-call | bytes 1966080 | tf_op jit(solution)/shard_map/add_0_3/pallas_call | solution.py:304
  109.2 2.7 %add_1_3.1 = (bf16[256,640]{1,0:T(8,128)(2,1)}, bf16[256,640]{1,0:T(8,128)(2,1)}) custom-call(s32[9]{0:T(128)} %pad_add_fusion.s, bf16[7,256,640]{2,1,0:T(8,128)(2,1)} %get-tuple-element.61.ou_ref.od_ref.g_ref, bf16[7,256,640]{2,1,0:T(8,128)(2,1)} %get-tuple-element.61.ou_ref.od_ref.g_ref, bf16[128,640]{1,0:T(8,128)(2,1)} %collective-permute-done.19.ui_ref, ...), custom_call_target="tpu_custom_call" | custom-call | bytes 1966080 | tf_op jit(solution)/shard_map/add_1_3/pallas_call | solution.py:304
  114.0 4.1 %collective-permute-done.32.ui_ref = bf16[256,640]{1,0:T(8,128)(2,1)} collective-permute-done((bf16[256,640]{1,0:T(8,128)(2,1)}, bf16[256,640]{1,0:T(8,128)(2,1)}, u32[]{:S(2)}, u32[]{:S(2)}) %collective-permute-start.32) | collective-permute-done | bytes 327712 | tf_op jit(solution)/shard_map/ppermute | solution.py:513
  119.5 2.9 %add_0_2.1 = (bf16[256,640]{1,0:T(8,128)(2,1)}, bf16[256,640]{1,0:T(8,128)(2,1)}) custom-call(s32[9]{0:T(128)} %pad_add_fusion.s, bf16[7,256,640]{2,1,0:T(8,128)(2,1)} %get-tuple-element.75.ou_ref.od_ref.g_ref, bf16[7,256,640]{2,1,0:T(8,128)(2,1)} %get-tuple-element.75.ou_ref.od_ref.g_ref, bf16[256,640]{1,0:T(8,128)(2,1)} %collective-permute-done.32.ui_ref, ...), custom_call_target="tpu_custom_call" | custom-call | bytes 1966080 | tf_op jit(solution)/shard_map/add_0_2/pallas_call | solution.py:304
  126.5 2.8 %add_1_2.1 = (bf16[256,640]{1,0:T(8,128)(2,1)}, bf16[256,640]{1,0:T(8,128)(2,1)}) custom-call(s32[9]{0:T(128)} %pad_add_fusion.s, bf16[7,256,640]{2,1,0:T(8,128)(2,1)} %get-tuple-element.61.ou_ref.od_ref.g_ref, bf16[7,256,640]{2,1,0:T(8,128)(2,1)} %get-tuple-element.61.ou_ref.od_ref.g_ref, bf16[256,640]{1,0:T(8,128)(2,1)} %collective-permute-done.21.ui_ref, ...), custom_call_target="tpu_custom_call" | custom-call | bytes 1966080 | tf_op jit(solution)/shard_map/add_1_2/pallas_call | solution.py:304
  133.8 2.8 %add_0_1.1 = (bf16[256,640]{1,0:T(8,128)(2,1)}, bf16[256,640]{1,0:T(8,128)(2,1)}) custom-call(s32[9]{0:T(128)} %pad_add_fusion.s, bf16[7,256,640]{2,1,0:T(8,128)(2,1)} %get-tuple-element.75.ou_ref.od_ref.g_ref, bf16[7,256,640]{2,1,0:T(8,128)(2,1)} %get-tuple-element.75.ou_ref.od_ref.g_ref, bf16[256,640]{1,0:T(8,128)(2,1)} %collective-permute-done.34.ui_ref, ...), custom_call_target="tpu_custom_call" | custom-call | bytes 1966080 | tf_op jit(solution)/shard_map/add_0_1/pallas_call | solution.py:304
  141.2 2.9 %add_1_1.1 = (bf16[256,640]{1,0:T(8,128)(2,1)}, bf16[256,640]{1,0:T(8,128)(2,1)}) custom-call(s32[9]{0:T(128)} %pad_add_fusion.s, bf16[7,256,640]{2,1,0:T(8,128)(2,1)} %get-tuple-element.61.ou_ref.od_ref.g_ref, bf16[7,256,640]{2,1,0:T(8,128)(2,1)} %get-tuple-element.61.ou_ref.od_ref.g_ref, bf16[256,640]{1,0:T(8,128)(2,1)} %collective-permute-done.23.ui_ref, ...), custom_call_target="tpu_custom_call" | custom-call | bytes 1966080 | tf_op jit(solution)/shard_map/add_1_1/pallas_call | solution.py:304
  147.3 3.4 %code_0.1 = (bf16[272,640]{1,0:T(8,128)(2,1)}, bf16[272,640]{1,0:T(8,128)(2,1)}, bf16[144,640]{1,0:T(8,128)(2,1)}, bf16[144,640]{1,0:T(8,128)(2,1)}) custom-call(s32[9]{0:T(128)} %pad_add_fusion.s, bf16[7,256,640]{2,1,0:T(8,128)(2,1)} %get-tuple-element.75.ou_ref.od_ref.g_ref, bf16[256,640]{1,0:T(8,128)(2,1)} %collective-permute-done.36.ui_ref, ...), custom_call_target="tpu_custom_call" | custom-call | bytes 2621440 | tf_op jit(solution)/shard_map/code_0/pallas_call | solution.py:358
  152.3 3.4 %code_1.1 = (bf16[272,640]{1,0:T(8,128)(2,1)}, bf16[272,640]{1,0:T(8,128)(2,1)}, bf16[144,640]{1,0:T(8,128)(2,1)}, bf16[144,640]{1,0:T(8,128)(2,1)}) custom-call(s32[9]{0:T(128)} %pad_add_fusion.s, bf16[7,256,640]{2,1,0:T(8,128)(2,1)} %get-tuple-element.61.ou_ref.od_ref.g_ref, bf16[256,640]{1,0:T(8,128)(2,1)} %collective-permute-done.25.ui_ref, ...), custom_call_target="tpu_custom_call" | custom-call | bytes 2621440 | tf_op jit(solution)/shard_map/code_1/pallas_call | solution.py:358
  158.7 4.3 %collective-permute-done.40.refs_4_ = bf16[144,640]{1,0:T(8,128)(2,1)} collective-permute-done((bf16[144,640]{1,0:T(8,128)(2,1)}, bf16[144,640]{1,0:T(8,128)(2,1)}, u32[]{:S(2)}, u32[]{:S(2)}) %collective-permute-start.40) | collective-permute-done | bytes 184352 | tf_op jit(solution)/shard_map/ppermute | solution.py:473
  163.0 4.6 %finish_0.1 = (bf16[320,1024]{1,0:T(8,128)(2,1)}, f32[320,1024]{1,0:T(8,128)}, f32[320,1024]{1,0:T(8,128)}) custom-call(s32[9]{0:T(128)} %pad_add_fusion.s, bf16[320,1024]{1,0:T(8,128)(2,1)} %bitcast.11, f32[320,1024]{1,0:T(8,128)} %k_ref.3, f32[320,1024]{1,0:T(8,128)} %m_ref.3, bf16[272,640]{1,0:T(8,128)(2,1)} %get-tuple-element.85.refs_0_.refs_2_, ...), custom_call_target="tpu_custom_call" | custom-call | bytes 3932160 | tf_op jit(solution)/shard_map/finish_0/pallas_call | solution.py:426
  167.6 3.3 %collective-permute-done.29.refs_4_ = bf16[144,640]{1,0:T(8,128)(2,1)} collective-permute-done((bf16[144,640]{1,0:T(8,128)(2,1)}, bf16[144,640]{1,0:T(8,128)(2,1)}, u32[]{:S(2)}, u32[]{:S(2)}) %collective-permute-start.29) | collective-permute-done | bytes 184352 | tf_op jit(solution)/shard_map/ppermute | solution.py:473
  170.9 4.6 %finish_1.1 = (bf16[320,1024]{1,0:T(8,128)(2,1)}, f32[320,1024]{1,0:T(8,128)}, f32[320,1024]{1,0:T(8,128)}) custom-call(s32[9]{0:T(128)} %pad_add_fusion.s, bf16[320,1024]{1,0:T(8,128)(2,1)} %bitcast.12, f32[320,1024]{1,0:T(8,128)} %k_ref.3, f32[320,1024]{1,0:T(8,128)} %m_ref.3, ...), custom_call_target="tpu_custom_call", output_to_operand_aliasing={{0}: (10, {}), {1}: (11, {}), {2}: (12, {})} | custom-call | bytes 3932160 | tf_op jit(solution)/shard_map/finish_1/pallas_call | solution.py:426
  (78 shorter events, 56.1 us)
Async XLA Ops:
  5.1 24.6 %collective-permute-start.2 = (bf16[2,256,2560]{2,1,0:T(8,128)(2,1)}, bf16[2,256,2560]{2,1,0:T(8,128)(2,1)}, u32[]{:S(2)}, u32[]{:S(2)}) collective-permute-start(bf16[2,256,2560]{2,1,0:T(8,128)(2,1)} %bitcast.16), channel_id=1, source_target_pairs={{0,1},{1,0},{2,3},{3,2},{4,5},{5,4},{6,7},{7,6},{8,9},{9,8},{10,11... | collective-permute-start | bytes 7864328 | tf_op jit(solution)/shard_map/ppermute | solution.py:486
  8.4 21.3 %collective-permute-start.3 = (bf16[2,256,2560]{2,1,0:T(8,128)(2,1)}, bf16[2,256,2560]{2,1,0:T(8,128)(2,1)}, u32[]{:S(2)}, u32[]{:S(2)}) collective-permute-start(bf16[2,256,2560]{2,1,0:T(8,128)(2,1)} %bitcast.18), channel_id=1, source_target_pairs={{0,1},{1,0},{2,3},{3,2},{4,5},{5,4},{6,7},{7,6},{8,9},{9,8},{10,11... | collective-permute-start | bytes 7864328 | tf_op jit(solution)/shard_map/ppermute | solution.py:487
  8.5 11.8 %collective-permute-start.6 = (bf16[640,256]{1,0:T(8,128)(2,1)}, bf16[640,256]{1,0:T(8,128)(2,1)}, u32[]{:S(2)}, u32[]{:S(2)}) collective-permute-start(bf16[640,256]{1,0:T(8,128)(2,1)} %get-tuple-element.51.refs_0_), channel_id=1, source_target_pairs={{0,2},{1,3},{2,6},{3,7},{4,0},{5,1},{6,10},{7,11},{8,4},{9,5},{10,... | collective-permute-start | bytes 983048 | tf_op jit(solution)/shard_map/ppermute | solution.py:495
  11.4 18.2 %collective-permute-start.4 = (bf16[640,256]{1,0:T(8,128)(2,1)}, bf16[640,256]{1,0:T(8,128)(2,1)}, u32[]{:S(2)}, u32[]{:S(2)}) collective-permute-start(bf16[640,256]{1,0:T(8,128)(2,1)} %get-tuple-element.51.refs_0_), channel_id=1, source_target_pairs={{0,4},{1,5},{2,0},{3,1},{4,8},{5,9},{6,2},{7,3},{8,12},{9,13},{10,... | collective-permute-start | bytes 983048 | tf_op jit(solution)/shard_map/ppermute | solution.py:495
  11.5 18.1 %collective-permute-start.7 = (bf16[640,256]{1,0:T(8,128)(2,1)}, bf16[640,256]{1,0:T(8,128)(2,1)}, u32[]{:S(2)}, u32[]{:S(2)}) collective-permute-start(bf16[640,256]{1,0:T(8,128)(2,1)} %get-tuple-element.52.refs_1_.refs_8_), channel_id=1, source_target_pairs={{0,2},{1,3},{2,6},{3,7},{4,0},{5,1},{6,10},{7,11},{8,4},{9,5},{10,... | collective-permute-start | bytes 983048 | tf_op jit(solution)/shard_map/ppermute | solution.py:495
  29.7 39.9 %collective-permute-start.8 = (bf16[8,512,640]{2,1,0:T(8,128)(2,1)}, bf16[8,512,640]{2,1,0:T(8,128)(2,1)}, u32[]{:S(2)}, u32[]{:S(2)}) collective-permute-start(bf16[8,512,640]{2,1,0:T(8,128)(2,1)} %norm.1.a_ref), channel_id=1, source_target_pairs={{0,1},{1,0},{2,3},{3,2},{4,5},{5,4},{6,7},{7,6},{8,9},{9,8},{10,11... | collective-permute-start | bytes 15728648 | tf_op jit(solution)/shard_map/ppermute | solution.py:500
  29.8 10.8 %collective-permute-start.10 = (bf16[640,256]{1,0:T(8,128)(2,1)}, bf16[640,256]{1,0:T(8,128)(2,1)S(1)}, u32[]{:S(2)}, u32[]{:S(2)}) collective-permute-start(bf16[640,256]{1,0:T(8,128)(2,1)} %collective-permute-done.4.refs_2_), channel_id=1, source_target_pairs={{0,4},{1,5},{2,0},{3,1},{4,8},{5,9},{6,2},{7,3},{8,12},{9,13},{10,... | collective-permute-start | bytes 983048 | tf_op jit(solution)/shard_map/ppermute | solution.py:495
  31.4 11.5 %collective-permute-start.14 = (bf16[640,256]{1,0:T(8,128)(2,1)}, bf16[640,256]{1,0:T(8,128)(2,1)S(1)}, u32[]{:S(2)}, u32[]{:S(2)}) collective-permute-start(bf16[640,256]{1,0:T(8,128)(2,1)} %collective-permute-done.7.refs_9_), channel_id=1, source_target_pairs={{0,2},{1,3},{2,6},{3,7},{4,0},{5,1},{6,10},{7,11},{8,4},{9,5},{10,... | collective-permute-start | bytes 983048 | tf_op jit(solution)/shard_map/ppermute | solution.py:495
  31.8 17.4 %collective-permute-start.9 = (bf16[640,256]{1,0:T(8,128)(2,1)}, bf16[640,256]{1,0:T(8,128)(2,1)}, u32[]{:S(2)}, u32[]{:S(2)}) collective-permute-start(bf16[640,256]{1,0:T(8,128)(2,1)} %collective-permute-done.6.refs_1_), channel_id=1, source_target_pairs={{0,2},{1,3},{2,6},{3,7},{4,0},{5,1},{6,10},{7,11},{8,4},{9,5},{10,... | collective-permute-start | bytes 983048 | tf_op jit(solution)/shard_map/ppermute | solution.py:495
  32.8 16.9 %collective-permute-start.15 = (bf16[640,256]{1,0:T(8,128)(2,1)}, bf16[640,256]{1,0:T(8,128)(2,1)}, u32[]{:S(2)}, u32[]{:S(2)}) collective-permute-start(bf16[640,256]{1,0:T(8,128)(2,1)} %collective-permute-done.5.refs_10_), channel_id=1, source_target_pairs={{0,4},{1,5},{2,0},{3,1},{4,8},{5,9},{6,2},{7,3},{8,12},{9,13},{10,... | collective-permute-start | bytes 983048 | tf_op jit(solution)/shard_map/ppermute | solution.py:495
  41.3 13.4 %collective-permute-start.12 = (bf16[640,256]{1,0:T(8,128)(2,1)S(1)}, bf16[640,256]{1,0:T(8,128)(2,1)}, u32[]{:S(2)}, u32[]{:S(2)}) collective-permute-start(bf16[640,256]{1,0:T(8,128)(2,1)S(1)} %collective-permute-done.10.refs_4_), channel_id=1, source_target_pairs={{0,4},{1,5},{2,0},{3,1},{4,8},{5,9},{6,2},{7,3},{8,12},{9,13},{10,... | collective-permute-start | bytes 983048 | tf_op jit(solution)/shard_map/ppermute | solution.py:495
  42.8 13.5 %collective-permute-start.16 = (bf16[640,256]{1,0:T(8,128)(2,1)S(1)}, bf16[640,256]{1,0:T(8,128)(2,1)}, u32[]{:S(2)}, u32[]{:S(2)}) collective-permute-start(bf16[640,256]{1,0:T(8,128)(2,1)S(1)} %collective-permute-done.14.refs_11_), channel_id=1, source_target_pairs={{0,2},{1,3},{2,6},{3,7},{4,0},{5,1},{6,10},{7,11},{8,4},{9,5},{10,... | collective-permute-start | bytes 983048 | tf_op jit(solution)/shard_map/ppermute | solution.py:495
  49.3 14.0 %collective-permute-start.11 = (bf16[640,256]{1,0:T(8,128)(2,1)}, bf16[640,256]{1,0:T(8,128)(2,1)}, u32[]{:S(2)}, u32[]{:S(2)}) collective-permute-start(bf16[640,256]{1,0:T(8,128)(2,1)} %collective-permute-done.9.refs_3_), channel_id=1, source_target_pairs={{0,2},{1,3},{2,6},{3,7},{4,0},{5,1},{6,10},{7,11},{8,4},{9,5},{10,... | collective-permute-start | bytes 983048 | tf_op jit(solution)/shard_map/ppermute | solution.py:495
  49.7 13.6 %collective-permute-start.17 = (bf16[640,256]{1,0:T(8,128)(2,1)}, bf16[640,256]{1,0:T(8,128)(2,1)}, u32[]{:S(2)}, u32[]{:S(2)}) collective-permute-start(bf16[640,256]{1,0:T(8,128)(2,1)} %collective-permute-done.15.refs_12_), channel_id=1, source_target_pairs={{0,4},{1,5},{2,0},{3,1},{4,8},{5,9},{6,2},{7,3},{8,12},{9,13},{10,... | collective-permute-start | bytes 983048 | tf_op jit(solution)/shard_map/ppermute | solution.py:495
  54.7 13.6 %collective-permute-start.13 = (bf16[640,256]{1,0:T(8,128)(2,1)}, bf16[640,256]{1,0:T(8,128)(2,1)}, u32[]{:S(2)}, u32[]{:S(2)}) collective-permute-start(bf16[640,256]{1,0:T(8,128)(2,1)} %collective-permute-done.12.refs_6_), channel_id=1, source_target_pairs={{0,4},{1,5},{2,0},{3,1},{4,8},{5,9},{6,2},{7,3},{8,12},{9,13},{10,... | collective-permute-start | bytes 983048 | tf_op jit(solution)/shard_map/ppermute | solution.py:498
  56.3 13.3 %collective-permute-start.18 = (bf16[640,256]{1,0:T(8,128)(2,1)}, bf16[640,256]{1,0:T(8,128)(2,1)}, u32[]{:S(2)}, u32[]{:S(2)}) collective-permute-start(bf16[640,256]{1,0:T(8,128)(2,1)} %collective-permute-done.16.refs_13_), channel_id=1, source_target_pairs={{0,2},{1,3},{2,6},{3,7},{4,0},{5,1},{6,10},{7,11},{8,4},{9,5},{10,... | collective-permute-start | bytes 983048 | tf_op jit(solution)/shard_map/ppermute | solution.py:498
  97.7 11.6 %collective-permute-start.19 = (bf16[128,640]{1,0:T(8,128)(2,1)}, bf16[128,640]{1,0:T(8,128)(2,1)}, u32[]{:S(2)}, u32[]{:S(2)}) collective-permute-start(bf16[128,640]{1,0:T(8,128)(2,1)} %get-tuple-element.62), channel_id=1, source_target_pairs={{0,4},{1,5},{2,0},{3,1},{4,8},{5,9},{6,2},{7,3},{8,12},{9,13},{10,... | collective-permute-start | bytes 491528 | tf_op jit(solution)/shard_map/ppermute | solution.py:513
  107.2 10.9 %collective-permute-start.32 = (bf16[256,640]{1,0:T(8,128)(2,1)}, bf16[256,640]{1,0:T(8,128)(2,1)}, u32[]{:S(2)}, u32[]{:S(2)}) collective-permute-start(bf16[256,640]{1,0:T(8,128)(2,1)} %get-tuple-element.78), channel_id=1, source_target_pairs={{0,4},{1,5},{2,0},{3,1},{4,8},{5,9},{6,2},{7,3},{8,12},{9,13},{10,... | collective-permute-start | bytes 983048 | tf_op jit(solution)/shard_map/ppermute | solution.py:513
  108.7 10.8 %collective-permute-start.33 = (bf16[256,640]{1,0:T(8,128)(2,1)}, bf16[256,640]{1,0:T(8,128)(2,1)}, u32[]{:S(2)}, u32[]{:S(2)}) collective-permute-start(bf16[256,640]{1,0:T(8,128)(2,1)} %get-tuple-element.79), channel_id=1, source_target_pairs={{0,2},{1,3},{2,6},{3,7},{4,0},{5,1},{6,10},{7,11},{8,4},{9,5},{10,... | collective-permute-start | bytes 983048 | tf_op jit(solution)/shard_map/ppermute | solution.py:513
  112.0 13.1 %collective-permute-start.21 = (bf16[256,640]{1,0:T(8,128)(2,1)}, bf16[256,640]{1,0:T(8,128)(2,1)}, u32[]{:S(2)}, u32[]{:S(2)}) collective-permute-start(bf16[256,640]{1,0:T(8,128)(2,1)} %get-tuple-element.64), channel_id=1, source_target_pairs={{0,4},{1,5},{2,0},{3,1},{4,8},{5,9},{6,2},{7,3},{8,12},{9,13},{10,... | collective-permute-start | bytes 983048 | tf_op jit(solution)/shard_map/ppermute | solution.py:513
  113.5 13.1 %collective-permute-start.22 = (bf16[256,640]{1,0:T(8,128)(2,1)}, bf16[256,640]{1,0:T(8,128)(2,1)}, u32[]{:S(2)}, u32[]{:S(2)}) collective-permute-start(bf16[256,640]{1,0:T(8,128)(2,1)} %get-tuple-element.65), channel_id=1, source_target_pairs={{0,2},{1,3},{2,6},{3,7},{4,0},{5,1},{6,10},{7,11},{8,4},{9,5},{10,... | collective-permute-start | bytes 983048 | tf_op jit(solution)/shard_map/ppermute | solution.py:513
  152.1 10.8 %collective-permute-start.39 = (bf16[272,640]{1,0:T(8,128)(2,1)}, bf16[272,640]{1,0:T(8,128)(2,1)}, u32[]{:S(2)}, u32[]{:S(2)}) collective-permute-start(bf16[272,640]{1,0:T(8,128)(2,1)} %get-tuple-element.87), channel_id=1, source_target_pairs={{0,1},{1,0},{2,3},{3,2},{4,5},{5,4},{6,7},{7,6},{8,9},{9,8},{10,11... | collective-permute-start | bytes 1044488 | tf_op jit(solution)/shard_map/ppermute | solution.py:518
  155.7 15.2 %collective-permute-start.28 = (bf16[272,640]{1,0:T(8,128)(2,1)}, bf16[272,640]{1,0:T(8,128)(2,1)}, u32[]{:S(2)}, u32[]{:S(2)}) collective-permute-start(bf16[272,640]{1,0:T(8,128)(2,1)} %get-tuple-element.73), channel_id=1, source_target_pairs={{0,1},{1,0},{2,3},{3,2},{4,5},{5,4},{6,7},{7,6},{8,9},{9,8},{10,11... | collective-permute-start | bytes 1044488 | tf_op jit(solution)/shard_map/ppermute | solution.py:518
  157.8 13.1 %collective-permute-start.29 = (bf16[144,640]{1,0:T(8,128)(2,1)}, bf16[144,640]{1,0:T(8,128)(2,1)}, u32[]{:S(2)}, u32[]{:S(2)}) collective-permute-start(bf16[144,640]{1,0:T(8,128)(2,1)} %get-tuple-element.74), channel_id=1, source_target_pairs={{0,17},{1,16},{2,19},{3,18},{4,21},{5,20},{6,23},{7,22},{8,25},{9,... | collective-permute-start | bytes 552968 | tf_op jit(solution)/shard_map/ppermute | solution.py:473
  (19 other events, 158.8 us)

commit v6 on v5

--- a/solution.py
+++ b/solution.py
@@ -67,7 +67,7 @@
 def norm_rows(scalars, hidden_rows, norm_gain, chips):
     tokens, width = hidden_rows.shape
     part = width // chips
-    tile = 128
+    tile = 256
 
     def body(s, x_ref, g_ref, o_ref):
         total = jnp.zeros((tile, 1), F32)
@@ -234,7 +234,7 @@
                     grads[h * wide + kv_at * HD : h * wide + (kv_at + 1) * HD, token] = grad.T.astype(BF16)
             return carry
 
-        lax.fori_loop(0, 2 * seqs, one, 0)
+        lax.fori_loop(0, 2 * seqs, one, 0, unroll=True)
 
         leaving = []
         for k in [last] + list(range(last))[::-1]:

time: 176 us -> 175 us (level)
    ppermute x8, starting transfers between devices: 5.86 us -> 3.19 us  [local(): down(going_down)]
    ppermute x8, starting transfers between devices: 10.4 us -> 13.1 us  [local(): up(going_up)]
  transfers between devices with their start and end apart: 41 -> 41, of which waited for: 22 -> 25; matrix products, arithmetic and copies ran while one was open for 1% -> 1% of each run, Pallas kernels for 24% -> 24%
where the time goes in v6:
time: 175 us; the launch traced here: 174 us
  Pallas kernels  71.4 us (41%)
  waiting for transfers between devices  60.9 us (35%)
  starting transfers between devices  39 us (22%)
    ppermute x12, waiting for transfers between devices, local(): ups[h], downs[h] = (up(ups[h]), down(downs[h]))  26.1 us
    pallas_call x1, Pallas kernels, group_step(): call(body, [jax.ShapeDtypeStruct((last, wide, part), BF16)] * heads + [ja...  25.4 us
    pallas_call x6, Pallas kernels, add_partials(): call(body, [shape] * 2, [pl.BlockSpec((1, HD, part), lambda i, s: (at, i,...  16.9 us
    ppermute x12, starting transfers between devices, local(): ups[h], downs[h] = (up(ups[h]), down(downs[h]))  15.1 us
    ppermute x8, starting transfers between devices, local(): up(going_up)  13.1 us
    ppermute x8, waiting for transfers between devices, local(): up(going_up)  11.1 us
    pallas_call x2, Pallas kernels, finish(): call(body, [jax.ShapeDtypeStruct((rows, cols), BF16), jax.ShapeDtypeStruc...  9.17 us
    ppermute x8, waiting for transfers between devices, local(): down(going_down)  8.07 us
  transfers between devices with their start and end apart: 41, of which 25 were waited for; matrix products, arithmetic and copies ran while one was open for 1% of the time, Pallas kernels for 24%

profile of v6, /device:TPU:0, one launch (start us, length us, event | category | flops | bytes accessed | tf_op | source)
XLA Modules:
  0.0 174.3 jit_solution(13893804829244972185)
XLA Ops:
  5.5 2.9 %own_blocks.1 = (bf16[640,256]{1,0:T(8,128)(2,1)}, bf16[640,256]{1,0:T(8,128)(2,1)}) custom-call(s32[9]{0:T(128)} %pad_add_fusion.s, bf16[320,1024]{1,0:T(8,128)(2,1)} %bitcast.10, bf16[320,1024]{1,0:T(8,128)(2,1)} %collective-permute-done.r_ref), custom_call_target="tpu_custom_call" | custom-call | bytes 1966080 | tf_op jit(solution)/shard_map/own_blocks/pallas_call | solution.py:113
  8.5 2.9 %collective-permute-start.6 = (bf16[640,256]{1,0:T(8,128)(2,1)}, bf16[640,256]{1,0:T(8,128)(2,1)}, u32[]{:S(2)}, u32[]{:S(2)}) collective-permute-start(bf16[640,256]{1,0:T(8,128)(2,1)} %get-tuple-element.51.refs_0_), channel_id=1, source_target_pairs={{0,2},{1,3},{2,6},{3,7},{4,0},{5,1},{6,10},{7,11},{8,4},{9,5},{10,... | collective-permute-start | bytes 983048 | tf_op jit(solution)/shard_map/ppermute | solution.py:495
  13.4 6.9 %collective-permute-done.6.refs_1_ = bf16[640,256]{1,0:T(8,128)(2,1)} collective-permute-done((bf16[640,256]{1,0:T(8,128)(2,1)}, bf16[640,256]{1,0:T(8,128)(2,1)}, u32[]{:S(2)}, u32[]{:S(2)}) %collective-permute-start.6) | collective-permute-done | bytes 327712 | tf_op jit(solution)/shard_map/ppermute | solution.py:495
  22.4 6.5 %norm.1.a_ref = bf16[8,512,640]{2,1,0:T(8,128)(2,1)} custom-call(s32[9]{0:T(128)} %pad_add_fusion.s, bf16[512,5120]{1,0:T(8,128)(2,1)} %bitcast.13, f32[1,5120]{1,0:T(1,128)} %bitcast.15), custom_call_target="tpu_custom_call" | custom-call | flops 15728640 | bytes 10485760 | tf_op jit(solution)/shard_map/norm/pallas_call | solution.py:82
  33.5 6.7 %collective-permute-done.10.refs_4_ = bf16[640,256]{1,0:T(8,128)(2,1)S(1)} collective-permute-done((bf16[640,256]{1,0:T(8,128)(2,1)}, bf16[640,256]{1,0:T(8,128)(2,1)S(1)}, u32[]{:S(2)}, u32[]{:S(2)}) %collective-permute-start.10) | collective-permute-done | bytes 327712 | tf_op jit(solution)/shard_map/ppermute | solution.py:495
  42.9 5.8 %collective-permute-done.9.refs_3_ = bf16[640,256]{1,0:T(8,128)(2,1)} collective-permute-done((bf16[640,256]{1,0:T(8,128)(2,1)}, bf16[640,256]{1,0:T(8,128)(2,1)}, u32[]{:S(2)}, u32[]{:S(2)}) %collective-permute-start.9) | collective-permute-done | bytes 327712 | tf_op jit(solution)/shard_map/ppermute | solution.py:495
  50.8 3.5 %collective-permute-done.12.refs_6_ = bf16[640,256]{1,0:T(8,128)(2,1)} collective-permute-done((bf16[640,256]{1,0:T(8,128)(2,1)S(1)}, bf16[640,256]{1,0:T(8,128)(2,1)}, u32[]{:S(2)}, u32[]{:S(2)}) %collective-permute-start.12) | collective-permute-done | bytes 327712 | tf_op jit(solution)/shard_map/ppermute | solution.py:495
  56.4 3.8 %start_deltas.1 = (f32[256,640]{1,0:T(8,128)}, f32[256,640]{1,0:T(8,128)}) custom-call(s32[9]{0:T(128)} %pad_add_fusion.s, f32[320,1024]{1,0:T(8,128)} %k_ref.3, f32[320,1024]{1,0:T(8,128)} %collective-permute-done.1.r_ref, bf16[640,256]{1,0:T(8,128)(2,1)} %get-tuple-element.51.refs_0_, bf16[640,256]{1,0:T(8,128)(2,1)} %get-tuple-element.52.refs_1_.refs_8_), custom_call_target="tpu_custom_call" | custom-call | bytes 4587520 | tf_op jit(solution)/shard_map/start_deltas/pallas_call | solution.py:140
  62.8 5.1 %collective-permute-done.13.refs_7_ = bf16[640,256]{1,0:T(8,128)(2,1)} collective-permute-done((bf16[640,256]{1,0:T(8,128)(2,1)}, bf16[640,256]{1,0:T(8,128)(2,1)}, u32[]{:S(2)}, u32[]{:S(2)}) %collective-permute-start.13) | collective-permute-done | bytes 327712 | tf_op jit(solution)/shard_map/ppermute | solution.py:498
  69.1 25.4 %group_step.1 = (bf16[7,256,640]{2,1,0:T(8,128)(2,1)}, bf16[7,256,640]{2,1,0:T(8,128)(2,1)}, bf16[128,640]{1,0:T(8,128)(2,1)}, bf16[128,640]{1,0:T(8,128)(2,1)},...) custom-call(s32[9]{0:T(128)} %pad_add_fusion.s, bf16[8,512,640]{2,1,0:T(8,128)(2,1)} %norm.1.a_ref, ...), custom_call_target="tpu_custom_call" | custom-call | flops 16106127360 | bytes 31457280 | tf_op jit(solution)/shard_map/group_step/pallas_call | solution.py:261
  98.6 3.4 %collective-permute-done.30.ui_ref = bf16[128,640]{1,0:T(8,128)(2,1)} collective-permute-done((bf16[128,640]{1,0:T(8,128)(2,1)}, bf16[128,640]{1,0:T(8,128)(2,1)}, u32[]{:S(2)}, u32[]{:S(2)}) %collective-permute-start.30) | collective-permute-done | bytes 163872 | tf_op jit(solution)/shard_map/ppermute | solution.py:513
  103.3 2.8 %add_0_3.1 = (bf16[256,640]{1,0:T(8,128)(2,1)}, bf16[256,640]{1,0:T(8,128)(2,1)}) custom-call(s32[9]{0:T(128)} %pad_add_fusion.s, bf16[7,256,640]{2,1,0:T(8,128)(2,1)} %get-tuple-element.75.ou_ref.od_ref.g_ref, bf16[7,256,640]{2,1,0:T(8,128)(2,1)} %get-tuple-element.75.ou_ref.od_ref.g_ref, bf16[128,640]{1,0:T(8,128)(2,1)} %collective-permute-done.30.ui_ref, ...), custom_call_target="tpu_custom_call" | custom-call | bytes 1966080 | tf_op jit(solution)/shard_map/add_0_3/pallas_call | solution.py:304
  108.1 2.7 %add_1_3.1 = (bf16[256,640]{1,0:T(8,128)(2,1)}, bf16[256,640]{1,0:T(8,128)(2,1)}) custom-call(s32[9]{0:T(128)} %pad_add_fusion.s, bf16[7,256,640]{2,1,0:T(8,128)(2,1)} %get-tuple-element.61.ou_ref.od_ref.g_ref, bf16[7,256,640]{2,1,0:T(8,128)(2,1)} %get-tuple-element.61.ou_ref.od_ref.g_ref, bf16[128,640]{1,0:T(8,128)(2,1)} %collective-permute-done.19.ui_ref, ...), custom_call_target="tpu_custom_call" | custom-call | bytes 1966080 | tf_op jit(solution)/shard_map/add_1_3/pallas_call | solution.py:304
  112.9 4.1 %collective-permute-done.32.ui_ref = bf16[256,640]{1,0:T(8,128)(2,1)} collective-permute-done((bf16[256,640]{1,0:T(8,128)(2,1)}, bf16[256,640]{1,0:T(8,128)(2,1)}, u32[]{:S(2)}, u32[]{:S(2)}) %collective-permute-start.32) | collective-permute-done | bytes 327712 | tf_op jit(solution)/shard_map/ppermute | solution.py:513
  118.5 2.9 %add_0_2.1 = (bf16[256,640]{1,0:T(8,128)(2,1)}, bf16[256,640]{1,0:T(8,128)(2,1)}) custom-call(s32[9]{0:T(128)} %pad_add_fusion.s, bf16[7,256,640]{2,1,0:T(8,128)(2,1)} %get-tuple-element.75.ou_ref.od_ref.g_ref, bf16[7,256,640]{2,1,0:T(8,128)(2,1)} %get-tuple-element.75.ou_ref.od_ref.g_ref, bf16[256,640]{1,0:T(8,128)(2,1)} %collective-permute-done.32.ui_ref, ...), custom_call_target="tpu_custom_call" | custom-call | bytes 1966080 | tf_op jit(solution)/shard_map/add_0_2/pallas_call | solution.py:304
  125.4 2.8 %add_1_2.1 = (bf16[256,640]{1,0:T(8,128)(2,1)}, bf16[256,640]{1,0:T(8,128)(2,1)}) custom-call(s32[9]{0:T(128)} %pad_add_fusion.s, bf16[7,256,640]{2,1,0:T(8,128)(2,1)} %get-tuple-element.61.ou_ref.od_ref.g_ref, bf16[7,256,640]{2,1,0:T(8,128)(2,1)} %get-tuple-element.61.ou_ref.od_ref.g_ref, bf16[256,640]{1,0:T(8,128)(2,1)} %collective-permute-done.21.ui_ref, ...), custom_call_target="tpu_custom_call" | custom-call | bytes 1966080 | tf_op jit(solution)/shard_map/add_1_2/pallas_call | solution.py:304
  132.4 2.8 %add_0_1.1 = (bf16[256,640]{1,0:T(8,128)(2,1)}, bf16[256,640]{1,0:T(8,128)(2,1)}) custom-call(s32[9]{0:T(128)} %pad_add_fusion.s, bf16[7,256,640]{2,1,0:T(8,128)(2,1)} %get-tuple-element.75.ou_ref.od_ref.g_ref, bf16[7,256,640]{2,1,0:T(8,128)(2,1)} %get-tuple-element.75.ou_ref.od_ref.g_ref, bf16[256,640]{1,0:T(8,128)(2,1)} %collective-permute-done.34.ui_ref, ...), custom_call_target="tpu_custom_call" | custom-call | bytes 1966080 | tf_op jit(solution)/shard_map/add_0_1/pallas_call | solution.py:304
  139.8 2.9 %add_1_1.1 = (bf16[256,640]{1,0:T(8,128)(2,1)}, bf16[256,640]{1,0:T(8,128)(2,1)}) custom-call(s32[9]{0:T(128)} %pad_add_fusion.s, bf16[7,256,640]{2,1,0:T(8,128)(2,1)} %get-tuple-element.61.ou_ref.od_ref.g_ref, bf16[7,256,640]{2,1,0:T(8,128)(2,1)} %get-tuple-element.61.ou_ref.od_ref.g_ref, bf16[256,640]{1,0:T(8,128)(2,1)} %collective-permute-done.23.ui_ref, ...), custom_call_target="tpu_custom_call" | custom-call | bytes 1966080 | tf_op jit(solution)/shard_map/add_1_1/pallas_call | solution.py:304
  146.2 3.4 %code_0.1 = (bf16[272,640]{1,0:T(8,128)(2,1)}, bf16[272,640]{1,0:T(8,128)(2,1)}, bf16[144,640]{1,0:T(8,128)(2,1)}, bf16[144,640]{1,0:T(8,128)(2,1)}) custom-call(s32[9]{0:T(128)} %pad_add_fusion.s, bf16[7,256,640]{2,1,0:T(8,128)(2,1)} %get-tuple-element.75.ou_ref.od_ref.g_ref, bf16[256,640]{1,0:T(8,128)(2,1)} %collective-permute-done.36.ui_ref, ...), custom_call_target="tpu_custom_call" | custom-call | bytes 2621440 | tf_op jit(solution)/shard_map/code_0/pallas_call | solution.py:358
  151.7 3.4 %code_1.1 = (bf16[272,640]{1,0:T(8,128)(2,1)}, bf16[272,640]{1,0:T(8,128)(2,1)}, bf16[144,640]{1,0:T(8,128)(2,1)}, bf16[144,640]{1,0:T(8,128)(2,1)}) custom-call(s32[9]{0:T(128)} %pad_add_fusion.s, bf16[7,256,640]{2,1,0:T(8,128)(2,1)} %get-tuple-element.61.ou_ref.od_ref.g_ref, bf16[256,640]{1,0:T(8,128)(2,1)} %collective-permute-done.25.ui_ref, ...), custom_call_target="tpu_custom_call" | custom-call | bytes 2621440 | tf_op jit(solution)/shard_map/code_1/pallas_call | solution.py:358
  158.0 3.9 %collective-permute-done.40.refs_4_ = bf16[144,640]{1,0:T(8,128)(2,1)} collective-permute-done((bf16[144,640]{1,0:T(8,128)(2,1)}, bf16[144,640]{1,0:T(8,128)(2,1)}, u32[]{:S(2)}, u32[]{:S(2)}) %collective-permute-start.40) | collective-permute-done | bytes 184352 | tf_op jit(solution)/shard_map/ppermute | solution.py:473
  162.0 4.6 %finish_0.1 = (bf16[320,1024]{1,0:T(8,128)(2,1)}, f32[320,1024]{1,0:T(8,128)}, f32[320,1024]{1,0:T(8,128)}) custom-call(s32[9]{0:T(128)} %pad_add_fusion.s, bf16[320,1024]{1,0:T(8,128)(2,1)} %bitcast.11, f32[320,1024]{1,0:T(8,128)} %k_ref.3, f32[320,1024]{1,0:T(8,128)} %m_ref.3, bf16[272,640]{1,0:T(8,128)(2,1)} %get-tuple-element.85.refs_0_.refs_2_, ...), custom_call_target="tpu_custom_call" | custom-call | bytes 3932160 | tf_op jit(solution)/shard_map/finish_0/pallas_call | solution.py:426
  166.9 2.7 %collective-permute-done.29.refs_4_ = bf16[144,640]{1,0:T(8,128)(2,1)} collective-permute-done((bf16[144,640]{1,0:T(8,128)(2,1)}, bf16[144,640]{1,0:T(8,128)(2,1)}, u32[]{:S(2)}, u32[]{:S(2)}) %collective-permute-start.29) | collective-permute-done | bytes 184352 | tf_op jit(solution)/shard_map/ppermute | solution.py:473
  169.5 4.6 %finish_1.1 = (bf16[320,1024]{1,0:T(8,128)(2,1)}, f32[320,1024]{1,0:T(8,128)}, f32[320,1024]{1,0:T(8,128)}) custom-call(s32[9]{0:T(128)} %pad_add_fusion.s, bf16[320,1024]{1,0:T(8,128)(2,1)} %bitcast.12, f32[320,1024]{1,0:T(8,128)} %k_ref.3, f32[320,1024]{1,0:T(8,128)} %m_ref.3, ...), custom_call_target="tpu_custom_call", output_to_operand_aliasing={{0}: (10, {}), {1}: (11, {}), {2}: (12, {})} | custom-call | bytes 3932160 | tf_op jit(solution)/shard_map/finish_1/pallas_call | solution.py:426
  (78 shorter events, 57.1 us)
Async XLA Ops:
  5.1 24.3 %collective-permute-start.2 = (bf16[2,256,2560]{2,1,0:T(8,128)(2,1)}, bf16[2,256,2560]{2,1,0:T(8,128)(2,1)}, u32[]{:S(2)}, u32[]{:S(2)}) collective-permute-start(bf16[2,256,2560]{2,1,0:T(8,128)(2,1)} %bitcast.16), channel_id=1, source_target_pairs={{0,1},{1,0},{2,3},{3,2},{4,5},{5,4},{6,7},{7,6},{8,9},{9,8},{10,11... | collective-permute-start | bytes 7864328 | tf_op jit(solution)/shard_map/ppermute | solution.py:486
  8.4 21.0 %collective-permute-start.3 = (bf16[2,256,2560]{2,1,0:T(8,128)(2,1)}, bf16[2,256,2560]{2,1,0:T(8,128)(2,1)}, u32[]{:S(2)}, u32[]{:S(2)}) collective-permute-start(bf16[2,256,2560]{2,1,0:T(8,128)(2,1)} %bitcast.18), channel_id=1, source_target_pairs={{0,1},{1,0},{2,3},{3,2},{4,5},{5,4},{6,7},{7,6},{8,9},{9,8},{10,11... | collective-permute-start | bytes 7864328 | tf_op jit(solution)/shard_map/ppermute | solution.py:487
  8.5 11.8 %collective-permute-start.6 = (bf16[640,256]{1,0:T(8,128)(2,1)}, bf16[640,256]{1,0:T(8,128)(2,1)}, u32[]{:S(2)}, u32[]{:S(2)}) collective-permute-start(bf16[640,256]{1,0:T(8,128)(2,1)} %get-tuple-element.51.refs_0_), channel_id=1, source_target_pairs={{0,2},{1,3},{2,6},{3,7},{4,0},{5,1},{6,10},{7,11},{8,4},{9,5},{10,... | collective-permute-start | bytes 983048 | tf_op jit(solution)/shard_map/ppermute | solution.py:495
  11.4 17.4 %collective-permute-start.4 = (bf16[640,256]{1,0:T(8,128)(2,1)}, bf16[640,256]{1,0:T(8,128)(2,1)}, u32[]{:S(2)}, u32[]{:S(2)}) collective-permute-start(bf16[640,256]{1,0:T(8,128)(2,1)} %get-tuple-element.51.refs_0_), channel_id=1, source_target_pairs={{0,4},{1,5},{2,0},{3,1},{4,8},{5,9},{6,2},{7,3},{8,12},{9,13},{10,... | collective-permute-start | bytes 983048 | tf_op jit(solution)/shard_map/ppermute | solution.py:495
  11.5 17.3 %collective-permute-start.7 = (bf16[640,256]{1,0:T(8,128)(2,1)}, bf16[640,256]{1,0:T(8,128)(2,1)}, u32[]{:S(2)}, u32[]{:S(2)}) collective-permute-start(bf16[640,256]{1,0:T(8,128)(2,1)} %get-tuple-element.52.refs_1_.refs_8_), channel_id=1, source_target_pairs={{0,2},{1,3},{2,6},{3,7},{4,0},{5,1},{6,10},{7,11},{8,4},{9,5},{10,... | collective-permute-start | bytes 983048 | tf_op jit(solution)/shard_map/ppermute | solution.py:495
  29.4 39.7 %collective-permute-start.8 = (bf16[8,512,640]{2,1,0:T(8,128)(2,1)}, bf16[8,512,640]{2,1,0:T(8,128)(2,1)}, u32[]{:S(2)}, u32[]{:S(2)}) collective-permute-start(bf16[8,512,640]{2,1,0:T(8,128)(2,1)} %norm.1.a_ref), channel_id=1, source_target_pairs={{0,1},{1,0},{2,3},{3,2},{4,5},{5,4},{6,7},{7,6},{8,9},{9,8},{10,11... | collective-permute-start | bytes 15728648 | tf_op jit(solution)/shard_map/ppermute | solution.py:500
  30.9 11.5 %collective-permute-start.14 = (bf16[640,256]{1,0:T(8,128)(2,1)}, bf16[640,256]{1,0:T(8,128)(2,1)S(1)}, u32[]{:S(2)}, u32[]{:S(2)}) collective-permute-start(bf16[640,256]{1,0:T(8,128)(2,1)} %collective-permute-done.7.refs_9_), channel_id=1, source_target_pairs={{0,2},{1,3},{2,6},{3,7},{4,0},{5,1},{6,10},{7,11},{8,4},{9,5},{10,... | collective-permute-start | bytes 983048 | tf_op jit(solution)/shard_map/ppermute | solution.py:495
  31.5 17.3 %collective-permute-start.9 = (bf16[640,256]{1,0:T(8,128)(2,1)}, bf16[640,256]{1,0:T(8,128)(2,1)}, u32[]{:S(2)}, u32[]{:S(2)}) collective-permute-start(bf16[640,256]{1,0:T(8,128)(2,1)} %collective-permute-done.6.refs_1_), channel_id=1, source_target_pairs={{0,2},{1,3},{2,6},{3,7},{4,0},{5,1},{6,10},{7,11},{8,4},{9,5},{10,... | collective-permute-start | bytes 983048 | tf_op jit(solution)/shard_map/ppermute | solution.py:495
  32.8 16.5 %collective-permute-start.15 = (bf16[640,256]{1,0:T(8,128)(2,1)}, bf16[640,256]{1,0:T(8,128)(2,1)}, u32[]{:S(2)}, u32[]{:S(2)}) collective-permute-start(bf16[640,256]{1,0:T(8,128)(2,1)} %collective-permute-done.5.refs_10_), channel_id=1, source_target_pairs={{0,4},{1,5},{2,0},{3,1},{4,8},{5,9},{6,2},{7,3},{8,12},{9,13},{10,... | collective-permute-start | bytes 983048 | tf_op jit(solution)/shard_map/ppermute | solution.py:495
  40.9 13.4 %collective-permute-start.12 = (bf16[640,256]{1,0:T(8,128)(2,1)S(1)}, bf16[640,256]{1,0:T(8,128)(2,1)}, u32[]{:S(2)}, u32[]{:S(2)}) collective-permute-start(bf16[640,256]{1,0:T(8,128)(2,1)S(1)} %collective-permute-done.10.refs_4_), channel_id=1, source_target_pairs={{0,4},{1,5},{2,0},{3,1},{4,8},{5,9},{6,2},{7,3},{8,12},{9,13},{10,... | collective-permute-start | bytes 983048 | tf_op jit(solution)/shard_map/ppermute | solution.py:495
  42.3 13.5 %collective-permute-start.16 = (bf16[640,256]{1,0:T(8,128)(2,1)S(1)}, bf16[640,256]{1,0:T(8,128)(2,1)}, u32[]{:S(2)}, u32[]{:S(2)}) collective-permute-start(bf16[640,256]{1,0:T(8,128)(2,1)S(1)} %collective-permute-done.14.refs_11_), channel_id=1, source_target_pairs={{0,2},{1,3},{2,6},{3,7},{4,0},{5,1},{6,10},{7,11},{8,4},{9,5},{10,... | collective-permute-start | bytes 983048 | tf_op jit(solution)/shard_map/ppermute | solution.py:495
  48.8 14.0 %collective-permute-start.11 = (bf16[640,256]{1,0:T(8,128)(2,1)}, bf16[640,256]{1,0:T(8,128)(2,1)}, u32[]{:S(2)}, u32[]{:S(2)}) collective-permute-start(bf16[640,256]{1,0:T(8,128)(2,1)} %collective-permute-done.9.refs_3_), channel_id=1, source_target_pairs={{0,2},{1,3},{2,6},{3,7},{4,0},{5,1},{6,10},{7,11},{8,4},{9,5},{10,... | collective-permute-start | bytes 983048 | tf_op jit(solution)/shard_map/ppermute | solution.py:495
  49.4 13.4 %collective-permute-start.17 = (bf16[640,256]{1,0:T(8,128)(2,1)}, bf16[640,256]{1,0:T(8,128)(2,1)}, u32[]{:S(2)}, u32[]{:S(2)}) collective-permute-start(bf16[640,256]{1,0:T(8,128)(2,1)} %collective-permute-done.15.refs_12_), channel_id=1, source_target_pairs={{0,4},{1,5},{2,0},{3,1},{4,8},{5,9},{6,2},{7,3},{8,12},{9,13},{10,... | collective-permute-start | bytes 983048 | tf_op jit(solution)/shard_map/ppermute | solution.py:495
  54.3 13.6 %collective-permute-start.13 = (bf16[640,256]{1,0:T(8,128)(2,1)}, bf16[640,256]{1,0:T(8,128)(2,1)}, u32[]{:S(2)}, u32[]{:S(2)}) collective-permute-start(bf16[640,256]{1,0:T(8,128)(2,1)} %collective-permute-done.12.refs_6_), channel_id=1, source_target_pairs={{0,4},{1,5},{2,0},{3,1},{4,8},{5,9},{6,2},{7,3},{8,12},{9,13},{10,... | collective-permute-start | bytes 983048 | tf_op jit(solution)/shard_map/ppermute | solution.py:498
  55.8 13.3 %collective-permute-start.18 = (bf16[640,256]{1,0:T(8,128)(2,1)}, bf16[640,256]{1,0:T(8,128)(2,1)}, u32[]{:S(2)}, u32[]{:S(2)}) collective-permute-start(bf16[640,256]{1,0:T(8,128)(2,1)} %collective-permute-done.16.refs_13_), channel_id=1, source_target_pairs={{0,2},{1,3},{2,6},{3,7},{4,0},{5,1},{6,10},{7,11},{8,4},{9,5},{10,... | collective-permute-start | bytes 983048 | tf_op jit(solution)/shard_map/ppermute | solution.py:498
  96.5 11.6 %collective-permute-start.19 = (bf16[128,640]{1,0:T(8,128)(2,1)}, bf16[128,640]{1,0:T(8,128)(2,1)}, u32[]{:S(2)}, u32[]{:S(2)}) collective-permute-start(bf16[128,640]{1,0:T(8,128)(2,1)} %get-tuple-element.62), channel_id=1, source_target_pairs={{0,4},{1,5},{2,0},{3,1},{4,8},{5,9},{6,2},{7,3},{8,12},{9,13},{10,... | collective-permute-start | bytes 491528 | tf_op jit(solution)/shard_map/ppermute | solution.py:513
  106.1 10.9 %collective-permute-start.32 = (bf16[256,640]{1,0:T(8,128)(2,1)}, bf16[256,640]{1,0:T(8,128)(2,1)}, u32[]{:S(2)}, u32[]{:S(2)}) collective-permute-start(bf16[256,640]{1,0:T(8,128)(2,1)} %get-tuple-element.78), channel_id=1, source_target_pairs={{0,4},{1,5},{2,0},{3,1},{4,8},{5,9},{6,2},{7,3},{8,12},{9,13},{10,... | collective-permute-start | bytes 983048 | tf_op jit(solution)/shard_map/ppermute | solution.py:513
  107.7 10.8 %collective-permute-start.33 = (bf16[256,640]{1,0:T(8,128)(2,1)}, bf16[256,640]{1,0:T(8,128)(2,1)}, u32[]{:S(2)}, u32[]{:S(2)}) collective-permute-start(bf16[256,640]{1,0:T(8,128)(2,1)} %get-tuple-element.79), channel_id=1, source_target_pairs={{0,2},{1,3},{2,6},{3,7},{4,0},{5,1},{6,10},{7,11},{8,4},{9,5},{10,... | collective-permute-start | bytes 983048 | tf_op jit(solution)/shard_map/ppermute | solution.py:513
  110.9 13.1 %collective-permute-start.21 = (bf16[256,640]{1,0:T(8,128)(2,1)}, bf16[256,640]{1,0:T(8,128)(2,1)}, u32[]{:S(2)}, u32[]{:S(2)}) collective-permute-start(bf16[256,640]{1,0:T(8,128)(2,1)} %get-tuple-element.64), channel_id=1, source_target_pairs={{0,4},{1,5},{2,0},{3,1},{4,8},{5,9},{6,2},{7,3},{8,12},{9,13},{10,... | collective-permute-start | bytes 983048 | tf_op jit(solution)/shard_map/ppermute | solution.py:513
  112.4 12.9 %collective-permute-start.22 = (bf16[256,640]{1,0:T(8,128)(2,1)}, bf16[256,640]{1,0:T(8,128)(2,1)}, u32[]{:S(2)}, u32[]{:S(2)}) collective-permute-start(bf16[256,640]{1,0:T(8,128)(2,1)} %get-tuple-element.65), channel_id=1, source_target_pairs={{0,2},{1,3},{2,6},{3,7},{4,0},{5,1},{6,10},{7,11},{8,4},{9,5},{10,... | collective-permute-start | bytes 983048 | tf_op jit(solution)/shard_map/ppermute | solution.py:513
  128.2 11.0 %collective-permute-start.23 = (bf16[256,640]{1,0:T(8,128)(2,1)}, bf16[256,640]{1,0:T(8,128)(2,1)}, u32[]{:S(2)}, u32[]{:S(2)}) collective-permute-start(bf16[256,640]{1,0:T(8,128)(2,1)} %get-tuple-element.66), channel_id=1, source_target_pairs={{0,4},{1,5},{2,0},{3,1},{4,8},{5,9},{6,2},{7,3},{8,12},{9,13},{10,... | collective-permute-start | bytes 983048 | tf_op jit(solution)/shard_map/ppermute | solution.py:513
  151.1 10.9 %collective-permute-start.39 = (bf16[272,640]{1,0:T(8,128)(2,1)}, bf16[272,640]{1,0:T(8,128)(2,1)}, u32[]{:S(2)}, u32[]{:S(2)}) collective-permute-start(bf16[272,640]{1,0:T(8,128)(2,1)} %get-tuple-element.87), channel_id=1, source_target_pairs={{0,1},{1,0},{2,3},{3,2},{4,5},{5,4},{6,7},{7,6},{8,9},{9,8},{10,11... | collective-permute-start | bytes 1044488 | tf_op jit(solution)/shard_map/ppermute | solution.py:518
  155.0 14.5 %collective-permute-start.28 = (bf16[272,640]{1,0:T(8,128)(2,1)}, bf16[272,640]{1,0:T(8,128)(2,1)}, u32[]{:S(2)}, u32[]{:S(2)}) collective-permute-start(bf16[272,640]{1,0:T(8,128)(2,1)} %get-tuple-element.73), channel_id=1, source_target_pairs={{0,1},{1,0},{2,3},{3,2},{4,5},{5,4},{6,7},{7,6},{8,9},{9,8},{10,11... | collective-permute-start | bytes 1044488 | tf_op jit(solution)/shard_map/ppermute | solution.py:518
  157.2 12.4 %collective-permute-start.29 = (bf16[144,640]{1,0:T(8,128)(2,1)}, bf16[144,640]{1,0:T(8,128)(2,1)}, u32[]{:S(2)}, u32[]{:S(2)}) collective-permute-start(bf16[144,640]{1,0:T(8,128)(2,1)} %get-tuple-element.74), channel_id=1, source_target_pairs={{0,17},{1,16},{2,19},{3,18},{4,21},{5,20},{6,23},{7,22},{8,25},{9,... | collective-permute-start | bytes 552968 | tf_op jit(solution)/shard_map/ppermute | solution.py:473
  (19 other events, 157.6 us)
